TPU v7x, 32 devices: a whole 2x2x4 slice. The times are simulated.
32 devices in a mesh: ctx: 8 (over y, x, core), tp: 4 (over z).
Axes of the slice: x: 2, y: 2, z: 4, core: 2. Of those that a mesh axis runs over, the one named last changes fastest.
Arguments:
- queries: bfloat16 [5120, 4096], P('ctx', 'tp'), may hold values from -6 to 6
- key_rows: bfloat16 [5120, 1024], P(('ctx', 'tp')), may hold values from -6 to 6
- value_rows: bfloat16 [5120, 1024], P(('ctx', 'tp')), may hold values from -6 to 6
- out_grad: bfloat16 [5120, 4096], P('ctx', 'tp'), may hold values from -6 to 6
- block_list: int32 [40, 8], P('ctx'), may hold values from 0 to 39, as said below
Outputs:
- attended: bfloat16 [5120, 4096], P('ctx', 'tp')
- query_grad: bfloat16 [5120, 4096], P('ctx', 'tp')
- key_grad: bfloat16 [5120, 1024], P(('ctx', 'tp'))
- value_grad: bfloat16 [5120, 1024], P(('ctx', 'tp'))
Inputs may be any that keep to these rules, and one draw needn't show every extreme that they name: `block_list`: row i: columns 0 and 1 are two different global blocks, the same in every row; columns 2, 3, 4 are (i - 1) mod 40, i, (i + 1) mod 40; columns 5 to 7 are random blocks. Shard s holds blocks s * 5 to (s + 1) * 5 - 1. The random entries of the 5 rows of one shard name blocks of any one shard at most 2 times, and exactly 2 times for some pair of shards in every draw.
All inputs are finite; a program needn't handle non-finite values.
Results may differ from a plain program's by a relative error of at most 0.025.
Values may be sent and summed in bfloat16 or wider, within the bound.
No kernel may reach another device: no remote copies, remote signals or barrier semaphores. Data moves between devices by JAX's collectives and lax.ppermute only.
A program may use at most 192 MiB of HBM per device.

v0:
```python
import jax
import jax.numpy as jnp
from jax import lax
from jax.sharding import PartitionSpec as P

HD = 128
BLK = 128
GLOB = 2
WIN = 3
RAND = 3


def padded_2(cells, sides, width):
    for axis, dim in sides:
        count = lax.axis_size(axis)
        head = lax.slice_in_dim(cells, 0, width, axis=dim)
        tail = lax.slice_in_dim(cells, cells.shape[dim] - width, cells.shape[dim], axis=dim)
        cells = jnp.concatenate(
            [
                lax.ppermute(tail, axis, [(i, (i + 1) % count) for i in range(count)]),
                cells,
                lax.ppermute(head, axis, [((i + 1) % count, i) for i in range(count)]),
            ],
            axis=dim,
        )
    return cells


def spread(x, axis, root):
    mine = lax.axis_index(axis) == root
    return lax.psum(jnp.where(mine, x, jnp.zeros_like(x)), axis)


def shifted(value, axis, steps):
    count = lax.axis_size(axis)
    pairs = [(source, (source + steps) % count) for source in range(count)]
    return lax.ppermute(value, axis, pairs)


def attend_block(tiles):
    query_tile, grad_tile, keys_tile, values_tile = tiles
    inverse_root = float(HD) ** (-0.5)
    scores = (
        jnp.einsum("qkgd,nkd->kgqn", query_tile, keys_tile, preferred_element_type=jnp.float32)
        * inverse_root
    )
    row_max = jnp.max(scores, axis=-1, keepdims=True)
    logsum = row_max + jnp.log(jnp.sum(jnp.exp(scores - row_max), axis=-1, keepdims=True))
    weights_f = jnp.exp(scores - logsum)
    weights_low = weights_f.astype(jnp.bfloat16)
    attended = jnp.einsum(
        "kgqn,nkd->qkgd", weights_low, values_tile, preferred_element_type=jnp.float32
    ).astype(jnp.bfloat16)
    row_delta = jnp.sum(grad_tile.astype(jnp.float32) * attended.astype(jnp.float32), axis=-1)
    row_delta = jnp.transpose(row_delta, (1, 2, 0))
    dweights = jnp.einsum(
        "qkgd,nkd->kgqn", grad_tile, values_tile, preferred_element_type=jnp.float32
    )
    dscores_low = (weights_f * (dweights - row_delta[..., None])).astype(jnp.bfloat16)
    query_grad = (
        jnp.einsum("kgqn,nkd->qkgd", dscores_low, keys_tile, preferred_element_type=jnp.float32)
        * inverse_root
    ).astype(jnp.bfloat16)
    value_part = jnp.einsum(
        "kgqn,qkgd->nkd", weights_low, grad_tile, preferred_element_type=jnp.float32
    )
    key_part = (
        jnp.einsum("kgqn,qkgd->nkd", dscores_low, query_tile, preferred_element_type=jnp.float32)
        * inverse_root
    )
    return (attended, query_grad, key_part, value_part)


def shards(queries, key_rows, value_rows, out_grad, block_list):
    tokens_here = queries.shape[0]
    block_count = tokens_here // BLK
    shard_total = lax.axis_size("ctx")
    my_index = lax.axis_index("ctx")
    local_keys, local_values = (
        lax.all_to_all(key_rows, "tp", split_axis=1, concat_axis=0, tiled=True),
        lax.all_to_all(value_rows, "tp", split_axis=1, concat_axis=0, tiled=True),
    )
    head_width = local_keys.shape[1]
    kv_heads = head_width // HD
    both_width = 2 * head_width
    joined = jnp.concatenate([local_keys, local_values], axis=1)
    joined_blocks = joined.reshape(block_count, BLK, both_width)
    padded = padded_2(joined, (("ctx", 0),), BLK)
    padded = padded.reshape(block_count + 2, BLK, both_width)
    window_kv = jnp.stack(
        [padded[0:block_count], padded[1 : block_count + 1], padded[2 : block_count + 2]], axis=1
    )
    global_ids = block_list[0, 0:GLOB]
    global_owner = global_ids // block_count
    global_local = global_ids % block_count
    fetched_list = []
    for column in range(GLOB):
        owned = lax.dynamic_index_in_dim(joined_blocks, global_local[column], 0, keepdims=False)
        fetched_list.append(spread(owned, "ctx", global_owner[column]))
    global_kv = jnp.stack(fetched_list, axis=0)
    random_ids = block_list[:, GLOB + WIN :].reshape(-1)
    ref_count = random_ids.shape[0]
    capacity = (ref_count + shard_total - 1) // shard_total
    slot_count = shard_total * capacity
    ref_owner = random_ids // block_count
    ref_local = random_ids % block_count
    ref_order = jnp.arange(ref_count, dtype=jnp.int32)
    earlier = (ref_owner[:, None] == ref_owner[None, :]) & (ref_order[None, :] < ref_order[:, None])
    ref_rank = jnp.sum(earlier, axis=1)
    ref_slot = ref_owner * capacity + ref_rank
    slot_hit = ref_slot[:, None] == jnp.arange(slot_count, dtype=jnp.int32)[None, :]
    wanted = jnp.sum(jnp.where(slot_hit, ref_local[:, None] + 1, 0), axis=0) - 1
    asked = lax.all_to_all(
        wanted.reshape(shard_total, capacity), "ctx", split_axis=0, concat_axis=0, tiled=True
    )
    valid_ask = asked >= 0
    served = jnp.where(
        valid_ask[:, :, None, None],
        joined_blocks[jnp.maximum(asked, 0)],
        jnp.zeros((), jnp.bfloat16),
    )
    arrived = lax.all_to_all(served, "ctx", split_axis=0, concat_axis=0, tiled=True).reshape(
        slot_count, BLK, both_width
    )
    random_kv = arrived[ref_slot].reshape(block_count, RAND, BLK, both_width)
    list_len = GLOB + WIN + RAND
    global_rep = jnp.broadcast_to(global_kv[None], (block_count, GLOB, BLK, both_width))
    listed_kv = jnp.concatenate([global_rep, window_kv, random_kv], axis=1)
    keys_here = listed_kv[..., :head_width].reshape(block_count, list_len * BLK, kv_heads, HD)
    values_here = listed_kv[..., head_width:].reshape(block_count, list_len * BLK, kv_heads, HD)
    group_size = queries.shape[1] // head_width
    query_tiles = queries.reshape(block_count, BLK, kv_heads, group_size, HD)
    grad_tiles = out_grad.reshape(block_count, BLK, kv_heads, group_size, HD)
    attended, query_grad, key_part, value_part = lax.map(
        attend_block, (query_tiles, grad_tiles, keys_here, values_here)
    )
    grad_kv = jnp.concatenate(
        [
            key_part.reshape(block_count, list_len, BLK, head_width),
            value_part.reshape(block_count, list_len, BLK, head_width),
        ],
        axis=-1,
    )
    window_grad = grad_kv[:, GLOB : GLOB + WIN]
    zero_block = jnp.zeros((1, BLK, both_width), jnp.float32)
    rim_acc = (
        jnp.concatenate([window_grad[:, 0], zero_block, zero_block], axis=0)
        + jnp.concatenate([zero_block, window_grad[:, 1], zero_block], axis=0)
        + jnp.concatenate([zero_block, zero_block, window_grad[:, 2]], axis=0)
    )
    from_left = shifted(rim_acc[block_count + 1].astype(jnp.bfloat16), "ctx", 1).astype(jnp.float32)
    from_right = shifted(rim_acc[0].astype(jnp.bfloat16), "ctx", -1).astype(jnp.float32)
    own_grads = rim_acc[1 : block_count + 1]
    own_grads = own_grads.at[0].add(from_left)
    own_grads = own_grads.at[block_count - 1].add(from_right)
    global_terms = lax.psum(jnp.sum(grad_kv[:, 0:GLOB], axis=0), "ctx")
    global_place = (global_local[:, None] == jnp.arange(block_count, dtype=jnp.int32)[None, :]) & (
        global_owner == my_index
    )[:, None]
    own_grads = own_grads + jnp.einsum(
        "ro,rhn->ohn",
        global_place.astype(jnp.float32),
        global_terms,
        precision=lax.Precision.HIGHEST,
    )
    random_grad = grad_kv[:, GLOB + WIN :].reshape(ref_count, BLK, both_width)
    outgoing = jnp.zeros((slot_count, BLK, both_width), jnp.float32).at[ref_slot].set(random_grad)
    returned = lax.all_to_all(
        outgoing.reshape(shard_total, capacity, BLK, both_width).astype(jnp.bfloat16),
        "ctx",
        split_axis=0,
        concat_axis=0,
        tiled=True,
    ).astype(jnp.float32)
    returned = returned.reshape(slot_count, BLK, both_width)
    slot_place = (
        asked.reshape(slot_count)[:, None] == jnp.arange(block_count, dtype=jnp.int32)[None, :]
    ).astype(jnp.float32)
    own_grads = own_grads + jnp.einsum(
        "sj,sxc->jxc", slot_place, returned, precision=lax.Precision.HIGHEST
    )
    own_grads = own_grads.reshape(tokens_here, both_width).astype(jnp.bfloat16)
    key_grad, value_grad = (
        lax.all_to_all(own_grads[:, :head_width], "tp", split_axis=0, concat_axis=1, tiled=True),
        lax.all_to_all(own_grads[:, head_width:], "tp", split_axis=0, concat_axis=1, tiled=True),
    )
    return (
        attended.reshape(tokens_here, -1),
        query_grad.reshape(tokens_here, -1),
        key_grad,
        value_grad,
    )


def solution(mesh):
    in_specs = (
        P("ctx", "tp"),
        P(("ctx", "tp"), None),
        P(("ctx", "tp"), None),
        P("ctx", "tp"),
        P("ctx", None),
    )
    out_specs = (P("ctx", "tp"), P("ctx", "tp"), P(("ctx", "tp"), None), P(("ctx", "tp"), None))
    return jax.shard_map(shards, mesh=mesh, in_specs=in_specs, out_specs=out_specs, check_vma=False)
```

profile of v0, /device:TPU:0, one launch (start us, length us, event | category | flops | bytes accessed | tf_op | source)
XLA Modules:
  0.0 400.3 jit_solution(2010313917641656042)
XLA Ops:
  9.9 5.2 %all-to-all-start.2 = ((s32[8,1,2]{2,1,0:T(1,128)}), s32[8,1,2]{2,1,0:T(1,128)S(1)}, u32[]{:S(2)}, u32[]{:S(2)}) async-start(s32[8,1,2]{2,1,0:T(1,128)} %bitcast.45), calls=%async_computation.2 | async-start | bytes 8192 | tf_op jit(solution)/shard_map/all_to_all | solution.py:113
  19.7 4.9 %all-to-all-start = ((bf16[160,4,256]{2,0,1:T(8,128)(2,1)}), bf16[160,4,256]{2,0,1:T(8,128)(2,1)S(1)}, u32[]{:S(2)}, u32[]{:S(2)}) async-start(bf16[160,4,256]{2,0,1:T(8,128)(2,1)} %bitcast.208), calls=%async_computation | async-start | bytes 655360 | tf_op jit(solution)/shard_map/all_to_all | solution.py:80
  26.3 8.6 %all-to-all-done = bf16[160,4,256]{2,0,1:T(8,128)(2,1)S(1)} async-done(((bf16[160,4,256]{2,0,1:T(8,128)(2,1)}), bf16[160,4,256]{2,0,1:T(8,128)(2,1)S(1)}, u32[]{:S(2)}, u32[]{:S(2)}) %all-to-all-start) | async-done | bytes 327712 | tf_op jit(solution)/shard_map/all_to_all | solution.py:80
  34.9 3.5 all-to-all-start.1
  40.5 6.4 %all-to-all-done.1 = bf16[160,4,256]{2,0,1:T(8,128)(2,1)S(1)} async-done(((bf16[160,4,256]{2,0,1:T(8,128)(2,1)}), bf16[160,4,256]{2,0,1:T(8,128)(2,1)S(1)}, u32[]{:S(2)}, u32[]{:S(2)}) %all-to-all-start.1) | async-done | bytes 327712 | tf_op jit(solution)/shard_map/all_to_all | solution.py:81
  49.2 3.6 all-to-all-start.3
  63.6 3.8 reshape.356
  67.4 3.8 reshape.357
  71.1 46.1 %all-reduce.8.cloned.1.call-done = (bf16[1,128,512]{2,1,0:T(8,128)(2,1)}, bf16[1,128,512]{2,1,0:T(8,128)(2,1)}) async-done(((bf16[1,128,512]{2,1,0:T(8,128)(2,1)}, bf16[1,128,512]{2,1,0:T(8,128)(2,1)}), (bf16[1,128,512]{2,1,0:T(8,128)(2,1)}, bf16[1,128,512]{2,1,0:T(8,128)(2,1)})) %all-reduce.8.cloned.1.call-update) | async-done | bytes 262160 | tf_op jit(solution)/shard_map/psum | solution.py:31
  127.3 4.5 %fusion.48 = (bf16[5,8,128,256]{3,2,1,0:T(8,128)(2,1)S(1)}, bf16[5,8,128,256]{3,2,1,0:T(8,128)(2,1)}) fusion(bf16[5,8,128,512]{3,2,1,0:T(8,128)(2,1)} %constant_dynamic-update-slice_fusion.2), kind=kLoop, calls=%fused_computation.117 | loop fusion | bytes 10485760 | tf_op jit(solution)/shard_map/slice | solution.py:129
  131.9 4.9 %reshape.354 = bf16[5,1024,2,128]{3,2,1,0:T(2,128)(2,1)} reshape(bf16[5,8,128,256]{3,2,1,0:T(8,128)(2,1)} %get-tuple-element.156) | data formatting | bytes 5242880 | tf_op jit(solution)/shard_map/reshape | solution.py:130
  139.6 105.0 %while.18 = (s32[]{:T(128)}, bf16[5,128,2,4,128]{4,3,2,1,0:T(4,128)(2,1)}, bf16[5,128,2,4,128]{4,3,2,1,0:T(4,128)(2,1)}, f32[5,1024,2,128]{1,3,2,0:T(8,128)}, f3...) while((s32[]{:T(128)}, ...), condition=%wide.region_8.9_spmd, body=%wide.region_4.8_spmd.sunk | while | flops 1628567552 | bytes 73709224 | solution.py:134
  146.1 4.1 %fusion.77 = f32[5,1024,2,128]{1,3,2,0:T(8,128)} fusion(f32[5,1024,2,128]{1,3,2,0:T(8,128)} %get-tuple-element.256, s32[]{:T(128)} %get-tuple-element.252, f32[2,1024,128,4]{2,1,3,0:T(8,128)} %copy-done, f32[2,4,128]{2,1,0:T(4,128)S(1)} %bitcast.289, bf16[1,128,2,4,128]{1,4,3,2,0:T(8,128)(2,1)S(1)} %copy.212), kind=kOutput, calls=%fused_computation.14.clone.1 | convolution fusion | flops 271581184 | bytes 5509632 | tf_op jit(solution)/shard_map/while/body/eval_jaxpr/kgqn,qkgd->nkd/dot_general | solution.py:64
  167.1 4.1 %fusion.77 = f32[5,1024,2,128]{1,3,2,0:T(8,128)} fusion(f32[5,1024,2,128]{1,3,2,0:T(8,128)} %get-tuple-element.256, s32[]{:T(128)} %get-tuple-element.252, f32[2,1024,128,4]{2,1,3,0:T(8,128)} %copy-done, f32[2,4,128]{2,1,0:T(4,128)S(1)} %bitcast.289, bf16[1,128,2,4,128]{1,4,3,2,0:T(8,128)(2,1)S(1)} %copy.212), kind=kOutput, calls=%fused_computation.14.clone.1 | convolution fusion | flops 271581184 | bytes 5509632 | tf_op jit(solution)/shard_map/while/body/eval_jaxpr/kgqn,qkgd->nkd/dot_general | solution.py:64
  173.1 3.2 multiply_reduce_fusion.2
  188.1 4.2 %fusion.77 = f32[5,1024,2,128]{1,3,2,0:T(8,128)} fusion(f32[5,1024,2,128]{1,3,2,0:T(8,128)} %get-tuple-element.256, s32[]{:T(128)} %get-tuple-element.252, f32[2,1024,128,4]{2,1,3,0:T(8,128)} %copy-done, f32[2,4,128]{2,1,0:T(4,128)S(1)} %bitcast.289, bf16[1,128,2,4,128]{1,4,3,2,0:T(8,128)(2,1)S(1)} %copy.212), kind=kOutput, calls=%fused_computation.14.clone.1 | convolution fusion | flops 271581184 | bytes 5509632 | tf_op jit(solution)/shard_map/while/body/eval_jaxpr/kgqn,qkgd->nkd/dot_general | solution.py:64
  209.1 4.2 %fusion.77 = f32[5,1024,2,128]{1,3,2,0:T(8,128)} fusion(f32[5,1024,2,128]{1,3,2,0:T(8,128)} %get-tuple-element.256, s32[]{:T(128)} %get-tuple-element.252, f32[2,1024,128,4]{2,1,3,0:T(8,128)} %copy-done, f32[2,4,128]{2,1,0:T(4,128)S(1)} %bitcast.289, bf16[1,128,2,4,128]{1,4,3,2,0:T(8,128)(2,1)S(1)} %copy.212), kind=kOutput, calls=%fused_computation.14.clone.1 | convolution fusion | flops 271581184 | bytes 5509632 | tf_op jit(solution)/shard_map/while/body/eval_jaxpr/kgqn,qkgd->nkd/dot_general | solution.py:64
  230.2 4.1 %fusion.77 = f32[5,1024,2,128]{1,3,2,0:T(8,128)} fusion(f32[5,1024,2,128]{1,3,2,0:T(8,128)} %get-tuple-element.256, s32[]{:T(128)} %get-tuple-element.252, f32[2,1024,128,4]{2,1,3,0:T(8,128)} %copy-done, f32[2,4,128]{2,1,0:T(4,128)S(1)} %bitcast.289, bf16[1,128,2,4,128]{1,4,3,2,0:T(8,128)(2,1)S(1)} %copy.212), kind=kOutput, calls=%fused_computation.14.clone.1 | convolution fusion | flops 271581184 | bytes 5509632 | tf_op jit(solution)/shard_map/while/body/eval_jaxpr/kgqn,qkgd->nkd/dot_general | solution.py:64
  244.6 6.1 %copy.183 = f32[160,8,8,128]{3,2,1,0:T(8,128)} copy(f32[160,8,8,128]{3,1,2,0:T(8,128)} %bitcast.284) | data formatting | bytes 10485760
  250.7 6.1 %copy.142 = f32[5,8,128,256]{3,2,0,1:T(8,128)} copy(f32[5,8,128,256]{2,1,3,0:T(8,128)} %bitcast.267) | data formatting | bytes 10485760 | tf_op jit(solution)/shard_map/reshape | solution.py:139
  256.8 6.1 %copy.184 = f32[160,8,8,128]{3,2,1,0:T(8,128)} copy(f32[160,8,8,128]{3,1,2,0:T(8,128)} %bitcast.285) | data formatting | bytes 10485760
  263.0 6.2 %copy.143 = f32[5,8,128,256]{3,2,0,1:T(8,128)} copy(f32[5,8,128,256]{2,1,3,0:T(8,128)} %bitcast.268) | data formatting | bytes 10485760 | tf_op jit(solution)/shard_map/reshape | solution.py:140
  276.7 7.8 %scatter_fusion = f32[16,128,512]{2,1,0:T(8,128)} fusion(f32[16,128,512]{2,1,0:T(8,128)} %broadcast_in_dim.74, s32[15]{0:T(128)S(1)} %fusion.42, f32[15,128,512]{2,1,0:T(8,128)} %bitcast.269), kind=kCustom, calls=%fused_computation.2 | custom fusion | bytes 11796540 | tf_op jit(solution)/shard_map/scatter | solution.py:167
  287.0 3.5 copy.148
  290.5 4.4 %all-to-all-start.4 = ((bf16[8,2,128,512]{3,1,2,0:T(2,128)(2,1)}), bf16[8,2,128,512]{3,1,2,0:T(2,128)(2,1)}, u32[]{:S(2)}, u32[]{:S(2)}) async-start(bf16[8,2,128,512]{3,1,2,0:T(2,128)(2,1)} %copy.148), calls=%async_computation.4 | async-start | bytes 4194304 | tf_op jit(solution)/shard_map/all_to_all | solution.py:168
  304.4 21.5 %collective-permute-done.2 = bf16[128,512]{1,0:T(8,128)(2,1)S(1)} collective-permute-done((bf16[128,512]{1,0:T(8,128)(2,1)S(1)}, bf16[128,512]{1,0:T(8,128)(2,1)S(1)}, u32[]{:S(2)}, u32[]{:S(2)}) %collective-permute-start.2) | collective-permute-done | bytes 131104 | tf_op jit(solution)/shard_map/ppermute | solution.py:37
  329.6 6.0 %copy.149 = bf16[8,2,128,512]{3,1,0,2:T(2,128)(2,1)} copy(bf16[8,2,128,512]{3,1,2,0:T(2,128)(2,1)} %all-to-all-done.4) | data formatting | bytes 4194304 | tf_op jit(solution)/shard_map/all_to_all | solution.py:168
  335.7 4.1 %reshape.365 = bf16[16,128,512]{2,0,1:T(8,128)(2,1)} reshape(bf16[8,2,128,512]{3,1,0,2:T(2,128)(2,1)} %copy.149) | data formatting | bytes 4194304 | tf_op jit(solution)/shard_map/reshape | solution.py:175
  341.9 20.8 %all-reduce.6.cloned.1.call-done = f32[2,128,512]{2,0,1:T(2,128)} async-done(((f32[2,128,512]{2,0,1:T(2,128)}), f32[2,128,512]{2,0,1:T(2,128)}) %all-reduce.6.cloned.1.call-update) | async-done | bytes 524304 | tf_op jit(solution)/shard_map/psum | solution.py:156
  366.7 13.8 %all_to_all.92 = bf16[4,160,256]{2,1,0:T(8,128)(2,1)S(1)} all-to-all(bf16[4,160,256]{2,1,0:T(8,128)(2,1)S(1)} %bitcast.292), channel_id=1, replica_groups=mesh['ctx'=8,'tp'=4] {'tp'}, dimensions={0} | all-to-all | bytes 655360 | tf_op jit(solution)/shard_map/all_to_all | solution.py:184
  380.5 3.5 all-to-all-start.6
  388.3 4.5 %all-to-all-done.6 = bf16[4,160,256]{2,1,0:T(8,128)(2,1)S(1)} async-done(((bf16[4,160,256]{2,1,0:T(8,128)(2,1)}), bf16[4,160,256]{2,1,0:T(8,128)(2,1)S(1)}, u32[]{:S(2)}, u32[]{:S(2)}) %all-to-all-start.6) | async-done | bytes 327712 | tf_op jit(solution)/shard_map/all_to_all | solution.py:185
  (191 shorter events, 147.0 us)
Async XLA Ops:
  9.9 9.8 %all-to-all-start.2 = ((s32[8,1,2]{2,1,0:T(1,128)}), s32[8,1,2]{2,1,0:T(1,128)S(1)}, u32[]{:S(2)}, u32[]{:S(2)}) async-start(s32[8,1,2]{2,1,0:T(1,128)} %bitcast.45), calls=%async_computation.2 | async-start | bytes 8192 | tf_op jit(solution)/shard_map/all_to_all | solution.py:113
  19.7 15.2 %all-to-all-start = ((bf16[160,4,256]{2,0,1:T(8,128)(2,1)}), bf16[160,4,256]{2,0,1:T(8,128)(2,1)S(1)}, u32[]{:S(2)}, u32[]{:S(2)}) async-start(bf16[160,4,256]{2,0,1:T(8,128)(2,1)} %bitcast.208), calls=%async_computation | async-start | bytes 655360 | tf_op jit(solution)/shard_map/all_to_all | solution.py:80
  34.9 12.1 %all-to-all-start.1 = ((bf16[160,4,256]{2,0,1:T(8,128)(2,1)}), bf16[160,4,256]{2,0,1:T(8,128)(2,1)S(1)}, u32[]{:S(2)}, u32[]{:S(2)}) async-start(bf16[160,4,256]{2,0,1:T(8,128)(2,1)} %bitcast.207), calls=%async_computation.1 | async-start | bytes 655360 | tf_op jit(solution)/shard_map/all_to_all | solution.py:81
  49.2 73.2 %all-to-all-start.3 = ((bf16[8,2,128,512]{3,2,1,0:T(8,128)(2,1)}), bf16[8,2,128,512]{3,2,1,0:T(8,128)(2,1)S(1)}, u32[]{:S(2)}, u32[]{:S(2)}) async-start(bf16[8,2,128,512]{3,2,1,0:T(8,128)(2,1)} %broadcast_select_fusion), calls=%async_computation.3 | async-start | bytes 4194304 | tf_op jit(solution)/shard_map/all_to_all | solution.py:122
  52.8 64.5 %all-reduce.8.cloned.1.call-start = ((), (), s32[]{:S(2)}) async-start(), calls=%async_computation.8 | async-start | bytes 524288 | tf_op jit(solution)/shard_map/psum | solution.py:31
  60.9 57.4 %collective-permute-start = (bf16[128,512]{1,0:T(8,128)(2,1)S(1)}, bf16[128,512]{1,0:T(8,128)(2,1)S(1)}, u32[]{:S(2)}, u32[]{:S(2)}) collective-permute-start(bf16[128,512]{1,0:T(8,128)(2,1)S(1)} %get-tuple-element.164), channel_id=1, source_target_pairs={{0,4},{4,8},{8,12},{12,16},{16,20},{20,24},{24,28},{28,0},{1,5},{5... | collective-permute-start | bytes 393224 | tf_op jit(solution)/shard_map/ppermute | solution.py:20
  61.3 57.0 %collective-permute-start.1 = (bf16[128,512]{1,0:T(8,128)(2,1)S(1)}, bf16[128,512]{1,0:T(8,128)(2,1)S(1)}, u32[]{:S(2)}, u32[]{:S(2)}) collective-permute-start(bf16[128,512]{1,0:T(8,128)(2,1)S(1)} %get-tuple-element.163), channel_id=1, source_target_pairs={{4,0},{8,4},{12,8},{16,12},{20,16},{24,20},{28,24},{0,28},{5,1},{9... | collective-permute-start | bytes 393224 | tf_op jit(solution)/shard_map/ppermute | solution.py:22
  142.8 2.1 copy-start
  152.1 3.5 copy-start.1
  163.7 2.1 copy-start
  173.0 3.5 copy-start.1
  184.7 2.1 copy-start
  194.1 3.5 copy-start.1
  205.7 2.1 copy-start
  215.1 3.5 copy-start.1
  226.8 2.1 copy-start
  236.1 3.5 copy-start.1
  290.5 39.1 %all-to-all-start.4 = ((bf16[8,2,128,512]{3,1,2,0:T(2,128)(2,1)}), bf16[8,2,128,512]{3,1,2,0:T(2,128)(2,1)}, u32[]{:S(2)}, u32[]{:S(2)}) async-start(bf16[8,2,128,512]{3,1,2,0:T(2,128)(2,1)} %copy.148), calls=%async_computation.4 | async-start | bytes 4194304 | tf_op jit(solution)/shard_map/all_to_all | solution.py:168
  294.9 67.7 %all-reduce.6.cloned.1.call-start = ((), (), s32[]{:S(2)}) async-start(), calls=%async_computation.7 | async-start | bytes 1048576 | tf_op jit(solution)/shard_map/psum | solution.py:156
  298.2 27.7 %collective-permute-start.2 = (bf16[128,512]{1,0:T(8,128)(2,1)S(1)}, bf16[128,512]{1,0:T(8,128)(2,1)S(1)}, u32[]{:S(2)}, u32[]{:S(2)}) collective-permute-start(bf16[128,512]{1,0:T(8,128)(2,1)S(1)} %get-tuple-element.158), channel_id=1, source_target_pairs={{0,4},{4,8},{8,12},{12,16},{16,20},{20,24},{24,28},{28,0},{1,5},{5... | collective-permute-start | bytes 393224 | tf_op jit(solution)/shard_map/ppermute | solution.py:37
  302.0 24.8 %collective-permute-start.3 = (bf16[128,512]{1,0:T(8,128)(2,1)S(1)}, bf16[128,512]{1,0:T(8,128)(2,1)S(1)}, u32[]{:S(2)}, u32[]{:S(2)}) collective-permute-start(bf16[128,512]{1,0:T(8,128)(2,1)S(1)} %get-tuple-element.157), channel_id=1, source_target_pairs={{0,28},{4,0},{8,4},{12,8},{16,12},{20,16},{24,20},{28,24},{1,29},{... | collective-permute-start | bytes 393224 | tf_op jit(solution)/shard_map/ppermute | solution.py:37
  329.6 6.1 %copy-start.2 = (f32[5,128,512]{2,0,1:T(8,128)}, f32[5,128,512]{2,0,1:T(8,128)S(1)}, u32[]{:S(2)}) copy-start(f32[5,128,512]{2,0,1:T(8,128)S(1)} %scatter-add.9) | copy-start | bytes 3932164
  365.7 18.3 %copy-start.3 = (bf16[5,128,2,4,128]{4,3,2,1,0:T(4,128)(2,1)S(1)}, bf16[5,128,2,4,128]{4,3,2,1,0:T(4,128)(2,1)}, u32[]{:S(2)}) copy-start(bf16[5,128,2,4,128]{4,3,2,1,0:T(4,128)(2,1)} %get-tuple-element.78) | copy-start | bytes 3932164
  366.7 19.1 %copy-start.4 = (bf16[5,128,2,4,128]{4,3,2,1,0:T(4,128)(2,1)S(1)}, bf16[5,128,2,4,128]{4,3,2,1,0:T(4,128)(2,1)}, u32[]{:S(2)}) copy-start(bf16[5,128,2,4,128]{4,3,2,1,0:T(4,128)(2,1)} %get-tuple-element.79) | copy-start | bytes 3932164
  380.5 12.2 %all-to-all-start.6 = ((bf16[4,160,256]{2,1,0:T(8,128)(2,1)}), bf16[4,160,256]{2,1,0:T(8,128)(2,1)S(1)}, u32[]{:S(2)}, u32[]{:S(2)}) async-start(bf16[4,160,256]{2,1,0:T(8,128)(2,1)} %bitcast.65), calls=%async_computation.6 | async-start | bytes 655360 | tf_op jit(solution)/shard_map/all_to_all | solution.py:185
Sparse Core Ops, SparseCore 0:
  61.0 56.2 all-reduce.7
  302.0 60.5 all-reduce.5
where the time goes:
time: 403 us; the launch traced here: 400 us
  local copies, waits for them, and re-layouts  139 us (34%)
  waiting for transfers between devices  111 us (28%)
  matrix products  63.8 us (16%)
  starting transfers between devices  30.5 us (8%)
  other arithmetic  22.5 us (6%)
  between operations  19.5 us (5%)
  blocking collectives  13.8 us (3%)
    psum x1, waiting for transfers between devices, spread(): return lax.psum(jnp.where(mine, x, jnp.zeros_like(x)), axis)  46.1 us
    dynamic_slice x30, local copies, waits for them, and re-layouts, shards(): lax.map(attend_block, (query_tiles, grad_tiles, keys_here, values_here))  27.7 us
    ppermute x2, waiting for transfers between devices, shifted(): return lax.ppermute(value, axis, pairs)  21.5 us
    psum x1, waiting for transfers between devices, shards(): global_terms = lax.psum(jnp.sum(grad_kv[:, 0:GLOB], axis=0), 'ctx')  20.8 us
    dot_general x5, matrix products, attend_block(): jnp.einsum('kgqn,qkgd->nkd', weights_low, grad_tile, preferred_element_ty...  20.6 us
    dot_general x5, matrix products, attend_block(): jnp.einsum('kgqn,nkd->qkgd', weights_low, values_tile, preferred_element_...  16.1 us
    unnamed x11, local copies, waits for them, and re-layouts  15.3 us
    all_to_all x1, blocking collectives, shards(): lax.all_to_all(own_grads[:, :head_width], 'tp', split_axis=0, concat_axis...  13.8 us
  transfers between devices with their start and end apart: 12, of which 7 were waited for; matrix products, arithmetic and copies ran while one was open for 12% of the time, Pallas kernels for 0%

commit v1 on v0

--- a/solution.py
+++ b/solution.py
@@ -1,6 +1,10 @@
+import functools
+
 import jax
 import jax.numpy as jnp
 from jax import lax
+from jax.experimental import pallas as pl
+from jax.experimental.pallas import tpu as pltpu
 from jax.sharding import PartitionSpec as P
 
 HD = 128
@@ -71,7 +75,7 @@
     return (attended, query_grad, key_part, value_part)
 
 
-def shards(queries, key_rows, value_rows, out_grad, block_list):
+def sparse_plan(queries, key_rows, value_rows, out_grad, block_list):
     tokens_here = queries.shape[0]
     block_count = tokens_here // BLK
     shard_total = lax.axis_size("ctx")
@@ -192,7 +196,362 @@
     )
 
 
+LOG2E = 1.4426950408889634
+DENSE_SHARDS = 8
+NT = (((1,), (1,)), ((), ()))
+TN = (((0,), (0,)), ((), ()))
+
+
+def swap(value, axis, mask):
+    count = lax.axis_size(axis)
+    return lax.ppermute(value, axis, [(i, i ^ mask) for i in range(count)])
+
+
+def rows_of(quarter, shard, spot, tokens, me_tp):
+    return pl.multiple_of(shard * tokens + (spot ^ me_tp) * quarter, 16)
+
+
+def gather_pieces(piece_refs, pieces, tokens, me_tp, buffer, sems):
+    copies = []
+    for ref, (shard, first, count) in zip(piece_refs, pieces):
+        quarter = ref.shape[1]
+        for at in range(count):
+            start = rows_of(quarter, shard, first + at, tokens, me_tp)
+            copies.append(
+                pltpu.make_async_copy(
+                    ref.at[at], buffer.at[pl.ds(start, quarter)], sems.at[len(copies)]
+                )
+            )
+    for copy in copies:
+        copy.start()
+    for copy in copies:
+        copy.wait()
+
+
+def scatter_pieces(acc, buffer, targets, tokens, me_tp, sems):
+    copies = []
+    for ref, shard in targets:
+        spots, quarter = ref.shape[0], ref.shape[1]
+        rows = slice(shard * tokens, (shard + 1) * tokens)
+        buffer[rows] = acc[rows].astype(buffer.dtype)
+        for spot in range(spots):
+            start = rows_of(quarter, shard, spot, tokens, me_tp)
+            copy = pltpu.make_async_copy(
+                buffer.at[pl.ds(start, quarter)], ref.at[spot], sems.at[len(copies)]
+            )
+            copy.start()
+            copies.append(copy)
+    for copy in copies:
+        copy.wait()
+
+
+def list_rows(place_ref, row, width, buffer, listed):
+    places = []
+    for column in range(width):
+        place = pl.multiple_of(place_ref[row * width + column] * BLK, BLK)
+        listed[0, column * BLK : (column + 1) * BLK] = buffer[pl.ds(place, BLK)]
+        places.append(place)
+    return places
+
+
+def fold(value, op):
+    rows, width = value.shape
+    return op(value.reshape(rows // 8, 8, width), axis=0)
+
+
+def probs_kernel(pieces, tokens, width, heads, group, place_ref, tp_ref, *refs):
+    count = len(pieces)
+    query_ref, grad_ref = refs[0:2]
+    piece_refs = refs[2 : 2 + count]
+    exp_ref, query_t_ref, grad_t_ref, inv_ref, listed_ref = refs[2 + count : 7 + count]
+    out_refs = refs[7 + count : 11 + count]
+    buffer, acc, score_ref, load_sems, store_sems = refs[11 + count :]
+    row = pl.program_id(0)
+    me_tp = tp_ref[0]
+
+    @pl.when(row == 0)
+    def _():
+        acc[...] = jnp.zeros_like(acc)
+        gather_pieces(piece_refs, pieces, tokens, me_tp, buffer, load_sems)
+
+    places = list_rows(place_ref, row, width, buffer, listed_ref)
+    factor = LOG2E * float(HD) ** (-0.5)
+    for head in range(heads):
+        lanes = slice(head * HD, (head + 1) * HD)
+        parts = [
+            slice((head * group + g) * HD, (head * group + g + 1) * HD) for g in range(group)
+        ]
+        query_t = jnp.concatenate([query_ref[:, part].T for part in parts], axis=1)
+        grad_t = jnp.concatenate([grad_ref[:, part].T for part in parts], axis=1)
+        query_t_ref[0, head] = query_t
+        score_ref[head] = jnp.dot(
+            listed_ref[0, :, lanes], query_t, preferred_element_type=jnp.float32
+        )
+        top = None
+        for column in range(width):
+            chunk = slice(column * BLK, (column + 1) * BLK)
+            here = fold(score_ref[head, chunk], jnp.max)
+            top = here if top is None else jnp.maximum(top, here)
+        top = jnp.max(top, axis=0, keepdims=True) * factor
+        total = None
+        for column in range(width):
+            chunk = slice(column * BLK, (column + 1) * BLK)
+            weight = jnp.exp2(score_ref[head, chunk] * factor - top)
+            exp_ref[0, head, chunk] = weight.astype(jnp.bfloat16)
+            here = fold(weight, jnp.sum)
+            total = here if total is None else total + here
+        inverse = 1.0 / jnp.sum(total, axis=0, keepdims=True)
+        inv_ref[0, head] = jnp.broadcast_to(inverse, inv_ref.shape[2:])
+        grad_low = (grad_t.astype(jnp.float32) * inverse).astype(jnp.bfloat16)
+        grad_t_ref[0, head] = grad_low
+        part = lax.dot_general(exp_ref[0, head], grad_low, NT, preferred_element_type=jnp.float32)
+        for column in range(width):
+            acc[pl.ds(places[column], BLK), lanes] += part[column * BLK : (column + 1) * BLK]
+
+    @pl.when(row == pl.num_programs(0) - 1)
+    def _():
+        write_out(acc, buffer, out_refs, tokens, me_tp, store_sems)
+
+
+def write_out(acc, buffer, out_refs, tokens, me_tp, sems):
+    near_ref, far3_ref, far12_ref, far0_ref = out_refs
+    targets = [(far3_ref, 7), (far12_ref.at[0], 3), (far12_ref.at[1], 5), (far0_ref, 1)]
+    targets += [(near_ref.at[k], 2 * k) for k in (3, 1, 2, 0)]
+    scatter_pieces(acc, buffer, targets, tokens, me_tp, sems)
+
+
+def scores_kernel(pieces, tokens, width, heads, place_ref, tp_ref, *refs):
+    count = len(pieces)
+    exp_ref, query_t_ref, grad_t_ref, inv_ref = refs[0:4]
+    piece_refs = refs[4 : 4 + count]
+    ds_ref, listed_ref = refs[4 + count : 6 + count]
+    out_refs = refs[6 + count : 10 + count]
+    buffer, acc, dprob_ref, load_sems, store_sems = refs[10 + count :]
+    row = pl.program_id(0)
+    me_tp = tp_ref[0]
+
+    @pl.when(row == 0)
+    def _():
+        acc[...] = jnp.zeros_like(acc)
+        gather_pieces(piece_refs, pieces, tokens, me_tp, buffer, load_sems)
+
+    places = list_rows(place_ref, row, width, buffer, listed_ref)
+    for head in range(heads):
+        lanes = slice(head * HD, (head + 1) * HD)
+        dprob_ref[head] = jnp.dot(
+            listed_ref[0, :, lanes], grad_t_ref[0, head], preferred_element_type=jnp.float32
+        )
+        delta = None
+        for column in range(width):
+            chunk = slice(column * BLK, (column + 1) * BLK)
+            weight = exp_ref[0, head, chunk].astype(jnp.float32)
+            here = fold(weight * dprob_ref[head, chunk], jnp.sum)
+            delta = here if delta is None else delta + here
+        delta = jnp.sum(delta, axis=0, keepdims=True) * inv_ref[0, head, 0:1]
+        for column in range(width):
+            chunk = slice(column * BLK, (column + 1) * BLK)
+            weight = exp_ref[0, head, chunk].astype(jnp.float32)
+            ds_ref[0, head, chunk] = (weight * (dprob_ref[head, chunk] - delta)).astype(
+                jnp.bfloat16
+            )
+        part = lax.dot_general(
+            ds_ref[0, head], query_t_ref[0, head], NT, preferred_element_type=jnp.float32
+        ) * float(HD) ** (-0.5)
+        for column in range(width):
+            acc[pl.ds(places[column], BLK), lanes] += part[column * BLK : (column + 1) * BLK]
+
+    @pl.when(row == pl.num_programs(0) - 1)
+    def _():
+        write_out(acc, buffer, out_refs, tokens, me_tp, store_sems)
+
+
+def rows_kernel(heads, group, exp_ref, ds_ref, inv_ref, keys_ref, values_ref, out_ref, dq_ref):
+    for head in range(heads):
+        lanes = slice(head * HD, (head + 1) * HD)
+        attended = lax.dot_general(
+            values_ref[0, :, lanes], exp_ref[0, head], TN, preferred_element_type=jnp.float32
+        )
+        attended = attended * inv_ref[0, head, 0:1]
+        query_grad = lax.dot_general(
+            keys_ref[0, :, lanes], ds_ref[0, head], TN, preferred_element_type=jnp.float32
+        ) * float(HD) ** (-0.5)
+        for g in range(group):
+            part = slice((head * group + g) * HD, (head * group + g + 1) * HD)
+            out_ref[:, part] = attended[:, g * BLK : (g + 1) * BLK].T.astype(jnp.bfloat16)
+            dq_ref[:, part] = query_grad[:, g * BLK : (g + 1) * BLK].T.astype(jnp.bfloat16)
+
+
+def to_head_groups(rows):
+    me = lax.axis_index("tp")
+    count = lax.axis_size("tp")
+    width = rows.shape[1] // count
+    parts = []
+    for mask in range(count):
+        part = lax.dynamic_slice_in_dim(rows, (me ^ mask) * width, width, 1)
+        parts.append(part if mask == 0 else swap(part, "tp", mask))
+    return jnp.stack(parts)
+
+
+def to_quarters(pieces):
+    me = lax.axis_index("tp")
+    count, quarter, width = pieces.shape
+    out = jnp.zeros((quarter, count * width), pieces.dtype)
+    for mask in range(count):
+        part = pieces[mask] if mask == 0 else swap(pieces[mask], "tp", mask)
+        out = lax.dynamic_update_slice(out, part, (0, (me ^ mask) * width))
+    return out
+
+
+def gather_shards(own):
+    half = own.shape[0] // 2
+    across = swap(own, "ctx", 2)
+    along = swap(own, "ctx", 4)
+    first = swap(along[:half], "ctx", 2)
+    second = swap(across[half:], "ctx", 4)
+    near = [own, across, along, first, second]
+    far = [swap(part, "ctx", 1) for part in near]
+    return near + far
+
+
+def shard_pieces(count):
+    half = count // 2
+    near = [(0, 0, count), (2, 0, count), (4, 0, count), (6, 0, half), (6, half, half)]
+    return near + [(shard + 1, first, many) for shard, first, many in near]
+
+
+def sum_shards(near, far3, far12, far0):
+    half = near.shape[1] // 2
+    got3 = swap(far3, "ctx", 1)
+    got12 = swap(far12, "ctx", 1)
+    got0 = swap(far0, "ctx", 1)
+    diag_a = near[3, :half] + got3[:half]
+    diag_b = near[3, half:] + got3[half:]
+    from_x = swap(diag_a, "ctx", 2)
+    from_y = swap(diag_b, "ctx", 4)
+    across_a = near[1, :half] + got12[0, :half]
+    along_b = near[2, half:] + got12[1, half:]
+    own_a = swap(across_a, "ctx", 2)
+    own_b = swap(along_b, "ctx", 4)
+    across_b = near[1, half:] + got12[0, half:] + from_y
+    along_a = near[2, :half] + got12[1, :half] + from_x
+    more_b = swap(across_b, "ctx", 2)
+    more_a = swap(along_a, "ctx", 4)
+    own = near[0] + got0
+    return own + jnp.concatenate([own_a + more_a, own_b + more_b], axis=0)
+
+
+def dense_plan(queries, key_rows, value_rows, out_grad, block_list):
+    tokens = queries.shape[0]
+    blocks = tokens // BLK
+    shard_total = lax.axis_size("ctx")
+    quarters = lax.axis_size("tp")
+    width = block_list.shape[1]
+    head_width = key_rows.shape[1] // quarters
+    heads = head_width // HD
+    group = queries.shape[1] // head_width
+    rows = shard_total * tokens
+    me_ctx = lax.axis_index("ctx")
+    me_tp = lax.axis_index("tp").reshape(1)
+    places = ((block_list // blocks) ^ me_ctx) * blocks + block_list % blocks
+    places = places.reshape(-1)
+    quarter = tokens // quarters
+    pieces = shard_pieces(quarters)
+    list_len = width * BLK
+    query_rows = group * BLK
+    far_pieces = shard_total * quarters
+
+    any_spec = pl.BlockSpec(memory_space=pl.ANY)
+
+    def per_row(*shape):
+        return pl.BlockSpec((1, *shape), lambda i, *_: (i,) + (0,) * len(shape))
+
+    def flat(columns):
+        return pl.BlockSpec((BLK, columns), lambda i, *_: (i, 0))
+
+    def stash(*shape, dtype=jnp.bfloat16):
+        return jax.ShapeDtypeStruct((blocks, *shape), dtype)
+
+    sum_shapes = [
+        jax.ShapeDtypeStruct((shard_total // 2, quarters, quarter, head_width), jnp.bfloat16),
+        jax.ShapeDtypeStruct((quarters, quarter, head_width), jnp.bfloat16),
+        jax.ShapeDtypeStruct((2, quarters, quarter, head_width), jnp.bfloat16),
+        jax.ShapeDtypeStruct((quarters, quarter, head_width), jnp.bfloat16),
+    ]
+    scratch = [
+        pltpu.VMEM((rows, head_width), jnp.bfloat16),
+        pltpu.VMEM((rows, head_width), jnp.float32),
+        pltpu.VMEM((heads, list_len, query_rows), jnp.float32),
+        pltpu.SemaphoreType.DMA((far_pieces,)),
+        pltpu.SemaphoreType.DMA((far_pieces,)),
+    ]
+    params = pltpu.CompilerParams(vmem_limit_bytes=48 * 2**20)
+    flops = 4 * blocks * heads * list_len * query_rows * HD
+    big = (heads, list_len, query_rows)
+    small = (heads, HD, query_rows)
+    lse = (heads, 8, query_rows)
+    listed = (list_len, head_width)
+
+    keys = gather_shards(to_head_groups(key_rows))
+    values = gather_shards(to_head_groups(value_rows))
+
+    made = pl.pallas_call(
+        functools.partial(probs_kernel, pieces, tokens, width, heads, group),
+        grid_spec=pltpu.PrefetchScalarGridSpec(
+            num_scalar_prefetch=2,
+            grid=(blocks,),
+            in_specs=[flat(queries.shape[1]), flat(queries.shape[1])] + [any_spec] * len(pieces),
+            out_specs=[per_row(*big), per_row(*small), per_row(*small), per_row(*lse), per_row(*listed)]
+            + [any_spec] * 4,
+            scratch_shapes=scratch,
+        ),
+        out_shape=[
+            stash(*big),
+            stash(*small),
+            stash(*small),
+            stash(*lse, dtype=jnp.float32),
+            stash(*listed),
+        ]
+        + sum_shapes,
+        compiler_params=params,
+        cost_estimate=pl.CostEstimate(flops=flops, bytes_accessed=2**24, transcendentals=0),
+        name="probs",
+    )(places, me_tp, queries, out_grad, *keys)
+    exp_low, query_t, grad_t, inverse, keys_listed = made[:5]
+    value_sum = sum_shards(*made[5:])
+
+    made = pl.pallas_call(
+        functools.partial(scores_kernel, pieces, tokens, width, heads),
+        grid_spec=pltpu.PrefetchScalarGridSpec(
+            num_scalar_prefetch=2,
+            grid=(blocks,),
+            in_specs=[per_row(*big), per_row(*small), per_row(*small), per_row(*lse)]
+            + [any_spec] * len(pieces),
+            out_specs=[per_row(*big), per_row(*listed)] + [any_spec] * 4,
+            scratch_shapes=scratch,
+        ),
+        out_shape=[stash(*big), stash(*listed)] + sum_shapes,
+        compiler_params=params,
+        cost_estimate=pl.CostEstimate(flops=flops, bytes_accessed=2**24, transcendentals=0),
+        name="scores",
+    )(places, me_tp, exp_low, query_t, grad_t, inverse, *values)
+    ds_low, values_listed = made[:2]
+    key_sum = sum_shards(*made[2:])
+
+    attended, query_grad = pl.pallas_call(
+        functools.partial(rows_kernel, heads, group),
+        grid=(blocks,),
+        in_specs=[per_row(*big), per_row(*big), per_row(*lse), per_row(*listed), per_row(*listed)],
+        out_specs=[flat(queries.shape[1])] * 2,
+        out_shape=[jax.ShapeDtypeStruct(queries.shape, jnp.bfloat16)] * 2,
+        compiler_params=params,
+        cost_estimate=pl.CostEstimate(flops=flops, bytes_accessed=2**24, transcendentals=0),
+        name="rows",
+    )(exp_low, ds_low, inverse, keys_listed, values_listed)
+    return attended, query_grad, to_quarters(key_sum), to_quarters(value_sum)
+
+
 def solution(mesh):
+    dense = mesh.shape["ctx"] == DENSE_SHARDS and mesh.shape["tp"] % 4 == 0
     in_specs = (
         P("ctx", "tp"),
         P(("ctx", "tp"), None),
@@ -201,4 +560,10 @@
         P("ctx", None),
     )
     out_specs = (P("ctx", "tp"), P("ctx", "tp"), P(("ctx", "tp"), None), P(("ctx", "tp"), None))
-    return jax.shard_map(shards, mesh=mesh, in_specs=in_specs, out_specs=out_specs, check_vma=False)
+    return jax.shard_map(
+        dense_plan if dense else sparse_plan,
+        mesh=mesh,
+        in_specs=in_specs,
+        out_specs=out_specs,
+        check_vma=False,
+    )

time: 403 us -> 157 us (0.39)
  local copies, waits for them, and re-layouts: 139 us -> 10.8 us
  waiting for transfers between devices: 111 us -> 32 us
  matrix products: 63.8 us -> 0 us
  Pallas kernels: 0 us -> 61.4 us
  other arithmetic: 22.5 us -> 0.7 us
  starting transfers between devices: 30.5 us -> 50.8 us
  between operations: 19.5 us -> 0.98 us
  blocking collectives: 13.8 us -> 0 us
    psum x2 -> x0, waiting for transfers between devices: 66.9 us -> none  [the longest x1 46.1 us: spread(): return lax.psum(jnp.where(mine, x, jnp.zeros_like(x)), axis)]
    dot_general x32 -> x0, matrix products: 63.8 us -> none  [the longest x5 20.6 us: attend_block(): jnp.einsum('kgqn,qkgd->nkd', weights_low, grad_tile, preferred_element_ty...]
    pallas_call x0 -> x3, Pallas kernels: none -> 61.4 us  [the longest x1 26.3 us: dense_plan(): pl.pallas_call(functools.partial(scores_kernel, pieces, tokens, width, he...]
    ppermute x4 -> x48, starting transfers between devices: 5.45 us -> 50.8 us  [swap(): return lax.ppermute(value, axis, [(i, i ^ mask) for i in range(count)])]
    reshape x9 -> x1, local copies, waits for them, and re-layouts: 35.2 us -> 0.08 us  [dense_plan(): places = places.reshape(-1)]
    dynamic_slice x30 -> x0, local copies, waits for them, and re-layouts: 27.7 us -> none  [shards(): lax.map(attend_block, (query_tiles, grad_tiles, keys_here, values_here))]
    all_to_all x6 -> x0, starting transfers between devices: 24.9 us -> none  [the longest x1 5.17 us: shards(): lax.all_to_all(wanted.reshape(shard_total, capacity), 'ctx', split_axis=0...]
    all_to_all x6 -> x0, waiting for transfers between devices: 22.3 us -> none  [the longest x1 8.58 us: shards(): lax.all_to_all(key_rows, 'tp', split_axis=1, concat_axis=0, tiled=True)]
  transfers between devices with their start and end apart: 12 -> 48, of which waited for: 7 -> 14; matrix products, arithmetic and copies ran while one was open for 12% -> 1% of each run, Pallas kernels for 0% -> 39%
where the time goes in v1:
time: 157 us
  Pallas kernels  61.4 us (39%)
  starting transfers between devices  50.8 us (32%)
  waiting for transfers between devices  32 us (20%)
  local copies, waits for them, and re-layouts  10.8 us (7%)
    ppermute x48, starting transfers between devices, swap(): return lax.ppermute(value, axis, [(i, i ^ mask) for i in range(count)])  50.8 us
    ppermute x48, waiting for transfers between devices, swap(): return lax.ppermute(value, axis, [(i, i ^ mask) for i in range(count)])  32 us
    pallas_call x1, Pallas kernels, dense_plan(): pl.pallas_call(functools.partial(scores_kernel, pieces, tokens, width, he...  26.3 us
    pallas_call x1, Pallas kernels, dense_plan(): pl.pallas_call(functools.partial(probs_kernel, pieces, tokens, width, hea...  24 us
    pallas_call x1, Pallas kernels, dense_plan(): pl.pallas_call(functools.partial(rows_kernel, heads, group), grid=(blocks...  11.1 us
    unnamed x26, local copies, waits for them, and re-layouts  8.37 us
  transfers between devices with their start and end apart: 48, of which 14 were waited for; matrix products, arithmetic and copies ran while one was open for 1% of the time, Pallas kernels for 39%

profile of v1, /device:TPU:0, one launch (start us, length us, event | category | flops | bytes accessed | tf_op | source)
XLA Modules:
  0.0 156.5 jit_solution(17773347416672997112)
XLA Ops:
  1.7 3.1 %collective-permute-start = (bf16[160,256]{1,0:T(8,128)(2,1)S(1)}, bf16[160,256]{1,0:T(8,128)(2,1)S(1)}, u32[]{:S(2)}, u32[]{:S(2)}) collective-permute-start(bf16[160,256]{1,0:T(8,128)(2,1)S(1)} %get-tuple-element.61), channel_id=1, source_target_pairs={{0,1},{1,0},{2,3},{3,2},{4,5},{5,4},{6,7},{7,6},{8,9},{9,8},{10,11... | collective-permute-start | bytes 245768 | tf_op jit(solution)/shard_map/ppermute | solution.py:207
  4.8 2.6 %collective-permute-start.1 = (bf16[160,256]{1,0:T(8,128)(2,1)S(1)}, bf16[160,256]{1,0:T(8,128)(2,1)S(1)}, u32[]{:S(2)}, u32[]{:S(2)}) collective-permute-start(bf16[160,256]{1,0:T(8,128)(2,1)S(1)} %get-tuple-element.63), channel_id=1, source_target_pairs={{0,2},{1,3},{2,0},{3,1},{4,6},{5,7},{6,4},{7,5},{8,10},{9,11},{10,... | collective-permute-start | bytes 245768 | tf_op jit(solution)/shard_map/ppermute | solution.py:207
  9.4 3.5 %collective-permute-start.13 = (bf16[160,256]{1,0:T(8,128)(2,1)S(1)}, bf16[160,256]{1,0:T(8,128)(2,1)S(1)}, u32[]{:S(2)}, u32[]{:S(2)}) collective-permute-start(bf16[160,256]{1,0:T(8,128)(2,1)S(1)} %get-tuple-element.59), channel_id=1, source_target_pairs={{0,2},{1,3},{2,0},{3,1},{4,6},{5,7},{6,4},{7,5},{8,10},{9,11},{10,... | collective-permute-start | bytes 245768 | tf_op jit(solution)/shard_map/ppermute | solution.py:207
  12.9 1.9 %collective-permute-done.1 = bf16[160,256]{1,0:T(8,128)(2,1)S(1)} collective-permute-done((bf16[160,256]{1,0:T(8,128)(2,1)S(1)}, bf16[160,256]{1,0:T(8,128)(2,1)S(1)}, u32[]{:S(2)}, u32[]{:S(2)}) %collective-permute-start.1) | collective-permute-done | bytes 81952 | tf_op jit(solution)/shard_map/ppermute | solution.py:207
  14.8 1.6 %collective-permute-start.4 = (bf16[4,160,256]{2,1,0:T(8,128)(2,1)S(1)}, bf16[4,160,256]{2,1,0:T(8,128)(2,1)S(1)}, u32[]{:S(2)}, u32[]{:S(2)}) collective-permute-start(bf16[4,160,256]{2,1,0:T(8,128)(2,1)S(1)} %pad_maximum_fusion.refs_2_), channel_id=1, source_target_pairs={{0,16},{4,20},{8,24},{12,28},{16,0},{20,4},{24,8},{28,12},{1,17},{... | collective-permute-start | bytes 983048 | tf_op jit(solution)/shard_map/ppermute | solution.py:207
  16.4 1.5 collective-permute-start.3
  17.9 3.1 %collective-permute-done.13 = bf16[160,256]{1,0:T(8,128)(2,1)S(1)} collective-permute-done((bf16[160,256]{1,0:T(8,128)(2,1)S(1)}, bf16[160,256]{1,0:T(8,128)(2,1)S(1)}, u32[]{:S(2)}, u32[]{:S(2)}) %collective-permute-start.13) | collective-permute-done | bytes 81952 | tf_op jit(solution)/shard_map/ppermute | solution.py:207
  21.1 1.6 %collective-permute-start.16 = (bf16[4,160,256]{2,1,0:T(8,128)(2,1)S(1)}, bf16[4,160,256]{2,1,0:T(8,128)(2,1)S(1)}, u32[]{:S(2)}, u32[]{:S(2)}) collective-permute-start(bf16[4,160,256]{2,1,0:T(8,128)(2,1)S(1)} %pad_maximum_fusion.1.refs_4_), channel_id=1, source_target_pairs={{0,16},{4,20},{8,24},{12,28},{16,0},{20,4},{24,8},{28,12},{1,17},{... | collective-permute-start | bytes 983048 | tf_op jit(solution)/shard_map/ppermute | solution.py:207
  22.6 1.5 collective-permute-start.15
  25.9 4.3 %collective-permute-done.16.refs_6_ = bf16[4,160,256]{2,1,0:T(8,128)(2,1)S(1)} collective-permute-done((bf16[4,160,256]{2,1,0:T(8,128)(2,1)S(1)}, bf16[4,160,256]{2,1,0:T(8,128)(2,1)S(1)}, u32[]{:S(2)}, u32[]{:S(2)}) %collective-permute-start.16) | collective-permute-done | bytes 327712 | tf_op jit(solution)/shard_map/ppermute | solution.py:207
  30.3 1.6 %collective-permute-start.17 = (bf16[2,160,256]{2,1,0:T(8,128)(2,1)S(1)}, bf16[2,160,256]{2,1,0:T(8,128)(2,1)S(1)}, u32[]{:S(2)}, u32[]{:S(2)}) collective-permute-start(bf16[2,160,256]{2,1,0:T(8,128)(2,1)S(1)} %slice.154), channel_id=1, source_target_pairs={{0,8},{4,12},{8,0},{12,4},{16,24},{20,28},{24,16},{28,20},{1,9},{5... | collective-permute-start | bytes 491528 | tf_op jit(solution)/shard_map/ppermute | solution.py:207
  31.9 1.4 collective-permute-done.15.refs_5_
  43.4 24.0 %probs.1 = (bf16[5,2,1024,512]{3,2,1,0:T(8,128)(2,1)}, bf16[5,2,128,512]{3,2,1,0:T(8,128)(2,1)S(1)}, bf16[5,2,128,512]{3,2,1,0:T(8,128)(2,1)}, f32[5,2,8,512]{3,...) custom-call(s32[40]{0:T(128)S(1)} %reshape.22.place_ref, ...), custom_call_target="tpu_custom_call" | custom-call | flops 2684354560 | bytes 16777216 | tf_op jit(solution)/shard_map/probs/pallas_call | solution.py:497
  69.4 26.3 %scores.1 = (bf16[5,2,1024,512]{3,2,1,0:T(8,128)(2,1)}, bf16[5,1024,256]{2,1,0:T(8,128)(2,1)}, bf16[4,4,160,256]{3,2,1,0:T(8,128)(2,1)S(1)}, bf16[4,160,256]{2,1...) custom-call(s32[40]{0:T(128)S(1)} %reshape.22.place_ref, s32[1]{0:T(128)} %bitcast.tp_ref, ...), custom_call_target="tpu_custom_call" | custom-call | flops 2684354560 | bytes 16777216 | tf_op jit(solution)/shard_map/scores/pallas_call | solution.py:522
  96.3 1.7 %copy-done.1 = bf16[5,1024,256]{2,1,0:T(8,128)(2,1)S(1)} copy-done((bf16[5,1024,256]{2,1,0:T(8,128)(2,1)S(1)}, bf16[5,1024,256]{2,1,0:T(8,128)(2,1)}, u32[]{:S(2)}) %copy-start.1) | copy-done | bytes 2621464
  98.0 11.1 %rows.1 = (bf16[640,1024]{1,0:T(8,128)(2,1)}, bf16[640,1024]{1,0:T(8,128)(2,1)}) custom-call(bf16[5,2,1024,512]{3,2,1,0:T(8,128)(2,1)} %get-tuple-element.21.refs_0_.exp_ref, bf16[5,2,1024,512]{3,2,1,0:T(8,128)(2,1)} %get-tuple-element.25.ds_ref, f32[5,2,8,512]{3,2,1,0:T(8,128)S(1)} %get-tuple-element.24.refs_3_.inv_ref, bf16[5,1024,256]{2,1,0:T(8,128)(2,1)S(1)} %copy-done, ...), custom_call_target="tpu_custom_call" | custom-call | flops 2684354560 | bytes 16777216 | tf_op jit(solution)/shard_map/rows/pallas_call | solution.py:540
  109.2 1.5 collective-permute-start.40
  111.3 4.1 %collective-permute-done.40 = bf16[2,160,256]{2,1,0:T(8,128)(2,1)S(1)} collective-permute-done((bf16[2,160,256]{2,1,0:T(8,128)(2,1)S(1)}, bf16[2,160,256]{2,1,0:T(8,128)(2,1)S(1)}, u32[]{:S(2)}, u32[]{:S(2)}) %collective-permute-start.40) | collective-permute-done | bytes 163872 | tf_op jit(solution)/shard_map/ppermute | solution.py:207
  115.4 1.5 collective-permute-start.28
  117.5 1.6 %collective-permute-start.41 = (bf16[2,160,256]{2,1,0:T(8,128)(2,1)S(1)}, bf16[2,160,256]{2,1,0:T(8,128)(2,1)S(1)}, u32[]{:S(2)}, u32[]{:S(2)}) collective-permute-start(bf16[2,160,256]{2,1,0:T(8,128)(2,1)S(1)} %get-tuple-element.38), channel_id=1, source_target_pairs={{0,16},{4,20},{8,24},{12,28},{16,0},{20,4},{24,8},{28,12},{1,17},{... | collective-permute-start | bytes 491528 | tf_op jit(solution)/shard_map/ppermute | solution.py:207
  119.1 1.6 %collective-permute-done.28 = bf16[2,160,256]{2,1,0:T(8,128)(2,1)S(1)} collective-permute-done((bf16[2,160,256]{2,1,0:T(8,128)(2,1)S(1)}, bf16[2,160,256]{2,1,0:T(8,128)(2,1)S(1)}, u32[]{:S(2)}, u32[]{:S(2)}) %collective-permute-start.28) | collective-permute-done | bytes 163872 | tf_op jit(solution)/shard_map/ppermute | solution.py:207
  120.8 1.5 collective-permute-start.38
  122.3 1.8 %collective-permute-done.31 = bf16[2,160,256]{2,1,0:T(8,128)(2,1)S(1)} collective-permute-done((bf16[2,160,256]{2,1,0:T(8,128)(2,1)S(1)}, bf16[2,160,256]{2,1,0:T(8,128)(2,1)S(1)}, u32[]{:S(2)}, u32[]{:S(2)}) %collective-permute-start.31) | collective-permute-done | bytes 163872 | tf_op jit(solution)/shard_map/ppermute | solution.py:207
  125.5 1.7 %collective-permute-done.41 = bf16[2,160,256]{2,1,0:T(8,128)(2,1)S(1)} collective-permute-done((bf16[2,160,256]{2,1,0:T(8,128)(2,1)S(1)}, bf16[2,160,256]{2,1,0:T(8,128)(2,1)S(1)}, u32[]{:S(2)}, u32[]{:S(2)}) %collective-permute-start.41) | collective-permute-done | bytes 163872 | tf_op jit(solution)/shard_map/ppermute | solution.py:207
  127.8 1.6 collective-permute-done.44
  130.0 2.5 %collective-permute-start.32 = (bf16[2,160,256]{2,1,0:T(8,128)(2,1)S(1)}, bf16[2,160,256]{2,1,0:T(8,128)(2,1)S(1)}, u32[]{:S(2)}, u32[]{:S(2)}) collective-permute-start(bf16[2,160,256]{2,1,0:T(8,128)(2,1)S(1)} %get-tuple-element.43), channel_id=1, source_target_pairs={{0,8},{4,12},{8,0},{12,4},{16,24},{20,28},{24,16},{28,20},{1,9},{5... | collective-permute-start | bytes 491528 | tf_op jit(solution)/shard_map/ppermute | solution.py:207
  132.7 1.6 %collective-permute-done.29 = bf16[2,160,256]{2,1,0:T(8,128)(2,1)S(1)} collective-permute-done((bf16[2,160,256]{2,1,0:T(8,128)(2,1)S(1)}, bf16[2,160,256]{2,1,0:T(8,128)(2,1)S(1)}, u32[]{:S(2)}, u32[]{:S(2)}) %collective-permute-start.29) | collective-permute-done | bytes 163872 | tf_op jit(solution)/shard_map/ppermute | solution.py:207
  134.3 5.7 %collective-permute-start.45 = (bf16[160,256]{1,0:T(8,128)(2,1)S(1)}, bf16[160,256]{1,0:T(8,128)(2,1)S(1)}, u32[]{:S(2)}, u32[]{:S(2)}) collective-permute-start(bf16[160,256]{1,0:T(8,128)(2,1)S(1)} %get-tuple-element.52), channel_id=1, source_target_pairs={{0,1},{1,0},{2,3},{3,2},{4,5},{5,4},{6,7},{7,6},{8,9},{9,8},{10,11... | collective-permute-start | bytes 245768 | tf_op jit(solution)/shard_map/ppermute | solution.py:207
  140.0 2.9 %collective-permute-start.46 = (bf16[160,256]{1,0:T(8,128)(2,1)S(1)}, bf16[160,256]{1,0:T(8,128)(2,1)S(1)}, u32[]{:S(2)}, u32[]{:S(2)}) collective-permute-start(bf16[160,256]{1,0:T(8,128)(2,1)S(1)} %get-tuple-element.51), channel_id=1, source_target_pairs={{0,2},{1,3},{2,0},{3,1},{4,6},{5,7},{6,4},{7,5},{8,10},{9,11},{10,... | collective-permute-start | bytes 245768 | tf_op jit(solution)/shard_map/ppermute | solution.py:207
  145.5 2.3 %collective-permute-start.34 = (bf16[160,256]{1,0:T(8,128)(2,1)S(1)}, bf16[160,256]{1,0:T(8,128)(2,1)S(1)}, u32[]{:S(2)}, u32[]{:S(2)}) collective-permute-start(bf16[160,256]{1,0:T(8,128)(2,1)S(1)} %get-tuple-element.54), channel_id=1, source_target_pairs={{0,2},{1,3},{2,0},{3,1},{4,6},{5,7},{6,4},{7,5},{8,10},{9,11},{10,... | collective-permute-start | bytes 245768 | tf_op jit(solution)/shard_map/ppermute | solution.py:207
  148.8 2.0 %collective-permute-done.46 = bf16[160,256]{1,0:T(8,128)(2,1)S(1)} collective-permute-done((bf16[160,256]{1,0:T(8,128)(2,1)S(1)}, bf16[160,256]{1,0:T(8,128)(2,1)S(1)}, u32[]{:S(2)}, u32[]{:S(2)}) %collective-permute-start.46) | collective-permute-done | bytes 81952 | tf_op jit(solution)/shard_map/ppermute | solution.py:207
  150.9 4.9 %collective-permute-done.34 = bf16[160,256]{1,0:T(8,128)(2,1)S(1)} collective-permute-done((bf16[160,256]{1,0:T(8,128)(2,1)S(1)}, bf16[160,256]{1,0:T(8,128)(2,1)S(1)}, u32[]{:S(2)}, u32[]{:S(2)}) %collective-permute-start.34) | collective-permute-done | bytes 81952 | tf_op jit(solution)/shard_map/ppermute | solution.py:207
  (127 shorter events, 26.0 us)
Async XLA Ops:
  1.7 11.2 %collective-permute-start = (bf16[160,256]{1,0:T(8,128)(2,1)S(1)}, bf16[160,256]{1,0:T(8,128)(2,1)S(1)}, u32[]{:S(2)}, u32[]{:S(2)}) collective-permute-start(bf16[160,256]{1,0:T(8,128)(2,1)S(1)} %get-tuple-element.61), channel_id=1, source_target_pairs={{0,1},{1,0},{2,3},{3,2},{4,5},{5,4},{6,7},{7,6},{8,9},{9,8},{10,11... | collective-permute-start | bytes 245768 | tf_op jit(solution)/shard_map/ppermute | solution.py:207
  4.8 10.0 %collective-permute-start.1 = (bf16[160,256]{1,0:T(8,128)(2,1)S(1)}, bf16[160,256]{1,0:T(8,128)(2,1)S(1)}, u32[]{:S(2)}, u32[]{:S(2)}) collective-permute-start(bf16[160,256]{1,0:T(8,128)(2,1)S(1)} %get-tuple-element.63), channel_id=1, source_target_pairs={{0,2},{1,3},{2,0},{3,1},{4,6},{5,7},{6,4},{7,5},{8,10},{9,11},{10,... | collective-permute-start | bytes 245768 | tf_op jit(solution)/shard_map/ppermute | solution.py:207
  8.4 9.5 %collective-permute-start.12 = (bf16[160,256]{1,0:T(8,128)(2,1)S(1)}, bf16[160,256]{1,0:T(8,128)(2,1)S(1)}, u32[]{:S(2)}, u32[]{:S(2)}) collective-permute-start(bf16[160,256]{1,0:T(8,128)(2,1)S(1)} %get-tuple-element.57), channel_id=1, source_target_pairs={{0,1},{1,0},{2,3},{3,2},{4,5},{5,4},{6,7},{7,6},{8,9},{9,8},{10,11... | collective-permute-start | bytes 245768 | tf_op jit(solution)/shard_map/ppermute | solution.py:207
  9.4 11.6 %collective-permute-start.13 = (bf16[160,256]{1,0:T(8,128)(2,1)S(1)}, bf16[160,256]{1,0:T(8,128)(2,1)S(1)}, u32[]{:S(2)}, u32[]{:S(2)}) collective-permute-start(bf16[160,256]{1,0:T(8,128)(2,1)S(1)} %get-tuple-element.59), channel_id=1, source_target_pairs={{0,2},{1,3},{2,0},{3,1},{4,6},{5,7},{6,4},{7,5},{8,10},{9,11},{10,... | collective-permute-start | bytes 245768 | tf_op jit(solution)/shard_map/ppermute | solution.py:207
  12.9 8.1 %collective-permute-start.14 = (bf16[160,256]{1,0:T(8,128)(2,1)S(1)}, bf16[160,256]{1,0:T(8,128)(2,1)S(1)}, u32[]{:S(2)}, u32[]{:S(2)}) collective-permute-start(bf16[160,256]{1,0:T(8,128)(2,1)S(1)} %get-tuple-element.58), channel_id=1, source_target_pairs={{0,3},{1,2},{2,1},{3,0},{4,7},{5,6},{6,5},{7,4},{8,11},{9,10},{10,... | collective-permute-start | bytes 245768 | tf_op jit(solution)/shard_map/ppermute | solution.py:207
  14.8 9.3 %collective-permute-start.4 = (bf16[4,160,256]{2,1,0:T(8,128)(2,1)S(1)}, bf16[4,160,256]{2,1,0:T(8,128)(2,1)S(1)}, u32[]{:S(2)}, u32[]{:S(2)}) collective-permute-start(bf16[4,160,256]{2,1,0:T(8,128)(2,1)S(1)} %pad_maximum_fusion.refs_2_), channel_id=1, source_target_pairs={{0,16},{4,20},{8,24},{12,28},{16,0},{20,4},{24,8},{28,12},{1,17},{... | collective-permute-start | bytes 983048 | tf_op jit(solution)/shard_map/ppermute | solution.py:207
  16.4 8.3 %collective-permute-start.3 = (bf16[4,160,256]{2,1,0:T(8,128)(2,1)S(1)}, bf16[4,160,256]{2,1,0:T(8,128)(2,1)S(1)}, u32[]{:S(2)}, u32[]{:S(2)}) collective-permute-start(bf16[4,160,256]{2,1,0:T(8,128)(2,1)S(1)} %pad_maximum_fusion.refs_2_), channel_id=1, source_target_pairs={{0,8},{4,12},{8,0},{12,4},{16,24},{20,28},{24,16},{28,20},{1,9},{5... | collective-permute-start | bytes 983048 | tf_op jit(solution)/shard_map/ppermute | solution.py:207
  21.1 9.2 %collective-permute-start.16 = (bf16[4,160,256]{2,1,0:T(8,128)(2,1)S(1)}, bf16[4,160,256]{2,1,0:T(8,128)(2,1)S(1)}, u32[]{:S(2)}, u32[]{:S(2)}) collective-permute-start(bf16[4,160,256]{2,1,0:T(8,128)(2,1)S(1)} %pad_maximum_fusion.1.refs_4_), channel_id=1, source_target_pairs={{0,16},{4,20},{8,24},{12,28},{16,0},{20,4},{24,8},{28,12},{1,17},{... | collective-permute-start | bytes 983048 | tf_op jit(solution)/shard_map/ppermute | solution.py:207
  22.6 10.6 %collective-permute-start.15 = (bf16[4,160,256]{2,1,0:T(8,128)(2,1)S(1)}, bf16[4,160,256]{2,1,0:T(8,128)(2,1)S(1)}, u32[]{:S(2)}, u32[]{:S(2)}) collective-permute-start(bf16[4,160,256]{2,1,0:T(8,128)(2,1)S(1)} %pad_maximum_fusion.1.refs_4_), channel_id=1, source_target_pairs={{0,8},{4,12},{8,0},{12,4},{16,24},{20,28},{24,16},{28,20},{1,9},{5... | collective-permute-start | bytes 983048 | tf_op jit(solution)/shard_map/ppermute | solution.py:207
  24.1 12.8 %collective-permute-start.7 = (bf16[4,160,256]{2,1,0:T(8,128)(2,1)S(1)}, bf16[4,160,256]{2,1,0:T(8,128)(2,1)S(1)}, u32[]{:S(2)}, u32[]{:S(2)}) collective-permute-start(bf16[4,160,256]{2,1,0:T(8,128)(2,1)S(1)} %pad_maximum_fusion.refs_2_), channel_id=1, source_target_pairs={{0,4},{4,0},{8,12},{12,8},{16,20},{20,16},{24,28},{28,24},{1,5},{5... | collective-permute-start | bytes 983048 | tf_op jit(solution)/shard_map/ppermute | solution.py:207
  24.2 11.6 %collective-permute-start.5 = (bf16[2,160,256]{2,1,0:T(8,128)(2,1)S(1)}, bf16[2,160,256]{2,1,0:T(8,128)(2,1)S(1)}, u32[]{:S(2)}, u32[]{:S(2)}) collective-permute-start(bf16[2,160,256]{2,1,0:T(8,128)(2,1)S(1)} %slice.152), channel_id=1, source_target_pairs={{0,8},{4,12},{8,0},{12,4},{16,24},{20,28},{24,16},{28,20},{1,9},{5... | collective-permute-start | bytes 491528 | tf_op jit(solution)/shard_map/ppermute | solution.py:207
  24.8 11.0 %collective-permute-start.6 = (bf16[2,160,256]{2,1,0:T(8,128)(2,1)S(1)}, bf16[2,160,256]{2,1,0:T(8,128)(2,1)S(1)}, u32[]{:S(2)}, u32[]{:S(2)}) collective-permute-start(bf16[2,160,256]{2,1,0:T(8,128)(2,1)S(1)} %slice.153), channel_id=1, source_target_pairs={{0,16},{4,20},{8,24},{12,28},{16,0},{20,4},{24,8},{28,12},{1,17},{... | collective-permute-start | bytes 491528 | tf_op jit(solution)/shard_map/ppermute | solution.py:207
  38.7 29.7 %collective-permute-start.19 = (bf16[4,160,256]{2,1,0:T(8,128)(2,1)S(1)}, bf16[4,160,256]{2,1,0:T(8,128)(2,1)S(1)}, u32[]{:S(2)}, u32[]{:S(2)}) collective-permute-start(bf16[4,160,256]{2,1,0:T(8,128)(2,1)S(1)} %pad_maximum_fusion.1.refs_4_), channel_id=1, source_target_pairs={{0,4},{4,0},{8,12},{12,8},{16,20},{20,16},{24,28},{28,24},{1,5},{5... | collective-permute-start | bytes 983048 | tf_op jit(solution)/shard_map/ppermute | solution.py:207
  39.4 30.0 %collective-permute-start.20 = (bf16[4,160,256]{2,1,0:T(8,128)(2,1)S(1)}, bf16[4,160,256]{2,1,0:T(8,128)(2,1)S(1)}, u32[]{:S(2)}, u32[]{:S(2)}) collective-permute-start(bf16[4,160,256]{2,1,0:T(8,128)(2,1)S(1)} %collective-permute-done.15.refs_5_), channel_id=1, source_target_pairs={{0,4},{4,0},{8,12},{12,8},{16,20},{20,16},{24,28},{28,24},{1,5},{5... | collective-permute-start | bytes 983048 | tf_op jit(solution)/shard_map/ppermute | solution.py:207
  39.9 29.5 %collective-permute-start.21 = (bf16[4,160,256]{2,1,0:T(8,128)(2,1)S(1)}, bf16[4,160,256]{2,1,0:T(8,128)(2,1)S(1)}, u32[]{:S(2)}, u32[]{:S(2)}) collective-permute-start(bf16[4,160,256]{2,1,0:T(8,128)(2,1)S(1)} %collective-permute-done.16.refs_6_), channel_id=1, source_target_pairs={{0,4},{4,0},{8,12},{12,8},{16,20},{20,16},{24,28},{28,24},{1,5},{5... | collective-permute-start | bytes 983048 | tf_op jit(solution)/shard_map/ppermute | solution.py:207
  40.0 28.9 %collective-permute-start.22 = (bf16[2,160,256]{2,1,0:T(8,128)(2,1)S(1)}, bf16[2,160,256]{2,1,0:T(8,128)(2,1)S(1)}, u32[]{:S(2)}, u32[]{:S(2)}) collective-permute-start(bf16[2,160,256]{2,1,0:T(8,128)(2,1)S(1)} %collective-permute-done.17.refs_7_), channel_id=1, source_target_pairs={{0,4},{4,0},{8,12},{12,8},{16,20},{20,16},{24,28},{28,24},{1,5},{5... | collective-permute-start | bytes 491528 | tf_op jit(solution)/shard_map/ppermute | solution.py:207
  40.5 28.4 %collective-permute-start.23 = (bf16[2,160,256]{2,1,0:T(8,128)(2,1)S(1)}, bf16[2,160,256]{2,1,0:T(8,128)(2,1)S(1)}, u32[]{:S(2)}, u32[]{:S(2)}) collective-permute-start(bf16[2,160,256]{2,1,0:T(8,128)(2,1)S(1)} %collective-permute-done.18.refs_8_), channel_id=1, source_target_pairs={{0,4},{4,0},{8,12},{12,8},{16,20},{20,16},{24,28},{28,24},{1,5},{5... | collective-permute-start | bytes 491528 | tf_op jit(solution)/shard_map/ppermute | solution.py:207
  68.4 40.7 %collective-permute-start.39 = (bf16[4,160,256]{2,1,0:T(8,128)(2,1)S(1)}, bf16[4,160,256]{2,1,0:T(8,128)(2,1)S(1)}, u32[]{:S(2)}, u32[]{:S(2)}) collective-permute-start(bf16[4,160,256]{2,1,0:T(8,128)(2,1)S(1)} %get-tuple-element.37), channel_id=1, source_target_pairs={{0,4},{4,0},{8,12},{12,8},{16,20},{20,16},{24,28},{28,24},{1,5},{5... | collective-permute-start | bytes 983048 | tf_op jit(solution)/shard_map/ppermute | solution.py:207
  68.9 48.6 %collective-permute-start.37 = (bf16[2,4,160,256]{3,2,1,0:T(8,128)(2,1)S(1)}, bf16[2,4,160,256]{3,2,1,0:T(8,128)(2,1)S(1)}, u32[]{:S(2)}, u32[]{:S(2)}) collective-permute-start(bf16[2,4,160,256]{3,2,1,0:T(8,128)(2,1)S(1)} %get-tuple-element.36), channel_id=1, source_target_pairs={{0,4},{4,0},{8,12},{12,8},{16,20},{20,16},{24,28},{28,24},{1,5},{5... | collective-permute-start | bytes 1966088 | tf_op jit(solution)/shard_map/ppermute | solution.py:207
  68.9 63.6 %collective-permute-start.36 = (bf16[4,160,256]{2,1,0:T(8,128)(2,1)S(1)}, bf16[4,160,256]{2,1,0:T(8,128)(2,1)S(1)}, u32[]{:S(2)}, u32[]{:S(2)}) collective-permute-start(bf16[4,160,256]{2,1,0:T(8,128)(2,1)S(1)} %get-tuple-element.35), channel_id=1, source_target_pairs={{0,4},{4,0},{8,12},{12,8},{16,20},{20,16},{24,28},{28,24},{1,5},{5... | collective-permute-start | bytes 983048 | tf_op jit(solution)/shard_map/ppermute | solution.py:207
  95.7 15.0 %collective-permute-start.27 = (bf16[4,160,256]{2,1,0:T(8,128)(2,1)S(1)}, bf16[4,160,256]{2,1,0:T(8,128)(2,1)S(1)}, u32[]{:S(2)}, u32[]{:S(2)}) collective-permute-start(bf16[4,160,256]{2,1,0:T(8,128)(2,1)S(1)} %get-tuple-element.33), channel_id=1, source_target_pairs={{0,4},{4,0},{8,12},{12,8},{16,20},{20,16},{24,28},{28,24},{1,5},{5... | collective-permute-start | bytes 983048 | tf_op jit(solution)/shard_map/ppermute | solution.py:207
  95.9 28.4 %collective-permute-start.25 = (bf16[2,4,160,256]{3,2,1,0:T(8,128)(2,1)S(1)}, bf16[2,4,160,256]{3,2,1,0:T(8,128)(2,1)S(1)}, u32[]{:S(2)}, u32[]{:S(2)}) collective-permute-start(bf16[2,4,160,256]{3,2,1,0:T(8,128)(2,1)S(1)} %get-tuple-element.32), channel_id=1, source_target_pairs={{0,4},{4,0},{8,12},{12,8},{16,20},{20,16},{24,28},{28,24},{1,5},{5... | collective-permute-start | bytes 1966088 | tf_op jit(solution)/shard_map/ppermute | solution.py:207
  117.5 9.8 %collective-permute-start.41 = (bf16[2,160,256]{2,1,0:T(8,128)(2,1)S(1)}, bf16[2,160,256]{2,1,0:T(8,128)(2,1)S(1)}, u32[]{:S(2)}, u32[]{:S(2)}) collective-permute-start(bf16[2,160,256]{2,1,0:T(8,128)(2,1)S(1)} %get-tuple-element.38), channel_id=1, source_target_pairs={{0,16},{4,20},{8,24},{12,28},{16,0},{20,4},{24,8},{28,12},{1,17},{... | collective-permute-start | bytes 491528 | tf_op jit(solution)/shard_map/ppermute | solution.py:207
  127.3 16.8 %collective-permute-start.24 = (bf16[4,160,256]{2,1,0:T(8,128)(2,1)S(1)}, bf16[4,160,256]{2,1,0:T(8,128)(2,1)S(1)}, u32[]{:S(2)}, u32[]{:S(2)}) collective-permute-start(bf16[4,160,256]{2,1,0:T(8,128)(2,1)S(1)} %get-tuple-element.31), channel_id=1, source_target_pairs={{0,4},{4,0},{8,12},{12,8},{16,20},{20,16},{24,28},{28,24},{1,5},{5... | collective-permute-start | bytes 983048 | tf_op jit(solution)/shard_map/ppermute | solution.py:207
  129.4 10.6 %collective-permute-start.26 = (bf16[2,160,256]{2,1,0:T(8,128)(2,1)S(1)}, bf16[2,160,256]{2,1,0:T(8,128)(2,1)S(1)}, u32[]{:S(2)}, u32[]{:S(2)}) collective-permute-start(bf16[2,160,256]{2,1,0:T(8,128)(2,1)S(1)} %get-tuple-element.44), channel_id=1, source_target_pairs={{0,8},{4,12},{8,0},{12,4},{16,24},{20,28},{24,16},{28,20},{1,9},{5... | collective-permute-start | bytes 491528 | tf_op jit(solution)/shard_map/ppermute | solution.py:207
  130.0 13.0 %collective-permute-start.32 = (bf16[2,160,256]{2,1,0:T(8,128)(2,1)S(1)}, bf16[2,160,256]{2,1,0:T(8,128)(2,1)S(1)}, u32[]{:S(2)}, u32[]{:S(2)}) collective-permute-start(bf16[2,160,256]{2,1,0:T(8,128)(2,1)S(1)} %get-tuple-element.43), channel_id=1, source_target_pairs={{0,8},{4,12},{8,0},{12,4},{16,24},{20,28},{24,16},{28,20},{1,9},{5... | collective-permute-start | bytes 491528 | tf_op jit(solution)/shard_map/ppermute | solution.py:207
  132.5 11.5 %collective-permute-start.30 = (bf16[2,160,256]{2,1,0:T(8,128)(2,1)S(1)}, bf16[2,160,256]{2,1,0:T(8,128)(2,1)S(1)}, u32[]{:S(2)}, u32[]{:S(2)}) collective-permute-start(bf16[2,160,256]{2,1,0:T(8,128)(2,1)S(1)} %get-tuple-element.45), channel_id=1, source_target_pairs={{0,16},{4,20},{8,24},{12,28},{16,0},{20,4},{24,8},{28,12},{1,17},{... | collective-permute-start | bytes 491528 | tf_op jit(solution)/shard_map/ppermute | solution.py:207
  134.3 13.5 %collective-permute-start.45 = (bf16[160,256]{1,0:T(8,128)(2,1)S(1)}, bf16[160,256]{1,0:T(8,128)(2,1)S(1)}, u32[]{:S(2)}, u32[]{:S(2)}) collective-permute-start(bf16[160,256]{1,0:T(8,128)(2,1)S(1)} %get-tuple-element.52), channel_id=1, source_target_pairs={{0,1},{1,0},{2,3},{3,2},{4,5},{5,4},{6,7},{7,6},{8,9},{9,8},{10,11... | collective-permute-start | bytes 245768 | tf_op jit(solution)/shard_map/ppermute | solution.py:207
  140.0 10.8 %collective-permute-start.46 = (bf16[160,256]{1,0:T(8,128)(2,1)S(1)}, bf16[160,256]{1,0:T(8,128)(2,1)S(1)}, u32[]{:S(2)}, u32[]{:S(2)}) collective-permute-start(bf16[160,256]{1,0:T(8,128)(2,1)S(1)} %get-tuple-element.51), channel_id=1, source_target_pairs={{0,2},{1,3},{2,0},{3,1},{4,6},{5,7},{6,4},{7,5},{8,10},{9,11},{10,... | collective-permute-start | bytes 245768 | tf_op jit(solution)/shard_map/ppermute | solution.py:207
  142.9 7.9 %collective-permute-start.47 = (bf16[160,256]{1,0:T(8,128)(2,1)S(1)}, bf16[160,256]{1,0:T(8,128)(2,1)S(1)}, u32[]{:S(2)}, u32[]{:S(2)}) collective-permute-start(bf16[160,256]{1,0:T(8,128)(2,1)S(1)} %get-tuple-element.50), channel_id=1, source_target_pairs={{0,3},{1,2},{2,1},{3,0},{4,7},{5,6},{6,5},{7,4},{8,11},{9,10},{10,... | collective-permute-start | bytes 245768 | tf_op jit(solution)/shard_map/ppermute | solution.py:207
  145.5 10.2 %collective-permute-start.34 = (bf16[160,256]{1,0:T(8,128)(2,1)S(1)}, bf16[160,256]{1,0:T(8,128)(2,1)S(1)}, u32[]{:S(2)}, u32[]{:S(2)}) collective-permute-start(bf16[160,256]{1,0:T(8,128)(2,1)S(1)} %get-tuple-element.54), channel_id=1, source_target_pairs={{0,2},{1,3},{2,0},{3,1},{4,6},{5,7},{6,4},{7,5},{8,10},{9,11},{10,... | collective-permute-start | bytes 245768 | tf_op jit(solution)/shard_map/ppermute | solution.py:207
  147.8 8.0 %collective-permute-start.35 = (bf16[160,256]{1,0:T(8,128)(2,1)S(1)}, bf16[160,256]{1,0:T(8,128)(2,1)S(1)}, u32[]{:S(2)}, u32[]{:S(2)}) collective-permute-start(bf16[160,256]{1,0:T(8,128)(2,1)S(1)} %get-tuple-element.53), channel_id=1, source_target_pairs={{0,3},{1,2},{2,1},{3,0},{4,7},{5,6},{6,5},{7,4},{8,11},{9,10},{10,... | collective-permute-start | bytes 245768 | tf_op jit(solution)/shard_map/ppermute | solution.py:207
  (29 other events, 164.9 us)

commit v2 on v0

--- a/solution.py
+++ b/solution.py
@@ -1,6 +1,10 @@
+import functools
+
 import jax
 import jax.numpy as jnp
 from jax import lax
+from jax.experimental import pallas as pl
+from jax.experimental.pallas import tpu as pltpu
 from jax.sharding import PartitionSpec as P
 
 HD = 128
@@ -71,7 +75,7 @@
     return (attended, query_grad, key_part, value_part)
 
 
-def shards(queries, key_rows, value_rows, out_grad, block_list):
+def sparse_plan(queries, key_rows, value_rows, out_grad, block_list):
     tokens_here = queries.shape[0]
     block_count = tokens_here // BLK
     shard_total = lax.axis_size("ctx")
@@ -192,7 +196,337 @@
     )
 
 
+LOG2E = 1.4426950408889634
+DENSE_SHARDS = 8
+NT = (((1,), (1,)), ((), ()))
+TN = (((0,), (0,)), ((), ()))
+
+
+def swap(value, axis, mask):
+    count = lax.axis_size(axis)
+    return lax.ppermute(value, axis, [(i, i ^ mask) for i in range(count)])
+
+
+def rows_of(quarter, shard, spot, tokens, me_tp):
+    return pl.ds(pl.multiple_of(shard * tokens + (spot ^ me_tp) * quarter, 16), quarter)
+
+
+def place_pieces(piece_refs, pieces, tokens, me_tp, buffer):
+    for ref, (shard, first, count) in zip(piece_refs, pieces):
+        for at in range(count):
+            buffer[rows_of(ref.shape[1], shard, first + at, tokens, me_tp)] = ref[at]
+
+
+def write_sums(acc, out_refs, tokens, me_tp, scale):
+    near_ref, far3_ref, far12_ref, far0_ref = out_refs
+    targets = [(far3_ref, 7), (far12_ref.at[0], 3), (far12_ref.at[1], 5), (far0_ref, 1)]
+    targets += [(near_ref.at[k], 2 * k) for k in (3, 1, 2, 0)]
+    for ref, shard in targets:
+        for spot in range(ref.shape[0]):
+            part = acc[rows_of(ref.shape[1], shard, spot, tokens, me_tp)]
+            if scale is not None:
+                part = part * scale
+            ref[spot] = part.astype(ref.dtype)
+
+
+def block_of(place_ref, entry):
+    return pl.ds(pl.multiple_of(place_ref[entry] * BLK, BLK), BLK)
+
+
+def fold(value, op):
+    rows, width = value.shape
+    return op(value.reshape(rows // 8, 8, width), axis=0)
+
+
+def joined(op, total, value):
+    return value if total is None else op(total, value)
+
+
+class Units:
+    def __init__(self, blocks, width, heads, group):
+        self.blocks, self.width, self.heads, self.group = blocks, width, heads, group
+        self.count = blocks * heads
+
+    def rows(self, unit):
+        row = unit // self.heads
+        return slice(row * BLK, (row + 1) * BLK)
+
+    def lanes(self, unit):
+        head = unit % self.heads
+        return slice(head * HD, (head + 1) * HD)
+
+    def parts(self, unit):
+        first = (unit % self.heads) * self.group
+        return [slice((first + g) * HD, (first + g + 1) * HD) for g in range(self.group)]
+
+    def chunks(self):
+        return [(c, slice(c * BLK, (c + 1) * BLK)) for c in range(self.width)]
+
+    def entry(self, unit, column):
+        return (unit // self.heads) * self.width + column
+
+    def stacked(self, ref, unit):
+        return jnp.concatenate([ref[self.rows(unit), part] for part in self.parts(unit)], axis=0)
+
+    def flipped(self, ref, unit):
+        return jnp.concatenate([ref[self.rows(unit), part].T for part in self.parts(unit)], axis=1)
+
+
+def probs_kernel(pieces, units, tokens, place_ref, tp_ref, query_ref, grad_ref, *refs):
+    count = len(pieces)
+    piece_refs = refs[:count]
+    exp_ref, grad_t_ref, inv_ref, buffer = refs[count : count + 4]
+    out_refs = refs[count + 4 : count + 8]
+    acc, score_ref = refs[count + 8 :]
+    me_tp = tp_ref[0]
+    acc[...] = jnp.zeros_like(acc)
+    place_pieces(piece_refs, pieces, tokens, me_tp, buffer)
+    factor = LOG2E * float(HD) ** (-0.5)
+    tops, totals = {}, {}
+    for step in range(units.count + 2):
+        first, second, third = step, step - 1, step - 2
+        top_new = total_new = None
+        if first < units.count:
+            query = units.stacked(query_ref, first)
+        if 0 <= second < units.count:
+            top = jnp.max(tops[second], axis=0, keepdims=True) * factor
+        if 0 <= third:
+            inverse = 1.0 / jnp.sum(totals[third], axis=0, keepdims=True)
+            inv_ref[third] = jnp.broadcast_to(inverse, inv_ref.shape[1:])
+            grad_low = (units.flipped(grad_ref, third).astype(jnp.float32) * inverse).astype(
+                jnp.bfloat16
+            )
+            grad_t_ref[third] = grad_low
+        for column, chunk in units.chunks():
+            if first < units.count:
+                keys = buffer[block_of(place_ref, units.entry(first, column)), units.lanes(first)]
+                score = lax.dot_general(keys, query, NT, preferred_element_type=jnp.float32)
+                score_ref[first % 2, chunk] = score
+                top_new = joined(jnp.maximum, top_new, fold(score, jnp.max))
+            if 0 <= second < units.count:
+                weight = jnp.exp2(score_ref[second % 2, chunk] * factor - top)
+                exp_ref[second, chunk] = weight.astype(jnp.bfloat16)
+                total_new = joined(jnp.add, total_new, fold(weight, jnp.sum))
+            if 0 <= third:
+                acc[block_of(place_ref, units.entry(third, column)), units.lanes(third)] += (
+                    lax.dot_general(
+                        exp_ref[third, chunk], grad_low, NT, preferred_element_type=jnp.float32
+                    )
+                )
+        tops[first], totals[second] = top_new, total_new
+    write_sums(acc, out_refs, tokens, me_tp, None)
+
+
+def scores_kernel(pieces, units, tokens, place_ref, tp_ref, query_ref, exp_ref, grad_t_ref, inv_ref, *refs):
+    count = len(pieces)
+    piece_refs = refs[:count]
+    ds_ref, buffer = refs[count : count + 2]
+    out_refs = refs[count + 2 : count + 6]
+    acc, dprob_ref = refs[count + 6 :]
+    me_tp = tp_ref[0]
+    acc[...] = jnp.zeros_like(acc)
+    place_pieces(piece_refs, pieces, tokens, me_tp, buffer)
+    deltas = {}
+    for step in range(units.count + 2):
+        first, second, third = step, step - 1, step - 2
+        delta_new = None
+        if 0 <= second < units.count:
+            delta = jnp.sum(deltas[second], axis=0, keepdims=True) * inv_ref[second, 0:1]
+        if 0 <= third:
+            query = units.stacked(query_ref, third)
+        for column, chunk in units.chunks():
+            if first < units.count:
+                values = buffer[block_of(place_ref, units.entry(first, column)), units.lanes(first)]
+                dprob = jnp.dot(values, grad_t_ref[first], preferred_element_type=jnp.float32)
+                dprob_ref[first % 2, chunk] = dprob
+                weight = exp_ref[first, chunk].astype(jnp.float32)
+                delta_new = joined(jnp.add, delta_new, fold(weight * dprob, jnp.sum))
+            if 0 <= second < units.count:
+                weight = exp_ref[second, chunk].astype(jnp.float32)
+                ds_ref[second, chunk] = (weight * (dprob_ref[second % 2, chunk] - delta)).astype(
+                    jnp.bfloat16
+                )
+            if 0 <= third:
+                acc[block_of(place_ref, units.entry(third, column)), units.lanes(third)] += jnp.dot(
+                    ds_ref[third, chunk], query, preferred_element_type=jnp.float32
+                )
+        deltas[first] = delta_new
+    write_sums(acc, out_refs, tokens, me_tp, float(HD) ** (-0.5))
+
+
+def rows_kernel(units, place_ref, exp_ref, ds_ref, inv_ref, keys_ref, values_ref, out_ref, dq_ref, listed):
+    scale = float(HD) ** (-0.5)
+    for unit in range(units.count):
+        slot = unit % 2
+        for column, chunk in units.chunks():
+            block = block_of(place_ref, units.entry(unit, column))
+            listed[2 * slot, chunk] = values_ref[block, units.lanes(unit)]
+            listed[2 * slot + 1, chunk] = keys_ref[block, units.lanes(unit)]
+        attended = lax.dot_general(
+            listed[2 * slot], exp_ref[unit], TN, preferred_element_type=jnp.float32
+        )
+        attended = (attended * inv_ref[unit, 0:1]).astype(jnp.bfloat16)
+        query_grad = lax.dot_general(
+            listed[2 * slot + 1], ds_ref[unit], TN, preferred_element_type=jnp.float32
+        )
+        query_grad = (query_grad * scale).astype(jnp.bfloat16)
+        for g, part in enumerate(units.parts(unit)):
+            out_ref[units.rows(unit), part] = attended[:, g * BLK : (g + 1) * BLK].T
+            dq_ref[units.rows(unit), part] = query_grad[:, g * BLK : (g + 1) * BLK].T
+
+
+def to_head_groups(rows):
+    me = lax.axis_index("tp")
+    count = lax.axis_size("tp")
+    width = rows.shape[1] // count
+    parts = []
+    for mask in range(count):
+        part = lax.dynamic_slice_in_dim(rows, (me ^ mask) * width, width, 1)
+        parts.append(part if mask == 0 else swap(part, "tp", mask))
+    return jnp.stack(parts)
+
+
+def to_quarters(pieces):
+    me = lax.axis_index("tp")
+    count, quarter, width = pieces.shape
+    out = jnp.zeros((quarter, count * width), pieces.dtype)
+    for mask in range(count):
+        part = pieces[mask] if mask == 0 else swap(pieces[mask], "tp", mask)
+        out = lax.dynamic_update_slice(out, part, (0, (me ^ mask) * width))
+    return out
+
+
+def gather_shards(own, after):
+    half = own.shape[0] // 2
+    started = own if after is None else lax.optimization_barrier((own, after))[0]
+    across = swap(started, "ctx", 2)
+    along = swap(started, "ctx", 4)
+    first = swap(along[:half], "ctx", 2)
+    second = swap(across[half:], "ctx", 4)
+    near = [own, across, along, first, second]
+    far = [swap(part, "ctx", 1) for part in near]
+    return near + far
+
+
+def shard_pieces(count):
+    half = count // 2
+    near = [(0, 0, count), (2, 0, count), (4, 0, count), (6, 0, half), (6, half, half)]
+    return near + [(shard + 1, first, many) for shard, first, many in near]
+
+
+def sum_shards(near, far3, far12, far0):
+    half = near.shape[1] // 2
+    got3 = swap(far3, "ctx", 1)
+    got12 = swap(far12, "ctx", 1)
+    got0 = swap(far0, "ctx", 1)
+    diag_a = near[3, :half] + got3[:half]
+    diag_b = near[3, half:] + got3[half:]
+    from_x = swap(diag_a, "ctx", 2)
+    from_y = swap(diag_b, "ctx", 4)
+    across_a = near[1, :half] + got12[0, :half]
+    along_b = near[2, half:] + got12[1, half:]
+    own_a = swap(across_a, "ctx", 2)
+    own_b = swap(along_b, "ctx", 4)
+    across_b = near[1, half:] + got12[0, half:] + from_y
+    along_a = near[2, :half] + got12[1, :half] + from_x
+    more_b = swap(across_b, "ctx", 2)
+    more_a = swap(along_a, "ctx", 4)
+    own = near[0] + got0
+    return own + jnp.concatenate([own_a + more_a, own_b + more_b], axis=0)
+
+
+def dense_plan(queries, key_rows, value_rows, out_grad, block_list):
+    tokens = queries.shape[0]
+    blocks = tokens // BLK
+    shard_total = lax.axis_size("ctx")
+    quarters = lax.axis_size("tp")
+    width = block_list.shape[1]
+    head_width = key_rows.shape[1] // quarters
+    heads = head_width // HD
+    group = queries.shape[1] // head_width
+    rows = shard_total * tokens
+    me_ctx = lax.axis_index("ctx")
+    me_tp = lax.axis_index("tp").reshape(1)
+    places = ((block_list // blocks) ^ me_ctx) * blocks + block_list % blocks
+    places = places.reshape(-1)
+    quarter = tokens // quarters
+    pieces = shard_pieces(quarters)
+    units = Units(blocks, width, heads, group)
+    list_len = width * BLK
+    query_rows = group * BLK
+    big = (units.count, list_len, query_rows)
+
+    in_vmem = pl.BlockSpec(memory_space=pltpu.VMEM)
+    in_smem = pl.BlockSpec(memory_space=pltpu.SMEM)
+    shard_sum = (quarters, quarter, head_width)
+    sum_shapes = [
+        pltpu.VMEM((shard_total // 2, *shard_sum), jnp.bfloat16),
+        pltpu.VMEM(shard_sum, jnp.bfloat16),
+        pltpu.VMEM((2, *shard_sum), jnp.bfloat16),
+        pltpu.VMEM(shard_sum, jnp.bfloat16),
+    ]
+    scratch = [
+        pltpu.VMEM((rows, head_width), jnp.float32),
+        pltpu.VMEM((2, list_len, query_rows), jnp.float32),
+    ]
+    params = pltpu.CompilerParams(vmem_limit_bytes=16 * 2**20)
+    cost = pl.CostEstimate(
+        flops=4 * units.count * list_len * query_rows * HD, bytes_accessed=2**24, transcendentals=0
+    )
+
+    key_groups = to_head_groups(key_rows)
+    keys = gather_shards(key_groups, None)
+    value_rows = lax.optimization_barrier((value_rows, key_groups))[0]
+    values = gather_shards(to_head_groups(value_rows), (keys[3], keys[4]))
+
+    made = pl.pallas_call(
+        functools.partial(probs_kernel, pieces, units, tokens),
+        in_specs=[in_smem] * 2 + [in_vmem] * (2 + len(pieces)),
+        out_specs=[in_vmem] * 8,
+        out_shape=[
+            pltpu.VMEM(big, jnp.bfloat16),
+            pltpu.VMEM((units.count, HD, query_rows), jnp.bfloat16),
+            pltpu.VMEM((units.count, 8, query_rows), jnp.float32),
+            pltpu.VMEM((rows, head_width), jnp.bfloat16),
+        ]
+        + sum_shapes,
+        scratch_shapes=scratch,
+        compiler_params=params,
+        cost_estimate=cost,
+        name="probs",
+    )(places, me_tp, queries, out_grad, *keys)
+    exp_low, grad_t, inverse, keys_in_order = made[:4]
+    value_sum = sum_shards(*made[4:])
+
+    made = pl.pallas_call(
+        functools.partial(scores_kernel, pieces, units, tokens),
+        in_specs=[in_smem] * 2 + [in_vmem] * (4 + len(pieces)),
+        out_specs=[in_vmem] * 6,
+        out_shape=[pltpu.VMEM(big, jnp.bfloat16), pltpu.VMEM((rows, head_width), jnp.bfloat16)]
+        + sum_shapes,
+        scratch_shapes=scratch,
+        compiler_params=params,
+        cost_estimate=cost,
+        name="scores",
+    )(places, me_tp, queries, exp_low, grad_t, inverse, *values)
+    ds_low, values_in_order = made[:2]
+    key_sum = sum_shards(*made[2:])
+
+    attended, query_grad = pl.pallas_call(
+        functools.partial(rows_kernel, units),
+        in_specs=[in_smem] + [in_vmem] * 5,
+        out_specs=[in_vmem] * 2,
+        out_shape=[jax.ShapeDtypeStruct(queries.shape, jnp.bfloat16)] * 2,
+        scratch_shapes=[pltpu.VMEM((4, list_len, HD), jnp.bfloat16)],
+        compiler_params=params,
+        cost_estimate=cost,
+        name="rows",
+    )(places, exp_low, ds_low, inverse, keys_in_order, values_in_order)
+    return attended, query_grad, to_quarters(key_sum), to_quarters(value_sum)
+
+
 def solution(mesh):
+    dense = mesh.shape["ctx"] == DENSE_SHARDS and mesh.shape["tp"] % 4 == 0
     in_specs = (
         P("ctx", "tp"),
         P(("ctx", "tp"), None),
@@ -201,4 +535,10 @@
         P("ctx", None),
     )
     out_specs = (P("ctx", "tp"), P("ctx", "tp"), P(("ctx", "tp"), None), P(("ctx", "tp"), None))
-    return jax.shard_map(shards, mesh=mesh, in_specs=in_specs, out_specs=out_specs, check_vma=False)
+    return jax.shard_map(
+        dense_plan if dense else sparse_plan,
+        mesh=mesh,
+        in_specs=in_specs,
+        out_specs=out_specs,
+        check_vma=False,
+    )

time: 403 us -> 132 us (0.33)
  local copies, waits for them, and re-layouts: 139 us -> 12.8 us
  waiting for transfers between devices: 111 us -> 42.9 us
  matrix products: 63.8 us -> 0 us
  Pallas kernels: 0 us -> 29.4 us
  other arithmetic: 22.5 us -> 1.67 us
  between operations: 19.5 us -> 0.97 us
  blocking collectives: 13.8 us -> 0 us
  starting transfers between devices: 30.5 us -> 43.6 us
    psum x2 -> x0, waiting for transfers between devices: 66.9 us -> none  [the longest x1 46.1 us: spread(): return lax.psum(jnp.where(mine, x, jnp.zeros_like(x)), axis)]
    dot_general x32 -> x0, matrix products: 63.8 us -> none  [the longest x5 20.6 us: attend_block(): jnp.einsum('kgqn,qkgd->nkd', weights_low, grad_tile, preferred_element_ty...]
    ppermute x4 -> x48, starting transfers between devices: 5.45 us -> 43.6 us  [swap(): return lax.ppermute(value, axis, [(i, i ^ mask) for i in range(count)])]
    reshape x9 -> x1, local copies, waits for them, and re-layouts: 35.2 us -> 0.08 us  [dense_plan(): places = places.reshape(-1)]
    pallas_call x0 -> x3, Pallas kernels: none -> 29.4 us  [the longest x1 11.7 us: dense_plan(): pl.pallas_call(functools.partial(probs_kernel, pieces, units, tokens), in...]
    dynamic_slice x30 -> x0, local copies, waits for them, and re-layouts: 27.7 us -> none  [shards(): lax.map(attend_block, (query_tiles, grad_tiles, keys_here, values_here))]
    all_to_all x6 -> x0, starting transfers between devices: 24.9 us -> none  [the longest x1 5.17 us: shards(): lax.all_to_all(wanted.reshape(shard_total, capacity), 'ctx', split_axis=0...]
    all_to_all x6 -> x0, waiting for transfers between devices: 22.3 us -> none  [the longest x1 8.58 us: shards(): lax.all_to_all(key_rows, 'tp', split_axis=1, concat_axis=0, tiled=True)]
  transfers between devices with their start and end apart: 12 -> 48, of which waited for: 7 -> 21; matrix products, arithmetic and copies ran while one was open for 12% -> 2% of each run, Pallas kernels for 0% -> 22%
where the time goes in v2:
time: 132 us; the launch traced here: 131 us
  starting transfers between devices  43.6 us (33%)
  waiting for transfers between devices  42.9 us (32%)
  Pallas kernels  29.4 us (22%)
  local copies, waits for them, and re-layouts  12.8 us (10%)
  other arithmetic  1.67 us (1%)
    ppermute x48, starting transfers between devices, swap(): return lax.ppermute(value, axis, [(i, i ^ mask) for i in range(count)])  43.6 us
    ppermute x48, waiting for transfers between devices, swap(): return lax.ppermute(value, axis, [(i, i ^ mask) for i in range(count)])  42.9 us
    pallas_call x1, Pallas kernels, dense_plan(): pl.pallas_call(functools.partial(probs_kernel, pieces, units, tokens), in...  11.7 us
    pallas_call x1, Pallas kernels, dense_plan(): pl.pallas_call(functools.partial(scores_kernel, pieces, units, tokens), i...  11.1 us
    unnamed x16, local copies, waits for them, and re-layouts  10.1 us
    pallas_call x1, Pallas kernels, dense_plan(): pl.pallas_call(functools.partial(rows_kernel, units), in_specs=[in_smem]...  6.63 us
  transfers between devices with their start and end apart: 48, of which 21 were waited for; matrix products, arithmetic and copies ran while one was open for 2% of the time, Pallas kernels for 22%

profile of v2, /device:TPU:0, one launch (start us, length us, event | category | flops | bytes accessed | tf_op | source)
XLA Modules:
  0.0 131.3 jit_solution(2460830776286624181)
XLA Ops:
  1.8 3.1 %collective-permute-start = (bf16[160,256]{1,0:T(8,128)(2,1)S(1)}, bf16[160,256]{1,0:T(8,128)(2,1)S(1)}, u32[]{:S(2)}, u32[]{:S(2)}) collective-permute-start(bf16[160,256]{1,0:T(8,128)(2,1)S(1)} %get-tuple-element.63), channel_id=1, source_target_pairs={{0,1},{1,0},{2,3},{3,2},{4,5},{5,4},{6,7},{7,6},{8,9},{9,8},{10,11... | collective-permute-start | bytes 245768 | tf_op jit(solution)/shard_map/ppermute | solution.py:207
  4.8 2.6 %collective-permute-start.1 = (bf16[160,256]{1,0:T(8,128)(2,1)S(1)}, bf16[160,256]{1,0:T(8,128)(2,1)S(1)}, u32[]{:S(2)}, u32[]{:S(2)}) collective-permute-start(bf16[160,256]{1,0:T(8,128)(2,1)S(1)} %get-tuple-element.65), channel_id=1, source_target_pairs={{0,2},{1,3},{2,0},{3,1},{4,6},{5,7},{6,4},{7,5},{8,10},{9,11},{10,... | collective-permute-start | bytes 245768 | tf_op jit(solution)/shard_map/ppermute | solution.py:207
  7.4 6.6 %collective-permute-done.1 = bf16[160,256]{1,0:T(8,128)(2,1)S(1)} collective-permute-done((bf16[160,256]{1,0:T(8,128)(2,1)S(1)}, bf16[160,256]{1,0:T(8,128)(2,1)S(1)}, u32[]{:S(2)}, u32[]{:S(2)}) %collective-permute-start.1) | collective-permute-done | bytes 81952 | tf_op jit(solution)/shard_map/ppermute | solution.py:207
  14.1 1.6 %collective-permute-start.4 = (bf16[4,160,256]{2,1,0:T(8,128)(2,1)S(1)}, bf16[4,160,256]{2,1,0:T(8,128)(2,1)S(1)}, u32[]{:S(2)}, u32[]{:S(2)}) collective-permute-start(bf16[4,160,256]{2,1,0:T(8,128)(2,1)S(1)} %pad_maximum_fusion.refs_0_), channel_id=1, source_target_pairs={{0,16},{4,20},{8,24},{12,28},{16,0},{20,4},{24,8},{28,12},{1,17},{... | collective-permute-start | bytes 983048 | tf_op jit(solution)/shard_map/ppermute | solution.py:207
  15.7 1.5 %collective-permute-start.3 = (bf16[4,160,256]{2,1,0:T(8,128)(2,1)S(1)}, bf16[4,160,256]{2,1,0:T(8,128)(2,1)S(1)}, u32[]{:S(2)}, u32[]{:S(2)}) collective-permute-start(bf16[4,160,256]{2,1,0:T(8,128)(2,1)S(1)} %pad_maximum_fusion.refs_0_), channel_id=1, source_target_pairs={{0,8},{4,12},{8,0},{12,4},{16,24},{20,28},{24,16},{28,20},{1,9},{5... | collective-permute-start | bytes 983048 | tf_op jit(solution)/shard_map/ppermute | solution.py:207
  17.2 4.5 %collective-permute-done.4.refs_2_ = bf16[4,160,256]{2,1,0:T(8,128)(2,1)S(1)} collective-permute-done((bf16[4,160,256]{2,1,0:T(8,128)(2,1)S(1)}, bf16[4,160,256]{2,1,0:T(8,128)(2,1)S(1)}, u32[]{:S(2)}, u32[]{:S(2)}) %collective-permute-start.4) | collective-permute-done | bytes 327712 | tf_op jit(solution)/shard_map/ppermute | solution.py:207
  22.3 1.5 %collective-permute-start.5 = (bf16[2,160,256]{2,1,0:T(8,128)(2,1)}, bf16[2,160,256]{2,1,0:T(8,128)(2,1)S(1)}, u32[]{:S(2)}, u32[]{:S(2)}) collective-permute-start(bf16[2,160,256]{2,1,0:T(8,128)(2,1)} %slice.152), channel_id=1, source_target_pairs={{0,8},{4,12},{8,0},{12,4},{16,24},{20,28},{24,16},{28,20},{1,9},{5... | collective-permute-start | bytes 491528 | tf_op jit(solution)/shard_map/ppermute | solution.py:207
  24.5 1.5 %collective-permute-start.6 = (bf16[2,160,256]{2,1,0:T(8,128)(2,1)}, bf16[2,160,256]{2,1,0:T(8,128)(2,1)}, u32[]{:S(2)}, u32[]{:S(2)}) collective-permute-start(bf16[2,160,256]{2,1,0:T(8,128)(2,1)} %slice.153), channel_id=1, source_target_pairs={{0,16},{4,20},{8,24},{12,28},{16,0},{20,4},{24,8},{28,12},{1,17},{... | collective-permute-start | bytes 491528 | tf_op jit(solution)/shard_map/ppermute | solution.py:207
  26.1 2.5 %collective-permute-start.12 = (bf16[160,256]{1,0:T(8,128)(2,1)S(1)}, bf16[160,256]{1,0:T(8,128)(2,1)}, u32[]{:S(2)}, u32[]{:S(2)}) collective-permute-start(bf16[160,256]{1,0:T(8,128)(2,1)S(1)} %get-tuple-element.61), channel_id=1, source_target_pairs={{0,1},{1,0},{2,3},{3,2},{4,5},{5,4},{6,7},{7,6},{8,9},{9,8},{10,11... | collective-permute-start | bytes 245768 | tf_op jit(solution)/shard_map/ppermute | solution.py:207
  29.4 1.5 %collective-permute-start.14 = (bf16[160,256]{1,0:T(8,128)(2,1)S(1)}, bf16[160,256]{1,0:T(8,128)(2,1)}, u32[]{:S(2)}, u32[]{:S(2)}) collective-permute-start(bf16[160,256]{1,0:T(8,128)(2,1)S(1)} %get-tuple-element.59), channel_id=1, source_target_pairs={{0,3},{1,2},{2,1},{3,0},{4,7},{5,6},{6,5},{7,4},{8,11},{9,10},{10,... | collective-permute-start | bytes 245768 | tf_op jit(solution)/shard_map/ppermute | solution.py:207
  31.0 1.4 %collective-permute-done.12 = bf16[160,256]{1,0:T(8,128)(2,1)} collective-permute-done((bf16[160,256]{1,0:T(8,128)(2,1)S(1)}, bf16[160,256]{1,0:T(8,128)(2,1)}, u32[]{:S(2)}, u32[]{:S(2)}) %collective-permute-start.12) | collective-permute-done | bytes 81952 | tf_op jit(solution)/shard_map/ppermute | solution.py:207
  32.4 2.5 %collective-permute-done.13 = bf16[160,256]{1,0:T(8,128)(2,1)} collective-permute-done((bf16[160,256]{1,0:T(8,128)(2,1)S(1)}, bf16[160,256]{1,0:T(8,128)(2,1)}, u32[]{:S(2)}, u32[]{:S(2)}) %collective-permute-start.13) | collective-permute-done | bytes 81952 | tf_op jit(solution)/shard_map/ppermute | solution.py:207
  41.8 11.7 %probs.1 = (bf16[10,1024,512]{2,1,0:T(8,128)(2,1)S(1)}, bf16[10,128,512]{2,1,0:T(8,128)(2,1)S(1)}, f32[10,8,512]{2,1,0:T(8,128)S(1)}, bf16[5120,256]{1,0:T(8,128...) custom-call(s32[40]{0:T(128)S(1)} %reshape.22.place_ref, ...), custom_call_target="tpu_custom_call" | custom-call | flops 2684354560 | bytes 16777216 | tf_op jit(solution)/shard_map/probs/pallas_call | solution.py:482
  56.2 4.2 %collective-permute-done.17.refs_3_ = bf16[2,160,256]{2,1,0:T(8,128)(2,1)S(1)} collective-permute-done((bf16[2,160,256]{2,1,0:T(8,128)(2,1)S(1)}, bf16[2,160,256]{2,1,0:T(8,128)(2,1)S(1)}, u32[]{:S(2)}, u32[]{:S(2)}) %collective-permute-start.17) | collective-permute-done | bytes 163872 | tf_op jit(solution)/shard_map/ppermute | solution.py:207
  62.2 1.4 %collective-permute-start.40 = (bf16[2,160,256]{2,1,0:T(8,128)(2,1)S(1)}, bf16[2,160,256]{2,1,0:T(8,128)(2,1)S(1)}, u32[]{:S(2)}, u32[]{:S(2)}) collective-permute-start(bf16[2,160,256]{2,1,0:T(8,128)(2,1)S(1)} %get-tuple-element.48), channel_id=1, source_target_pairs={{0,8},{4,12},{8,0},{12,4},{16,24},{20,28},{24,16},{28,20},{1,9},{5... | collective-permute-start | bytes 491528 | tf_op jit(solution)/shard_map/ppermute | solution.py:207
  63.9 11.1 %scores.1 = (bf16[10,1024,512]{2,1,0:T(8,128)(2,1)S(1)}, bf16[5120,256]{1,0:T(8,128)(2,1)S(1)}, bf16[4,4,160,256]{3,2,1,0:T(8,128)(2,1)S(1)}, bf16[4,160,256]{2,...) custom-call(s32[40]{0:T(128)S(1)} %reshape.22.place_ref, s32[1]{0:T(128)} %bitcast.tp_ref, ...), custom_call_target="tpu_custom_call" | custom-call | flops 2684354560 | bytes 16777216 | tf_op jit(solution)/shard_map/scores/pallas_call | solution.py:501
  75.0 4.0 %copy-done = bf16[10,1024,512]{2,1,0:T(8,128)(2,1)} copy-done((bf16[10,1024,512]{2,1,0:T(8,128)(2,1)}, bf16[10,1024,512]{2,1,0:T(8,128)(2,1)S(1)}, u32[]{:S(2)}) %copy-start) | copy-done | bytes 10485784
  79.0 4.0 %copy-done.1 = bf16[10,1024,512]{2,1,0:T(8,128)(2,1)S(1)} copy-done((bf16[10,1024,512]{2,1,0:T(8,128)(2,1)S(1)}, bf16[10,1024,512]{2,1,0:T(8,128)(2,1)}, u32[]{:S(2)}) %copy-start.1) | copy-done | bytes 10485784
  83.0 6.6 %rows.1 = (bf16[640,1024]{1,0:T(8,128)(2,1)}, bf16[640,1024]{1,0:T(8,128)(2,1)}) custom-call(s32[40]{0:T(128)S(1)} %reshape.22.place_ref, bf16[10,1024,512]{2,1,0:T(8,128)(2,1)S(1)} %get-tuple-element.22.exp_ref, bf16[10,1024,512]{2,1,0:T(8,128)(2,1)S(1)} %copy-done.1, f32[10,8,512]{2,1,0:T(8,128)S(1)} %get-tuple-element.24.inv_ref, ...), custom_call_target="tpu_custom_call" | custom-call | flops 2684354560 | bytes 16777216 | tf_op jit(solution)/shard_map/rows/pallas_call | solution.py:515
  89.7 1.8 %collective-permute-start.41 = (bf16[2,160,256]{2,1,0:T(8,128)(2,1)S(1)}, bf16[2,160,256]{2,1,0:T(8,128)(2,1)S(1)}, u32[]{:S(2)}, u32[]{:S(2)}) collective-permute-start(bf16[2,160,256]{2,1,0:T(8,128)(2,1)S(1)} %get-tuple-element.40), channel_id=1, source_target_pairs={{0,16},{4,20},{8,24},{12,28},{16,0},{20,4},{24,8},{28,12},{1,17},{... | collective-permute-start | bytes 491528 | tf_op jit(solution)/shard_map/ppermute | solution.py:207
  94.0 2.8 %collective-permute-done.41 = bf16[2,160,256]{2,1,0:T(8,128)(2,1)S(1)} collective-permute-done((bf16[2,160,256]{2,1,0:T(8,128)(2,1)S(1)}, bf16[2,160,256]{2,1,0:T(8,128)(2,1)S(1)}, u32[]{:S(2)}, u32[]{:S(2)}) %collective-permute-start.41) | collective-permute-done | bytes 163872 | tf_op jit(solution)/shard_map/ppermute | solution.py:207
  96.8 1.9 %collective-permute-done.38 = bf16[2,160,256]{2,1,0:T(8,128)(2,1)S(1)} collective-permute-done((bf16[2,160,256]{2,1,0:T(8,128)(2,1)S(1)}, bf16[2,160,256]{2,1,0:T(8,128)(2,1)S(1)}, u32[]{:S(2)}, u32[]{:S(2)}) %collective-permute-start.38) | collective-permute-done | bytes 163872 | tf_op jit(solution)/shard_map/ppermute | solution.py:207
  98.7 2.8 %collective-permute-done.44 = bf16[2,160,256]{2,1,0:T(8,128)(2,1)S(1)} collective-permute-done((bf16[2,160,256]{2,1,0:T(8,128)(2,1)S(1)}, bf16[2,160,256]{2,1,0:T(8,128)(2,1)S(1)}, u32[]{:S(2)}, u32[]{:S(2)}) %collective-permute-start.44) | collective-permute-done | bytes 163872 | tf_op jit(solution)/shard_map/ppermute | solution.py:207
  104.8 3.1 %collective-permute-done.45 = bf16[160,256]{1,0:T(8,128)(2,1)S(1)} collective-permute-done((bf16[160,256]{1,0:T(8,128)(2,1)S(1)}, bf16[160,256]{1,0:T(8,128)(2,1)S(1)}, u32[]{:S(2)}, u32[]{:S(2)}) %collective-permute-start.45) | collective-permute-done | bytes 81952 | tf_op jit(solution)/shard_map/ppermute | solution.py:207
  107.9 1.6 %collective-permute-start.46 = (bf16[160,256]{1,0:T(8,128)(2,1)S(1)}, bf16[160,256]{1,0:T(8,128)(2,1)S(1)}, u32[]{:S(2)}, u32[]{:S(2)}) collective-permute-start(bf16[160,256]{1,0:T(8,128)(2,1)S(1)} %get-tuple-element.53), channel_id=1, source_target_pairs={{0,2},{1,3},{2,0},{3,1},{4,6},{5,7},{6,4},{7,5},{8,10},{9,11},{10,... | collective-permute-start | bytes 245768 | tf_op jit(solution)/shard_map/ppermute | solution.py:207
  109.6 2.1 %collective-permute-start.47 = (bf16[160,256]{1,0:T(8,128)(2,1)S(1)}, bf16[160,256]{1,0:T(8,128)(2,1)S(1)}, u32[]{:S(2)}, u32[]{:S(2)}) collective-permute-start(bf16[160,256]{1,0:T(8,128)(2,1)S(1)} %get-tuple-element.52), channel_id=1, source_target_pairs={{0,3},{1,2},{2,1},{3,0},{4,7},{5,6},{6,5},{7,4},{8,11},{9,10},{10,... | collective-permute-start | bytes 245768 | tf_op jit(solution)/shard_map/ppermute | solution.py:207
  112.9 1.8 %collective-permute-done.46 = bf16[160,256]{1,0:T(8,128)(2,1)S(1)} collective-permute-done((bf16[160,256]{1,0:T(8,128)(2,1)S(1)}, bf16[160,256]{1,0:T(8,128)(2,1)S(1)}, u32[]{:S(2)}, u32[]{:S(2)}) %collective-permute-start.46) | collective-permute-done | bytes 81952 | tf_op jit(solution)/shard_map/ppermute | solution.py:207
  116.0 1.6 %collective-permute-start.30 = (bf16[2,160,256]{2,1,0:T(8,128)(2,1)S(1)}, bf16[2,160,256]{2,1,0:T(8,128)(2,1)S(1)}, u32[]{:S(2)}, u32[]{:S(2)}) collective-permute-start(bf16[2,160,256]{2,1,0:T(8,128)(2,1)S(1)} %get-tuple-element.47), channel_id=1, source_target_pairs={{0,16},{4,20},{8,24},{12,28},{16,0},{20,4},{24,8},{28,12},{1,17},{... | collective-permute-start | bytes 491528 | tf_op jit(solution)/shard_map/ppermute | solution.py:207
  122.6 1.6 %collective-permute-start.34 = (bf16[160,256]{1,0:T(8,128)(2,1)S(1)}, bf16[160,256]{1,0:T(8,128)(2,1)S(1)}, u32[]{:S(2)}, u32[]{:S(2)}) collective-permute-start(bf16[160,256]{1,0:T(8,128)(2,1)S(1)} %get-tuple-element.56), channel_id=1, source_target_pairs={{0,2},{1,3},{2,0},{3,1},{4,6},{5,7},{6,4},{7,5},{8,10},{9,11},{10,... | collective-permute-start | bytes 245768 | tf_op jit(solution)/shard_map/ppermute | solution.py:207
  124.2 1.8 %collective-permute-start.35 = (bf16[160,256]{1,0:T(8,128)(2,1)S(1)}, bf16[160,256]{1,0:T(8,128)(2,1)S(1)}, u32[]{:S(2)}, u32[]{:S(2)}) collective-permute-start(bf16[160,256]{1,0:T(8,128)(2,1)S(1)} %get-tuple-element.55), channel_id=1, source_target_pairs={{0,3},{1,2},{2,1},{3,0},{4,7},{5,6},{6,5},{7,4},{8,11},{9,10},{10,... | collective-permute-start | bytes 245768 | tf_op jit(solution)/shard_map/ppermute | solution.py:207
  126.9 2.0 %collective-permute-done.34 = bf16[160,256]{1,0:T(8,128)(2,1)S(1)} collective-permute-done((bf16[160,256]{1,0:T(8,128)(2,1)S(1)}, bf16[160,256]{1,0:T(8,128)(2,1)S(1)}, u32[]{:S(2)}, u32[]{:S(2)}) %collective-permute-start.34) | collective-permute-done | bytes 81952 | tf_op jit(solution)/shard_map/ppermute | solution.py:207
  128.9 1.7 %collective-permute-done.35 = bf16[160,256]{1,0:T(8,128)(2,1)S(1)} collective-permute-done((bf16[160,256]{1,0:T(8,128)(2,1)S(1)}, bf16[160,256]{1,0:T(8,128)(2,1)S(1)}, u32[]{:S(2)}, u32[]{:S(2)}) %collective-permute-start.35) | collective-permute-done | bytes 81952 | tf_op jit(solution)/shard_map/ppermute | solution.py:207
  (117 shorter events, 30.1 us)
Async XLA Ops:
  4.8 9.2 %collective-permute-start.1 = (bf16[160,256]{1,0:T(8,128)(2,1)S(1)}, bf16[160,256]{1,0:T(8,128)(2,1)S(1)}, u32[]{:S(2)}, u32[]{:S(2)}) collective-permute-start(bf16[160,256]{1,0:T(8,128)(2,1)S(1)} %get-tuple-element.65), channel_id=1, source_target_pairs={{0,2},{1,3},{2,0},{3,1},{4,6},{5,7},{6,4},{7,5},{8,10},{9,11},{10,... | collective-permute-start | bytes 245768 | tf_op jit(solution)/shard_map/ppermute | solution.py:207
  7.4 6.6 %collective-permute-start.2 = (bf16[160,256]{1,0:T(8,128)(2,1)S(1)}, bf16[160,256]{1,0:T(8,128)(2,1)S(1)}, u32[]{:S(2)}, u32[]{:S(2)}) collective-permute-start(bf16[160,256]{1,0:T(8,128)(2,1)S(1)} %get-tuple-element.64), channel_id=1, source_target_pairs={{0,3},{1,2},{2,1},{3,0},{4,7},{5,6},{6,5},{7,4},{8,11},{9,10},{10,... | collective-permute-start | bytes 245768 | tf_op jit(solution)/shard_map/ppermute | solution.py:207
  14.1 7.6 %collective-permute-start.4 = (bf16[4,160,256]{2,1,0:T(8,128)(2,1)S(1)}, bf16[4,160,256]{2,1,0:T(8,128)(2,1)S(1)}, u32[]{:S(2)}, u32[]{:S(2)}) collective-permute-start(bf16[4,160,256]{2,1,0:T(8,128)(2,1)S(1)} %pad_maximum_fusion.refs_0_), channel_id=1, source_target_pairs={{0,16},{4,20},{8,24},{12,28},{16,0},{20,4},{24,8},{28,12},{1,17},{... | collective-permute-start | bytes 983048 | tf_op jit(solution)/shard_map/ppermute | solution.py:207
  15.7 8.2 %collective-permute-start.3 = (bf16[4,160,256]{2,1,0:T(8,128)(2,1)S(1)}, bf16[4,160,256]{2,1,0:T(8,128)(2,1)S(1)}, u32[]{:S(2)}, u32[]{:S(2)}) collective-permute-start(bf16[4,160,256]{2,1,0:T(8,128)(2,1)S(1)} %pad_maximum_fusion.refs_0_), channel_id=1, source_target_pairs={{0,8},{4,12},{8,0},{12,4},{16,24},{20,28},{24,16},{28,20},{1,9},{5... | collective-permute-start | bytes 983048 | tf_op jit(solution)/shard_map/ppermute | solution.py:207
  22.3 13.6 %collective-permute-start.5 = (bf16[2,160,256]{2,1,0:T(8,128)(2,1)}, bf16[2,160,256]{2,1,0:T(8,128)(2,1)S(1)}, u32[]{:S(2)}, u32[]{:S(2)}) collective-permute-start(bf16[2,160,256]{2,1,0:T(8,128)(2,1)} %slice.152), channel_id=1, source_target_pairs={{0,8},{4,12},{8,0},{12,4},{16,24},{20,28},{24,16},{28,20},{1,9},{5... | collective-permute-start | bytes 491528 | tf_op jit(solution)/shard_map/ppermute | solution.py:207
  24.5 11.9 %collective-permute-start.6 = (bf16[2,160,256]{2,1,0:T(8,128)(2,1)}, bf16[2,160,256]{2,1,0:T(8,128)(2,1)}, u32[]{:S(2)}, u32[]{:S(2)}) collective-permute-start(bf16[2,160,256]{2,1,0:T(8,128)(2,1)} %slice.153), channel_id=1, source_target_pairs={{0,16},{4,20},{8,24},{12,28},{16,0},{20,4},{24,8},{28,12},{1,17},{... | collective-permute-start | bytes 491528 | tf_op jit(solution)/shard_map/ppermute | solution.py:207
  29.4 6.4 %collective-permute-start.14 = (bf16[160,256]{1,0:T(8,128)(2,1)S(1)}, bf16[160,256]{1,0:T(8,128)(2,1)}, u32[]{:S(2)}, u32[]{:S(2)}) collective-permute-start(bf16[160,256]{1,0:T(8,128)(2,1)S(1)} %get-tuple-element.59), channel_id=1, source_target_pairs={{0,3},{1,2},{2,1},{3,0},{4,7},{5,6},{6,5},{7,4},{8,11},{9,10},{10,... | collective-permute-start | bytes 245768 | tf_op jit(solution)/shard_map/ppermute | solution.py:207
  37.6 18.0 %collective-permute-start.19 = (bf16[4,160,256]{2,1,0:T(8,128)(2,1)S(1)}, bf16[4,160,256]{2,1,0:T(8,128)(2,1)S(1)}, u32[]{:S(2)}, u32[]{:S(2)}) collective-permute-start(bf16[4,160,256]{2,1,0:T(8,128)(2,1)S(1)} %pad_maximum_fusion.1.refs_0_), channel_id=1, source_target_pairs={{0,4},{4,0},{8,12},{12,8},{16,20},{20,16},{24,28},{28,24},{1,5},{5... | collective-permute-start | bytes 983048 | tf_op jit(solution)/shard_map/ppermute | solution.py:207
  38.1 15.6 %collective-permute-start.16 = (bf16[4,160,256]{2,1,0:T(8,128)(2,1)S(1)}, bf16[4,160,256]{2,1,0:T(8,128)(2,1)S(1)}, u32[]{:S(2)}, u32[]{:S(2)}) collective-permute-start(bf16[4,160,256]{2,1,0:T(8,128)(2,1)S(1)} %pad_maximum_fusion.1.refs_0_), channel_id=1, source_target_pairs={{0,16},{4,20},{8,24},{12,28},{16,0},{20,4},{24,8},{28,12},{1,17},{... | collective-permute-start | bytes 983048 | tf_op jit(solution)/shard_map/ppermute | solution.py:207
  39.0 15.4 %collective-permute-start.15 = (bf16[4,160,256]{2,1,0:T(8,128)(2,1)S(1)}, bf16[4,160,256]{2,1,0:T(8,128)(2,1)S(1)}, u32[]{:S(2)}, u32[]{:S(2)}) collective-permute-start(bf16[4,160,256]{2,1,0:T(8,128)(2,1)S(1)} %pad_maximum_fusion.1.refs_0_), channel_id=1, source_target_pairs={{0,8},{4,12},{8,0},{12,4},{16,24},{20,28},{24,16},{28,20},{1,9},{5... | collective-permute-start | bytes 983048 | tf_op jit(solution)/shard_map/ppermute | solution.py:207
  53.7 6.7 %collective-permute-start.17 = (bf16[2,160,256]{2,1,0:T(8,128)(2,1)S(1)}, bf16[2,160,256]{2,1,0:T(8,128)(2,1)S(1)}, u32[]{:S(2)}, u32[]{:S(2)}) collective-permute-start(bf16[2,160,256]{2,1,0:T(8,128)(2,1)S(1)} %slice.154), channel_id=1, source_target_pairs={{0,8},{4,12},{8,0},{12,4},{16,24},{20,28},{24,16},{28,20},{1,9},{5... | collective-permute-start | bytes 491528 | tf_op jit(solution)/shard_map/ppermute | solution.py:207
  54.4 6.4 %collective-permute-start.18 = (bf16[2,160,256]{2,1,0:T(8,128)(2,1)S(1)}, bf16[2,160,256]{2,1,0:T(8,128)(2,1)S(1)}, u32[]{:S(2)}, u32[]{:S(2)}) collective-permute-start(bf16[2,160,256]{2,1,0:T(8,128)(2,1)S(1)} %slice.155), channel_id=1, source_target_pairs={{0,16},{4,20},{8,24},{12,28},{16,0},{20,4},{24,8},{28,12},{1,17},{... | collective-permute-start | bytes 491528 | tf_op jit(solution)/shard_map/ppermute | solution.py:207
  55.6 8.0 %collective-permute-start.20 = (bf16[4,160,256]{2,1,0:T(8,128)(2,1)S(1)}, bf16[4,160,256]{2,1,0:T(8,128)(2,1)S(1)}, u32[]{:S(2)}, u32[]{:S(2)}) collective-permute-start(bf16[4,160,256]{2,1,0:T(8,128)(2,1)S(1)} %collective-permute-done.15.refs_1_), channel_id=1, source_target_pairs={{0,4},{4,0},{8,12},{12,8},{16,20},{20,16},{24,28},{28,24},{1,5},{5... | collective-permute-start | bytes 983048 | tf_op jit(solution)/shard_map/ppermute | solution.py:207
  55.6 8.3 %collective-permute-start.21 = (bf16[4,160,256]{2,1,0:T(8,128)(2,1)S(1)}, bf16[4,160,256]{2,1,0:T(8,128)(2,1)S(1)}, u32[]{:S(2)}, u32[]{:S(2)}) collective-permute-start(bf16[4,160,256]{2,1,0:T(8,128)(2,1)S(1)} %collective-permute-done.16.refs_2_), channel_id=1, source_target_pairs={{0,4},{4,0},{8,12},{12,8},{16,20},{20,16},{24,28},{28,24},{1,5},{5... | collective-permute-start | bytes 983048 | tf_op jit(solution)/shard_map/ppermute | solution.py:207
  56.1 33.5 %collective-permute-start.37 = (bf16[2,4,160,256]{3,2,1,0:T(8,128)(2,1)S(1)}, bf16[2,4,160,256]{3,2,1,0:T(8,128)(2,1)S(1)}, u32[]{:S(2)}, u32[]{:S(2)}) collective-permute-start(bf16[2,4,160,256]{3,2,1,0:T(8,128)(2,1)S(1)} %get-tuple-element.38), channel_id=1, source_target_pairs={{0,4},{4,0},{8,12},{12,8},{16,20},{20,16},{24,28},{28,24},{1,5},{5... | collective-permute-start | bytes 1966088 | tf_op jit(solution)/shard_map/ppermute | solution.py:207
  61.8 41.5 %collective-permute-start.36 = (bf16[4,160,256]{2,1,0:T(8,128)(2,1)S(1)}, bf16[4,160,256]{2,1,0:T(8,128)(2,1)S(1)}, u32[]{:S(2)}, u32[]{:S(2)}) collective-permute-start(bf16[4,160,256]{2,1,0:T(8,128)(2,1)S(1)} %get-tuple-element.37), channel_id=1, source_target_pairs={{0,4},{4,0},{8,12},{12,8},{16,20},{20,16},{24,28},{28,24},{1,5},{5... | collective-permute-start | bytes 983048 | tf_op jit(solution)/shard_map/ppermute | solution.py:207
  62.2 27.4 %collective-permute-start.40 = (bf16[2,160,256]{2,1,0:T(8,128)(2,1)S(1)}, bf16[2,160,256]{2,1,0:T(8,128)(2,1)S(1)}, u32[]{:S(2)}, u32[]{:S(2)}) collective-permute-start(bf16[2,160,256]{2,1,0:T(8,128)(2,1)S(1)} %get-tuple-element.48), channel_id=1, source_target_pairs={{0,8},{4,12},{8,0},{12,4},{16,24},{20,28},{24,16},{28,20},{1,9},{5... | collective-permute-start | bytes 491528 | tf_op jit(solution)/shard_map/ppermute | solution.py:207
  63.6 26.1 %collective-permute-start.43 = (bf16[2,160,256]{2,1,0:T(8,128)(2,1)S(1)}, bf16[2,160,256]{2,1,0:T(8,128)(2,1)S(1)}, u32[]{:S(2)}, u32[]{:S(2)}) collective-permute-start(bf16[2,160,256]{2,1,0:T(8,128)(2,1)S(1)} %get-tuple-element.49), channel_id=1, source_target_pairs={{0,16},{4,20},{8,24},{12,28},{16,0},{20,4},{24,8},{28,12},{1,17},{... | collective-permute-start | bytes 491528 | tf_op jit(solution)/shard_map/ppermute | solution.py:207
  79.0 14.7 %collective-permute-start.27 = (bf16[4,160,256]{2,1,0:T(8,128)(2,1)S(1)}, bf16[4,160,256]{2,1,0:T(8,128)(2,1)S(1)}, u32[]{:S(2)}, u32[]{:S(2)}) collective-permute-start(bf16[4,160,256]{2,1,0:T(8,128)(2,1)S(1)} %get-tuple-element.35), channel_id=1, source_target_pairs={{0,4},{4,0},{8,12},{12,8},{16,20},{20,16},{24,28},{28,24},{1,5},{5... | collective-permute-start | bytes 983048 | tf_op jit(solution)/shard_map/ppermute | solution.py:207
  89.7 7.1 %collective-permute-start.41 = (bf16[2,160,256]{2,1,0:T(8,128)(2,1)S(1)}, bf16[2,160,256]{2,1,0:T(8,128)(2,1)S(1)}, u32[]{:S(2)}, u32[]{:S(2)}) collective-permute-start(bf16[2,160,256]{2,1,0:T(8,128)(2,1)S(1)} %get-tuple-element.40), channel_id=1, source_target_pairs={{0,16},{4,20},{8,24},{12,28},{16,0},{20,4},{24,8},{28,12},{1,17},{... | collective-permute-start | bytes 491528 | tf_op jit(solution)/shard_map/ppermute | solution.py:207
  91.6 7.1 %collective-permute-start.38 = (bf16[2,160,256]{2,1,0:T(8,128)(2,1)S(1)}, bf16[2,160,256]{2,1,0:T(8,128)(2,1)S(1)}, u32[]{:S(2)}, u32[]{:S(2)}) collective-permute-start(bf16[2,160,256]{2,1,0:T(8,128)(2,1)S(1)} %get-tuple-element.42), channel_id=1, source_target_pairs={{0,8},{4,12},{8,0},{12,4},{16,24},{20,28},{24,16},{28,20},{1,9},{5... | collective-permute-start | bytes 491528 | tf_op jit(solution)/shard_map/ppermute | solution.py:207
  92.3 9.2 %collective-permute-start.44 = (bf16[2,160,256]{2,1,0:T(8,128)(2,1)S(1)}, bf16[2,160,256]{2,1,0:T(8,128)(2,1)S(1)}, u32[]{:S(2)}, u32[]{:S(2)}) collective-permute-start(bf16[2,160,256]{2,1,0:T(8,128)(2,1)S(1)} %get-tuple-element.41), channel_id=1, source_target_pairs={{0,8},{4,12},{8,0},{12,4},{16,24},{20,28},{24,16},{28,20},{1,9},{5... | collective-permute-start | bytes 491528 | tf_op jit(solution)/shard_map/ppermute | solution.py:207
  93.7 8.5 %collective-permute-start.42 = (bf16[2,160,256]{2,1,0:T(8,128)(2,1)S(1)}, bf16[2,160,256]{2,1,0:T(8,128)(2,1)S(1)}, u32[]{:S(2)}, u32[]{:S(2)}) collective-permute-start(bf16[2,160,256]{2,1,0:T(8,128)(2,1)S(1)} %get-tuple-element.43), channel_id=1, source_target_pairs={{0,16},{4,20},{8,24},{12,28},{16,0},{20,4},{24,8},{28,12},{1,17},{... | collective-permute-start | bytes 491528 | tf_op jit(solution)/shard_map/ppermute | solution.py:207
  96.8 14.9 %collective-permute-start.25 = (bf16[2,4,160,256]{3,2,1,0:T(8,128)(2,1)S(1)}, bf16[2,4,160,256]{3,2,1,0:T(8,128)(2,1)S(1)}, u32[]{:S(2)}, u32[]{:S(2)}) collective-permute-start(bf16[2,4,160,256]{3,2,1,0:T(8,128)(2,1)S(1)} %get-tuple-element.34), channel_id=1, source_target_pairs={{0,4},{4,0},{8,12},{12,8},{16,20},{20,16},{24,28},{28,24},{1,5},{5... | collective-permute-start | bytes 1966088 | tf_op jit(solution)/shard_map/ppermute | solution.py:207
  98.7 22.7 %collective-permute-start.24 = (bf16[4,160,256]{2,1,0:T(8,128)(2,1)S(1)}, bf16[4,160,256]{2,1,0:T(8,128)(2,1)S(1)}, u32[]{:S(2)}, u32[]{:S(2)}) collective-permute-start(bf16[4,160,256]{2,1,0:T(8,128)(2,1)S(1)} %get-tuple-element.33), channel_id=1, source_target_pairs={{0,4},{4,0},{8,12},{12,8},{16,20},{20,16},{24,28},{28,24},{1,5},{5... | collective-permute-start | bytes 983048 | tf_op jit(solution)/shard_map/ppermute | solution.py:207
  101.5 8.1 %collective-permute-start.28 = (bf16[2,160,256]{2,1,0:T(8,128)(2,1)S(1)}, bf16[2,160,256]{2,1,0:T(8,128)(2,1)S(1)}, u32[]{:S(2)}, u32[]{:S(2)}) collective-permute-start(bf16[2,160,256]{2,1,0:T(8,128)(2,1)S(1)} %get-tuple-element.50), channel_id=1, source_target_pairs={{0,8},{4,12},{8,0},{12,4},{16,24},{20,28},{24,16},{28,20},{1,9},{5... | collective-permute-start | bytes 491528 | tf_op jit(solution)/shard_map/ppermute | solution.py:207
  102.1 9.5 %collective-permute-start.31 = (bf16[2,160,256]{2,1,0:T(8,128)(2,1)S(1)}, bf16[2,160,256]{2,1,0:T(8,128)(2,1)S(1)}, u32[]{:S(2)}, u32[]{:S(2)}) collective-permute-start(bf16[2,160,256]{2,1,0:T(8,128)(2,1)S(1)} %get-tuple-element.51), channel_id=1, source_target_pairs={{0,16},{4,20},{8,24},{12,28},{16,0},{20,4},{24,8},{28,12},{1,17},{... | collective-permute-start | bytes 491528 | tf_op jit(solution)/shard_map/ppermute | solution.py:207
  107.9 6.8 %collective-permute-start.46 = (bf16[160,256]{1,0:T(8,128)(2,1)S(1)}, bf16[160,256]{1,0:T(8,128)(2,1)S(1)}, u32[]{:S(2)}, u32[]{:S(2)}) collective-permute-start(bf16[160,256]{1,0:T(8,128)(2,1)S(1)} %get-tuple-element.53), channel_id=1, source_target_pairs={{0,2},{1,3},{2,0},{3,1},{4,6},{5,7},{6,4},{7,5},{8,10},{9,11},{10,... | collective-permute-start | bytes 245768 | tf_op jit(solution)/shard_map/ppermute | solution.py:207
  109.6 6.4 %collective-permute-start.47 = (bf16[160,256]{1,0:T(8,128)(2,1)S(1)}, bf16[160,256]{1,0:T(8,128)(2,1)S(1)}, u32[]{:S(2)}, u32[]{:S(2)}) collective-permute-start(bf16[160,256]{1,0:T(8,128)(2,1)S(1)} %get-tuple-element.52), channel_id=1, source_target_pairs={{0,3},{1,2},{2,1},{3,0},{4,7},{5,6},{6,5},{7,4},{8,11},{9,10},{10,... | collective-permute-start | bytes 245768 | tf_op jit(solution)/shard_map/ppermute | solution.py:207
  111.7 6.9 %collective-permute-start.29 = (bf16[2,160,256]{2,1,0:T(8,128)(2,1)S(1)}, bf16[2,160,256]{2,1,0:T(8,128)(2,1)S(1)}, u32[]{:S(2)}, u32[]{:S(2)}) collective-permute-start(bf16[2,160,256]{2,1,0:T(8,128)(2,1)S(1)} %get-tuple-element.44), channel_id=1, source_target_pairs={{0,16},{4,20},{8,24},{12,28},{16,0},{20,4},{24,8},{28,12},{1,17},{... | collective-permute-start | bytes 491528 | tf_op jit(solution)/shard_map/ppermute | solution.py:207
  112.3 6.3 %collective-permute-start.26 = (bf16[2,160,256]{2,1,0:T(8,128)(2,1)S(1)}, bf16[2,160,256]{2,1,0:T(8,128)(2,1)S(1)}, u32[]{:S(2)}, u32[]{:S(2)}) collective-permute-start(bf16[2,160,256]{2,1,0:T(8,128)(2,1)S(1)} %get-tuple-element.46), channel_id=1, source_target_pairs={{0,8},{4,12},{8,0},{12,4},{16,24},{20,28},{24,16},{28,20},{1,9},{5... | collective-permute-start | bytes 491528 | tf_op jit(solution)/shard_map/ppermute | solution.py:207
  124.2 6.3 %collective-permute-start.35 = (bf16[160,256]{1,0:T(8,128)(2,1)S(1)}, bf16[160,256]{1,0:T(8,128)(2,1)S(1)}, u32[]{:S(2)}, u32[]{:S(2)}) collective-permute-start(bf16[160,256]{1,0:T(8,128)(2,1)S(1)} %get-tuple-element.55), channel_id=1, source_target_pairs={{0,3},{1,2},{2,1},{3,0},{4,7},{5,6},{6,5},{7,4},{8,11},{9,10},{10,... | collective-permute-start | bytes 245768 | tf_op jit(solution)/shard_map/ppermute | solution.py:207
  (24 other events, 172.3 us)

commit v3 on v0

--- a/solution.py
+++ b/solution.py
@@ -1,6 +1,10 @@
+import functools
+
 import jax
 import jax.numpy as jnp
 from jax import lax
+from jax.experimental import pallas as pl
+from jax.experimental.pallas import tpu as pltpu
 from jax.sharding import PartitionSpec as P
 
 HD = 128
@@ -71,7 +75,7 @@
     return (attended, query_grad, key_part, value_part)
 
 
-def shards(queries, key_rows, value_rows, out_grad, block_list):
+def sparse_plan(queries, key_rows, value_rows, out_grad, block_list):
     tokens_here = queries.shape[0]
     block_count = tokens_here // BLK
     shard_total = lax.axis_size("ctx")
@@ -192,7 +196,417 @@
     )
 
 
+LOG2E = 1.4426950408889634
+DENSE_SHARDS = 8
+VMEM_MIB = 12
+NT = (((1,), (1,)), ((), ()))
+TN = (((0,), (0,)), ((), ()))
+
+
+def swap(value, axis, mask):
+    count = lax.axis_size(axis)
+    return lax.ppermute(value, axis, [(i, i ^ mask) for i in range(count)])
+
+
+def rows_of(quarter, shard, spot, tokens, me_tp):
+    return pl.ds(pl.multiple_of(shard * tokens + (spot ^ me_tp) * quarter, 16), quarter)
+
+
+def place_pieces(piece_refs, pieces, tokens, me_tp, buffer):
+    for ref, (shards, first, spots) in zip(piece_refs, pieces):
+        for at in range(ref.shape[0]):
+            shard, spot = shards[at // spots], first + at % spots
+            buffer[rows_of(ref.shape[1], shard, spot, tokens, me_tp)] = ref[at]
+
+
+def write_sums(acc, out_refs, tokens, me_tp, scale):
+    near_ref, far_ref = out_refs
+    for k in range(near_ref.shape[0]):
+        for ref, shard in ((far_ref.at[k], 2 * k + 1), (near_ref.at[k], 2 * k)):
+            for spot in range(ref.shape[0]):
+                part = acc[rows_of(ref.shape[1], shard, spot, tokens, me_tp)]
+                if scale is not None:
+                    part = part * scale
+                ref[spot] = part.astype(ref.dtype)
+
+
+def block_of(place_ref, entry):
+    return pl.ds(pl.multiple_of(place_ref[entry] * BLK, BLK), BLK)
+
+
+def fold(value, op):
+    rows, width = value.shape
+    return op(value.reshape(rows // 8, 8, width), axis=0)
+
+
+def joined(op, total, value):
+    return value if total is None else op(total, value)
+
+
+class Shape:
+    def __init__(self, blocks, width, heads, group):
+        self.blocks, self.width, self.heads, self.group = blocks, width, heads, group
+
+    def rows(self, row):
+        return slice(row * BLK, (row + 1) * BLK)
+
+    def lanes(self, head):
+        return slice(head * HD, (head + 1) * HD)
+
+    def parts(self, head):
+        first = head * self.group
+        return [slice((first + g) * HD, (first + g + 1) * HD) for g in range(self.group)]
+
+    def wide(self, head):
+        return slice(head * self.group * HD, (head + 1) * self.group * HD)
+
+    def chunks(self):
+        return [(c, slice(c * BLK, (c + 1) * BLK)) for c in range(self.width)]
+
+    def entry(self, row, column):
+        return row * self.width + column
+
+    def stacked(self, ref, row, head):
+        return jnp.concatenate([ref[self.rows(row), part] for part in self.parts(head)], axis=0)
+
+    def flipped(self, ref, row, head):
+        return jnp.concatenate([ref[self.rows(row), part].T for part in self.parts(head)], axis=1)
+
+
+def exps_kernel(head, pieces, dims, tokens, place_ref, tp_ref, query_ref, grad_ref, *refs):
+    query, grad, score_ref, sems = refs[-4:]
+    query_copy = pltpu.make_async_copy(query_ref.at[:, dims.wide(head)], query, sems.at[0])
+    grad_copy = pltpu.make_async_copy(grad_ref.at[:, dims.wide(head)], grad, sems.at[1])
+    query_copy.start()
+    grad_copy.start()
+    if pieces:
+        count = len(pieces)
+        exp_ref, grad_t_ref, inv_ref, buffer = refs[count:-4]
+        place_pieces(refs[:count], pieces, tokens, tp_ref[0], buffer)
+    else:
+        buffer, exp_ref, grad_t_ref, inv_ref = refs[:-4]
+    query_copy.wait()
+    grad_copy.wait()
+    factor = LOG2E * float(HD) ** (-0.5)
+    lanes = dims.lanes(head)
+    tops = {}
+    for step in range(dims.blocks + 1):
+        first, second = step, step - 1
+        top_new = total = None
+        if first < dims.blocks:
+            stacked = dims.stacked(query, first, 0)
+        if 0 <= second:
+            top = jnp.max(tops[second], axis=0, keepdims=True) * factor
+        for column, chunk in dims.chunks():
+            if first < dims.blocks:
+                keys = buffer[block_of(place_ref, dims.entry(first, column)), lanes]
+                score = lax.dot_general(keys, stacked, NT, preferred_element_type=jnp.float32)
+                score_ref[first % 2, chunk] = score
+                top_new = joined(jnp.maximum, top_new, fold(score, jnp.max))
+            if 0 <= second:
+                weight = jnp.exp2(score_ref[second % 2, chunk] * factor - top)
+                exp_ref[second, chunk] = weight.astype(jnp.bfloat16)
+                total = joined(jnp.add, total, fold(weight, jnp.sum))
+        tops[first] = top_new
+        if 0 <= second:
+            inverse = 1.0 / jnp.sum(total, axis=0, keepdims=True)
+            inv_ref[second] = jnp.broadcast_to(inverse, inv_ref.shape[1:])
+            grad_t = dims.flipped(grad, second, 0).astype(jnp.float32)
+            grad_t_ref[second] = (grad_t * inverse).astype(jnp.bfloat16)
+
+
+def values_kernel(dims, tokens, place_ref, tp_ref, *refs):
+    exp_refs, grad_t_refs = refs[: dims.heads], refs[dims.heads : 2 * dims.heads]
+    out_refs, acc = refs[2 * dims.heads : -1], refs[-1]
+    acc[...] = jnp.zeros_like(acc)
+    for row in range(dims.blocks):
+        for head in range(dims.heads):
+            for column, chunk in dims.chunks():
+                acc[block_of(place_ref, dims.entry(row, column)), dims.lanes(head)] += (
+                    lax.dot_general(
+                        exp_refs[head][row, chunk],
+                        grad_t_refs[head][row],
+                        NT,
+                        preferred_element_type=jnp.float32,
+                    )
+                )
+    write_sums(acc, out_refs, tokens, tp_ref[0], None)
+
+
+def add_keys(acc, dims, place_ref, row, head, ds_ref, query):
+    stacked = dims.stacked(query, row, head)
+    for column, chunk in dims.chunks():
+        acc[block_of(place_ref, dims.entry(row, column)), dims.lanes(head)] += jnp.dot(
+            ds_ref[row, chunk], stacked, preferred_element_type=jnp.float32
+        )
+
+
+def score_rows(head, dims, place_ref, exp_ref, grad_t_ref, inv_ref, buffer, ds_ref, dprob_ref, then):
+    lanes = dims.lanes(head)
+    deltas = {}
+    for step in range(dims.blocks + 1):
+        first, second = step, step - 1
+        delta_new = None
+        if 0 <= second:
+            delta = jnp.sum(deltas[second], axis=0, keepdims=True) * inv_ref[second, 0:1]
+        for column, chunk in dims.chunks():
+            if first < dims.blocks:
+                values = buffer[block_of(place_ref, dims.entry(first, column)), lanes]
+                dprob = jnp.dot(values, grad_t_ref[first], preferred_element_type=jnp.float32)
+                dprob_ref[first % 2, chunk] = dprob
+                weight = exp_ref[first, chunk].astype(jnp.float32)
+                delta_new = joined(jnp.add, delta_new, fold(weight * dprob, jnp.sum))
+            if 0 <= second:
+                weight = exp_ref[second, chunk].astype(jnp.float32)
+                ds_ref[second, chunk] = (weight * (dprob_ref[second % 2, chunk] - delta)).astype(
+                    jnp.bfloat16
+                )
+        then(step - 1)
+        deltas[first] = delta_new
+
+
+def scores_kernel(head, pieces, dims, tokens, place_ref, tp_ref, exp_ref, grad_t_ref, inv_ref, *refs):
+    count = len(pieces)
+    ds_ref, buffer, flag_ref, dprob_ref = refs[count:]
+    flag_ref[...] = jnp.zeros_like(flag_ref)
+    place_pieces(refs[:count], pieces, tokens, tp_ref[0], buffer)
+    score_rows(head, dims, place_ref, exp_ref, grad_t_ref, inv_ref, buffer, ds_ref, dprob_ref, lambda row: None)
+
+
+def keys_kernel(dims, tokens, place_ref, tp_ref, exp_ref, grad_t_ref, inv_ref, buffer, *refs):
+    done_refs, query_ref = refs[: dims.heads - 1], refs[dims.heads - 1]
+    ds_ref, *out_refs, acc, dprob_ref, query, sem = refs[dims.heads :]
+    query_copy = pltpu.make_async_copy(query_ref, query, sem)
+    query_copy.start()
+    acc[...] = jnp.zeros_like(acc)
+    query_copy.wait()
+
+    def then(row):
+        if row < 0:
+            return
+        for head, done_ref in enumerate(done_refs):
+            add_keys(acc, dims, place_ref, row, head, done_ref, query)
+        add_keys(acc, dims, place_ref, row, dims.heads - 1, ds_ref, query)
+
+    score_rows(dims.heads - 1, dims, place_ref, exp_ref, grad_t_ref, inv_ref, buffer, ds_ref, dprob_ref, then)
+    write_sums(acc, out_refs, tokens, tp_ref[0], float(HD) ** (-0.5))
+
+
+def rows_kernel(dims, scale, place_ref, buffer_ref, *refs):
+    weight_refs, inv_refs = refs[: dims.heads], refs[dims.heads : -2]
+    out_ref, listed = refs[-2:]
+    for row in range(dims.blocks):
+        for head in range(dims.heads):
+            for column, chunk in dims.chunks():
+                block = block_of(place_ref, dims.entry(row, column))
+                listed[head, chunk] = buffer_ref[block, dims.lanes(head)]
+            result = lax.dot_general(
+                listed[head], weight_refs[head][row], TN, preferred_element_type=jnp.float32
+            )
+            if scale is None:
+                result = result * inv_refs[head][row, 0:1]
+            else:
+                result = result * scale
+            result = result.astype(jnp.bfloat16)
+            for g, part in enumerate(dims.parts(head)):
+                out_ref[dims.rows(row), part] = result[:, g * BLK : (g + 1) * BLK].T
+
+
+def to_head_groups(rows):
+    me = lax.axis_index("tp")
+    count = lax.axis_size("tp")
+    width = rows.shape[1] // count
+    parts = []
+    for mask in range(count):
+        part = lax.dynamic_slice_in_dim(rows, (me ^ mask) * width, width, 1)
+        parts.append(part if mask == 0 else swap(part, "tp", mask))
+    return jnp.stack(parts)
+
+
+def to_quarters(pieces):
+    me = lax.axis_index("tp")
+    count, quarter, width = pieces.shape
+    out = jnp.zeros((quarter, count * width), pieces.dtype)
+    for mask in range(count):
+        part = pieces[mask] if mask == 0 else swap(pieces[mask], "tp", mask)
+        out = lax.dynamic_update_slice(out, part, (0, (me ^ mask) * width))
+    return out
+
+
+def cut(*values):
+    return lax.optimization_barrier(values)
+
+
+def held_until(value, *others):
+    return lax.optimization_barrier((value, *others))[0]
+
+
+def with_near(own):
+    return swap(own, "ctx", 2), swap(own, "ctx", 4)
+
+
+def with_diagonal(along_half, across_half):
+    return swap(along_half, "ctx", 2), swap(across_half, "ctx", 4)
+
+
+def to_diagonal(near, got):
+    half = near.shape[1] // 2
+    to_x = jnp.stack([near[3, :half] + got[3, :half], near[1, :half] + got[1, :half]])
+    to_y = jnp.stack([near[3, half:] + got[3, half:], near[2, half:] + got[2, half:]])
+    return to_x, to_y
+
+
+def send_near(near, got, from_x, from_y):
+    half = near.shape[1] // 2
+    more_b = swap(near[1, half:] + got[1, half:] + from_y[0], "ctx", 2)
+    more_a = swap(near[2, :half] + got[2, :half] + from_x[0], "ctx", 4)
+    return more_a, more_b
+
+
+def total_own(near, got, from_x, from_y, more_a, more_b):
+    own = near[0] + got[0]
+    return own + jnp.concatenate([from_x[1] + more_a, from_y[1] + more_b], axis=0)
+
+
+def dense_plan(queries, key_rows, value_rows, out_grad, block_list):
+    tokens = queries.shape[0]
+    blocks = tokens // BLK
+    shard_total = lax.axis_size("ctx")
+    quarters = lax.axis_size("tp")
+    width = block_list.shape[1]
+    head_width = key_rows.shape[1] // quarters
+    heads = head_width // HD
+    group = queries.shape[1] // head_width
+    rows = shard_total * tokens
+    me_ctx = lax.axis_index("ctx")
+    me_tp = lax.axis_index("tp").reshape(1)
+    places = ((block_list // blocks) ^ me_ctx) * blocks + block_list % blocks
+    places = places.reshape(-1)
+    quarter = tokens // quarters
+    half = quarters // 2
+    pieces = [((shard,), 0, quarters) for shard in (0, 2, 4)]
+    pieces += [((6,), 0, half), ((6,), half, half), ((1, 3, 5), 0, quarters)]
+    pieces += [((7,), 0, half), ((7,), half, half)]
+    dims = Shape(blocks, width, heads, group)
+    list_len = width * BLK
+    query_rows = group * BLK
+    bf16 = jnp.bfloat16
+
+    in_vmem = pl.BlockSpec(memory_space=pltpu.VMEM)
+    in_smem = pl.BlockSpec(memory_space=pltpu.SMEM)
+    in_any = pl.BlockSpec(memory_space=pl.ANY)
+    shape = jax.ShapeDtypeStruct
+    sums = [shape((shard_total // 2, quarters, quarter, head_width), bf16)] * 2
+    stash = shape((blocks, list_len, query_rows), bf16)
+    grads = shape((blocks, HD, query_rows), bf16)
+    inverses = shape((blocks, 8, query_rows), jnp.float32)
+    ordered = shape((rows, head_width), bf16)
+    flat = shape(queries.shape, bf16)
+    flag = shape((8, HD), jnp.float32)
+    two_rows = pltpu.VMEM((2, list_len, query_rows), jnp.float32)
+    total = pltpu.VMEM((rows, head_width), jnp.float32)
+    listed = pltpu.VMEM((heads, list_len, HD), bf16)
+    wide = pltpu.VMEM((tokens, group * HD), bf16)
+    whole = pltpu.VMEM(queries.shape, bf16)
+    sem = pltpu.SemaphoreType.DMA
+
+    def call(name, kernel, outs, scratch, scalars, operands):
+        return pl.pallas_call(
+            kernel,
+            in_specs=[in_smem] * len(scalars) + [in_any if x is queries or x is out_grad else in_vmem for x in operands],
+            out_specs=[in_vmem] * len(outs),
+            out_shape=outs,
+            scratch_shapes=scratch,
+            compiler_params=pltpu.CompilerParams(vmem_limit_bytes=VMEM_MIB * 2**20),
+            cost_estimate=pl.CostEstimate(flops=2**32, bytes_accessed=2**20, transcendentals=0),
+            name=name,
+        )(*scalars, *operands)
+
+    key_own = to_head_groups(key_rows)
+    key_x, key_y = with_near(key_own)
+    value_own = to_head_groups(value_rows)
+    key_x, key_y, key_own, value_own = cut(key_x, key_y, key_own, value_own)
+    key_y1, key_x2, key_three = cut(
+        key_y[:half], key_x[half:], jnp.concatenate([key_own, key_x, key_y])
+    )
+    key_d1, key_d2 = with_diagonal(key_y1, key_x2)
+    key_d1, key_d2, key_three = cut(key_d1, key_d2, key_three)
+    keys = [key_own, key_x, key_y, key_d1, key_d2]
+    keys += [swap(part, "ctx", 1) for part in (key_three, key_d1, key_d2)]
+    value_x, value_y = with_near(held_until(value_own, key_d1))
+
+    rows_scratch = [wide, wide, two_rows, sem((2,))]
+    exp_0, grad_0, inverse_0, keys_in_order = call(
+        "exps_0", functools.partial(exps_kernel, 0, pieces, dims, tokens),
+        [stash, grads, inverses, ordered], rows_scratch, (places, me_tp), (queries, out_grad, *keys),
+    )
+    value_x, value_y, inverse_0 = cut(value_x, value_y, inverse_0)
+    value_y1, value_x2, value_three, places_1 = cut(
+        value_y[:half], value_x[half:], jnp.concatenate([value_own, value_x, value_y]), places
+    )
+    value_d1, value_d2 = with_diagonal(value_y1, value_x2)
+    value_far = swap(value_three, "ctx", 1)
+    exps, grad_ts, inverse = [exp_0], [grad_0], [inverse_0]
+    for head in range(1, heads):
+        made = call(
+            "exps", functools.partial(exps_kernel, head, [], dims, tokens),
+            [stash, grads, inverses], rows_scratch, (places_1, me_tp),
+            (queries, out_grad, keys_in_order),
+        )
+        for kept, new in zip((exps, grad_ts, inverse), made):
+            kept.append(new)
+    value_d1, value_d2, value_far, inverse[-1] = cut(value_d1, value_d2, value_far, inverse[-1])
+    values = [value_own, value_x, value_y, value_d1, value_d2, value_far]
+    values += [swap(part, "ctx", 1) for part in (value_d1, value_d2)]
+    value_near, value_away = call(
+        "value_sums", functools.partial(values_kernel, dims, tokens),
+        sums, [total], (held_until(places, inverse[-1]), me_tp), (*exps, *grad_ts),
+    )
+    value_near, value_away, places_2, *values[-2:] = cut(value_near, value_away, places, *values[-2:])
+    value_got = swap(value_away, "ctx", 1)
+    ds, token = [], None
+    for head in range(heads - 1):
+        made, values_in_order, token = call(
+            "scores", functools.partial(scores_kernel, head, pieces, dims, tokens),
+            [stash, ordered, flag], [two_rows], (places_2, me_tp),
+            (exps[head], grad_ts[head], inverse[head], *values),
+        )
+        ds.append(made)
+    value_got, token = cut(value_got, token)
+    to_x, to_y = to_diagonal(value_near, value_got)
+    to_x, to_y, places_3 = cut(to_x, to_y, held_until(places, token))
+    value_first = swap(to_x, "ctx", 2), swap(to_y, "ctx", 4)
+    made, key_near, key_away = call(
+        "key_sums", functools.partial(keys_kernel, dims, tokens),
+        [stash, *sums], [total, two_rows, whole, sem], (places_3, me_tp),
+        (exps[-1], grad_ts[-1], inverse[-1], values_in_order, *ds, queries),
+    )
+    ds.append(made)
+    key_near, key_away, places_4, *value_first = cut(key_near, key_away, places, *value_first)
+    key_got = swap(key_away, "ctx", 1)
+    value_more = send_near(value_near, value_got, *value_first)
+    [attended] = call(
+        "attended", functools.partial(rows_kernel, dims, None),
+        [flat], [listed], (places_4,), (values_in_order, *exps, *inverse),
+    )
+    key_got, attended, *value_more = cut(key_got, attended, *value_more)
+    value_sum = total_own(value_near, value_got, *value_first, *value_more)
+    to_x, to_y = to_diagonal(key_near, key_got)
+    to_x, to_y, places_5, value_sum = cut(to_x, to_y, places, value_sum)
+    key_first = swap(to_x, "ctx", 2), swap(to_y, "ctx", 4)
+    value_grad = to_quarters(value_sum)
+    [query_grad] = call(
+        "query_grad", functools.partial(rows_kernel, dims, float(HD) ** (-0.5)),
+        [flat], [listed], (places_5,), (keys_in_order, *ds),
+    )
+    query_grad, *key_first = cut(query_grad, *key_first)
+    key_more = send_near(key_near, key_got, *key_first)
+    key_sum = total_own(key_near, key_got, *key_first, *key_more)
+    return attended, query_grad, to_quarters(key_sum), value_grad
+
+
 def solution(mesh):
+    dense = mesh.shape["ctx"] == DENSE_SHARDS and mesh.shape["tp"] % 4 == 0
     in_specs = (
         P("ctx", "tp"),
         P(("ctx", "tp"), None),
@@ -201,4 +615,10 @@
         P("ctx", None),
     )
     out_specs = (P("ctx", "tp"), P("ctx", "tp"), P(("ctx", "tp"), None), P(("ctx", "tp"), None))
-    return jax.shard_map(shards, mesh=mesh, in_specs=in_specs, out_specs=out_specs, check_vma=False)
+    return jax.shard_map(
+        dense_plan if dense else sparse_plan,
+        mesh=mesh,
+        in_specs=in_specs,
+        out_specs=out_specs,
+        check_vma=False,
+    )

time: 403 us -> 108 us (0.27)
  local copies, waits for them, and re-layouts: 139 us -> 3.5 us
  waiting for transfers between devices: 111 us -> 32.8 us
  matrix products: 63.8 us -> 0 us
  Pallas kernels: 0 us -> 34.2 us
  other arithmetic: 22.5 us -> 1.88 us
  between operations: 19.5 us -> 1.07 us
  blocking collectives: 13.8 us -> 0 us
  starting transfers between devices: 30.5 us -> 34.6 us
    psum x2 -> x0, waiting for transfers between devices: 66.9 us -> none  [the longest x1 46.1 us: spread(): return lax.psum(jnp.where(mine, x, jnp.zeros_like(x)), axis)]
    dot_general x32 -> x0, matrix products: 63.8 us -> none  [the longest x5 20.6 us: attend_block(): jnp.einsum('kgqn,qkgd->nkd', weights_low, grad_tile, preferred_element_ty...]
    reshape x9 -> x1, local copies, waits for them, and re-layouts: 35.2 us -> 0.08 us  [dense_plan(): places = places.reshape(-1)]
    pallas_call x0 -> x7, Pallas kernels: none -> 34.2 us  [call(): pl.pallas_call(kernel, in_specs=[in_smem] * len(scalars) + [in_any if x i...]
    ppermute x4 -> x36, starting transfers between devices: 5.45 us -> 34.6 us  [swap(): return lax.ppermute(value, axis, [(i, i ^ mask) for i in range(count)])]
    dynamic_slice x30 -> x0, local copies, waits for them, and re-layouts: 27.7 us -> none  [shards(): lax.map(attend_block, (query_tiles, grad_tiles, keys_here, values_here))]
    all_to_all x6 -> x0, starting transfers between devices: 24.9 us -> none  [the longest x1 5.17 us: shards(): lax.all_to_all(wanted.reshape(shard_total, capacity), 'ctx', split_axis=0...]
    all_to_all x6 -> x0, waiting for transfers between devices: 22.3 us -> none  [the longest x1 8.58 us: shards(): lax.all_to_all(key_rows, 'tp', split_axis=1, concat_axis=0, tiled=True)]
  transfers between devices with their start and end apart: 12 -> 36, of which waited for: 7 -> 20; matrix products, arithmetic and copies ran while one was open for 12% -> 0% of each run, Pallas kernels for 0% -> 32%
where the time goes in v3:
time: 108 us
  starting transfers between devices  34.6 us (32%)
  Pallas kernels  34.2 us (32%)
  waiting for transfers between devices  32.8 us (30%)
  local copies, waits for them, and re-layouts  3.5 us (3%)
  other arithmetic  1.88 us (2%)
    ppermute x36, starting transfers between devices, swap(): return lax.ppermute(value, axis, [(i, i ^ mask) for i in range(count)])  34.6 us
    pallas_call x7, Pallas kernels, call(): pl.pallas_call(kernel, in_specs=[in_smem] * len(scalars) + [in_any if x i...  34.2 us
    ppermute x36, waiting for transfers between devices, swap(): return lax.ppermute(value, axis, [(i, i ^ mask) for i in range(count)])  32.8 us
  transfers between devices with their start and end apart: 36, of which 20 were waited for; matrix products, arithmetic and copies ran while one was open for 0% of the time, Pallas kernels for 32%

profile of v3, /device:TPU:0, one launch (start us, length us, event | category | flops | bytes accessed | tf_op | source)
XLA Modules:
  0.0 108.1 jit_solution(17711006372576917049)
XLA Ops:
  1.8 5.1 %collective-permute-start.2 = (bf16[160,256]{1,0:T(8,128)(2,1)S(1)}, bf16[160,256]{1,0:T(8,128)(2,1)S(1)}, u32[]{:S(2)}, u32[]{:S(2)}) collective-permute-start(bf16[160,256]{1,0:T(8,128)(2,1)S(1)} %get-tuple-element.150), channel_id=1, source_target_pairs={{0,3},{1,2},{2,1},{3,0},{4,7},{5,6},{6,5},{7,4},{8,11},{9,10},{10,... | collective-permute-start | bytes 245768 | tf_op jit(solution)/shard_map/ppermute | solution.py:208
  7.5 2.4 %collective-permute-done.2 = bf16[160,256]{1,0:T(8,128)(2,1)S(1)} collective-permute-done((bf16[160,256]{1,0:T(8,128)(2,1)S(1)}, bf16[160,256]{1,0:T(8,128)(2,1)S(1)}, u32[]{:S(2)}, u32[]{:S(2)}) %collective-permute-start.2) | collective-permute-done | bytes 81952 | tf_op jit(solution)/shard_map/ppermute | solution.py:208
  9.9 3.8 %collective-permute-done.1 = bf16[160,256]{1,0:T(8,128)(2,1)S(1)} collective-permute-done((bf16[160,256]{1,0:T(8,128)(2,1)S(1)}, bf16[160,256]{1,0:T(8,128)(2,1)S(1)}, u32[]{:S(2)}, u32[]{:S(2)}) %collective-permute-start.1) | collective-permute-done | bytes 81952 | tf_op jit(solution)/shard_map/ppermute | solution.py:208
  13.8 1.6 %collective-permute-start.3 = (bf16[4,160,256]{2,1,0:T(8,128)(2,1)S(1)}, bf16[4,160,256]{2,1,0:T(8,128)(2,1)S(1)}, u32[]{:S(2)}, u32[]{:S(2)}) collective-permute-start(bf16[4,160,256]{2,1,0:T(8,128)(2,1)S(1)} %pad_maximum_fusion.2.refs_0_), channel_id=1, source_target_pairs={{0,8},{4,12},{8,0},{12,4},{16,24},{20,28},{24,16},{28,20},{1,9},{5... | collective-permute-start | bytes 983048 | tf_op jit(solution)/shard_map/ppermute | solution.py:208
  15.3 1.5 %collective-permute-start.4 = (bf16[4,160,256]{2,1,0:T(8,128)(2,1)S(1)}, bf16[4,160,256]{2,1,0:T(8,128)(2,1)S(1)}, u32[]{:S(2)}, u32[]{:S(2)}) collective-permute-start(bf16[4,160,256]{2,1,0:T(8,128)(2,1)S(1)} %pad_maximum_fusion.2.refs_0_), channel_id=1, source_target_pairs={{0,16},{4,20},{8,24},{12,28},{16,0},{20,4},{24,8},{28,12},{1,17},{... | collective-permute-start | bytes 983048 | tf_op jit(solution)/shard_map/ppermute | solution.py:208
  16.9 2.8 %collective-permute-start.7 = (bf16[160,256]{1,0:T(8,128)(2,1)S(1)}, bf16[160,256]{1,0:T(8,128)(2,1)S(1)}, u32[]{:S(2)}, u32[]{:S(2)}) collective-permute-start(bf16[160,256]{1,0:T(8,128)(2,1)S(1)} %get-tuple-element.146), channel_id=1, source_target_pairs={{0,3},{1,2},{2,1},{3,0},{4,7},{5,6},{6,5},{7,4},{8,11},{9,10},{10,... | collective-permute-start | bytes 245768 | tf_op jit(solution)/shard_map/ppermute | solution.py:208
  19.7 1.7 %collective-permute-start.5 = (bf16[160,256]{1,0:T(8,128)(2,1)S(1)}, bf16[160,256]{1,0:T(8,128)(2,1)S(1)}, u32[]{:S(2)}, u32[]{:S(2)}) collective-permute-start(bf16[160,256]{1,0:T(8,128)(2,1)S(1)} %get-tuple-element.145), channel_id=1, source_target_pairs={{0,1},{1,0},{2,3},{3,2},{4,5},{5,4},{6,7},{7,6},{8,9},{9,8},{10,11... | collective-permute-start | bytes 245768 | tf_op jit(solution)/shard_map/ppermute | solution.py:208
  21.4 2.6 %collective-permute-done.7 = bf16[160,256]{1,0:T(8,128)(2,1)S(1)} collective-permute-done((bf16[160,256]{1,0:T(8,128)(2,1)S(1)}, bf16[160,256]{1,0:T(8,128)(2,1)S(1)}, u32[]{:S(2)}, u32[]{:S(2)}) %collective-permute-start.7) | collective-permute-done | bytes 81952 | tf_op jit(solution)/shard_map/ppermute | solution.py:208
  23.9 2.5 %collective-permute-done.6 = bf16[160,256]{1,0:T(8,128)(2,1)S(1)} collective-permute-done((bf16[160,256]{1,0:T(8,128)(2,1)S(1)}, bf16[160,256]{1,0:T(8,128)(2,1)S(1)}, u32[]{:S(2)}, u32[]{:S(2)}) %collective-permute-start.6) | collective-permute-done | bytes 81952 | tf_op jit(solution)/shard_map/ppermute | solution.py:208
  28.5 4.4 %collective-permute-done.8.refs_3_ = bf16[2,160,256]{2,1,0:T(8,128)(2,1)S(1)} collective-permute-done((bf16[2,160,256]{2,1,0:T(8,128)(2,1)S(1)}, bf16[2,160,256]{2,1,0:T(8,128)(2,1)S(1)}, u32[]{:S(2)}, u32[]{:S(2)}) %collective-permute-start.8) | collective-permute-done | bytes 163872 | tf_op jit(solution)/shard_map/ppermute | solution.py:208
  34.1 1.5 %collective-permute-start.10 = (bf16[4,160,256]{2,1,0:T(8,128)(2,1)S(1)}, bf16[4,160,256]{2,1,0:T(8,128)(2,1)S(1)}, u32[]{:S(2)}, u32[]{:S(2)}) collective-permute-start(bf16[4,160,256]{2,1,0:T(8,128)(2,1)S(1)} %pad_maximum_fusion.3.refs_0_), channel_id=1, source_target_pairs={{0,8},{4,12},{8,0},{12,4},{16,24},{20,28},{24,16},{28,20},{1,9},{5... | collective-permute-start | bytes 983048 | tf_op jit(solution)/shard_map/ppermute | solution.py:208
  36.6 1.3 %copy-done.1 = bf16[640,1024]{1,0:T(8,128)(2,1)S(1)} copy-done((bf16[640,1024]{1,0:T(8,128)(2,1)S(1)}, bf16[640,1024]{1,0:T(8,128)(2,1)}, u32[]{:S(2)}) %copy-start.1) | copy-done | bytes 1310744
  37.9 5.3 %exps_0.1 = (bf16[5,1024,512]{2,1,0:T(8,128)(2,1)S(1)}, bf16[5,128,512]{2,1,0:T(8,128)(2,1)S(1)}, f32[5,8,512]{2,1,0:T(8,128)S(1)}, bf16[5120,256]{1,0:T(8,128)(2,1)S(1)}) custom-call(s32[40]{0:T(128)S(1)} %reshape.24.place_ref, s32[1]{0:T(128)} %bitcast.8.tp_ref, bf16[640,1024]{1,0:T(8,128)(2,1)S(1)} %copy-done.1, bf16[640,1024]{1,0:T(8,128)(2,1)S(1)} %copy-done, ...), custom_call_target="tpu_custom_call" | custom-call | flops 4294967296 | bytes 1048576 | tf_op jit(solution)/shard_map/exps_0/pallas_call | solution.py:514
  44.2 1.2 %collective-permute-done.11.refs_2_ = bf16[4,160,256]{2,1,0:T(8,128)(2,1)S(1)} collective-permute-done((bf16[4,160,256]{2,1,0:T(8,128)(2,1)S(1)}, bf16[4,160,256]{2,1,0:T(8,128)(2,1)S(1)}, u32[]{:S(2)}, u32[]{:S(2)}) %collective-permute-start.11) | collective-permute-done | bytes 327712 | tf_op jit(solution)/shard_map/ppermute | solution.py:208
  46.6 4.6 %exps.1 = (bf16[5,1024,512]{2,1,0:T(8,128)(2,1)S(1)}, bf16[5,128,512]{2,1,0:T(8,128)(2,1)S(1)}, f32[5,8,512]{2,1,0:T(8,128)S(1)}) custom-call(s32[40]{0:T(128)S(1)} %reshape.24.place_ref, s32[1]{0:T(128)} %bitcast.8.tp_ref, bf16[640,1024]{1,0:T(8,128)(2,1)S(1)} %copy-done.1, bf16[640,1024]{1,0:T(8,128)(2,1)S(1)} %copy-done, ...), custom_call_target="tpu_custom_call" | custom-call | flops 4294967296 | bytes 1048576 | tf_op jit(solution)/shard_map/exps/pallas_call | solution.py:514
  53.0 4.0 %value_sums.1 = (bf16[4,4,160,256]{3,2,1,0:T(8,128)(2,1)S(1)}, bf16[4,4,160,256]{3,2,1,0:T(8,128)(2,1)S(1)}) custom-call(s32[40]{0:T(128)S(1)} %reshape.24.place_ref, s32[1]{0:T(128)} %bitcast.8.tp_ref, bf16[5,1024,512]{2,1,0:T(8,128)(2,1)S(1)} %get-tuple-element.87.refs_0_.exp_ref, bf16[5,1024,512]{2,1,0:T(8,128)(2,1)S(1)} %get-tuple-element.88.refs_1_.exp_ref, ...), custom_call_target="tpu_custom_call" | custom-call | flops 4294967296 | bytes 1048576 | tf_op jit(solution)/shard_map/value_sums/pallas_call | solution.py:514
  57.1 4.9 %scores.1 = (bf16[5,1024,512]{2,1,0:T(8,128)(2,1)S(1)}, bf16[5120,256]{1,0:T(8,128)(2,1)S(1)}, f32[8,128]{1,0:T(8,128)}) custom-call(s32[40]{0:T(128)S(1)} %reshape.24.place_ref, s32[1]{0:T(128)} %bitcast.8.tp_ref, bf16[5,1024,512]{2,1,0:T(8,128)(2,1)S(1)} %get-tuple-element.87.refs_0_.exp_ref, ...), custom_call_target="tpu_custom_call" | custom-call | flops 4294967296 | bytes 1048576 | tf_op jit(solution)/shard_map/scores/pallas_call | solution.py:514
  62.2 1.6 %collective-permute-start.21 = (bf16[2,2,160,256]{3,2,1,0:T(8,128)(2,1)S(1)}, bf16[2,2,160,256]{3,2,1,0:T(8,128)(2,1)S(1)}, u32[]{:S(2)}, u32[]{:S(2)}) collective-permute-start(bf16[2,2,160,256]{3,2,1,0:T(8,128)(2,1)S(1)} %get-tuple-element.107), channel_id=1, source_target_pairs={{0,8},{4,12},{8,0},{12,4},{16,24},{20,28},{24,16},{28,20},{1,9},{5... | collective-permute-start | bytes 983048 | tf_op jit(solution)/shard_map/ppermute | solution.py:208
  64.3 7.8 %key_sums.1 = (bf16[5,1024,512]{2,1,0:T(8,128)(2,1)S(1)}, bf16[4,4,160,256]{3,2,1,0:T(8,128)(2,1)S(1)}, bf16[4,4,160,256]{3,2,1,0:T(8,128)(2,1)S(1)}) custom-call(s32[40]{0:T(128)S(1)} %reshape.24.place_ref, s32[1]{0:T(128)} %bitcast.8.tp_ref, bf16[5,1024,512]{2,1,0:T(8,128)(2,1)S(1)} %get-tuple-element.88.refs_1_.exp_ref, ...), custom_call_target="tpu_custom_call" | custom-call | flops 4294967296 | bytes 1048576 | tf_op jit(solution)/shard_map/key_sums/pallas_call | solution.py:514
  74.7 3.8 %attended.1 = bf16[640,1024]{1,0:T(8,128)(2,1)} custom-call(s32[40]{0:T(128)S(1)} %reshape.24.place_ref, bf16[5120,256]{1,0:T(8,128)(2,1)S(1)} %get-tuple-element.103.buffer.buffer_ref, bf16[5,1024,512]{2,1,0:T(8,128)(2,1)S(1)} %get-tuple-element.87.refs_0_.exp_ref, bf16[5,1024,512]{2,1,0:T(8,128)(2,1)S(1)} %get-tuple-element.88.refs_1_.exp_ref, ...), custom_call_target="tpu_custom_call" | custom-call | flops 4294967296 | bytes 1048576 | tf_op jit(solution)/shard_map/attended/pallas_call | solution.py:514
  78.5 1.8 %collective-permute-done.24 = bf16[2,160,256]{2,1,0:T(8,128)(2,1)S(1)} collective-permute-done((bf16[2,160,256]{2,1,0:T(8,128)(2,1)S(1)}, bf16[2,160,256]{2,1,0:T(8,128)(2,1)S(1)}, u32[]{:S(2)}, u32[]{:S(2)}) %collective-permute-start.24) | collective-permute-done | bytes 163872 | tf_op jit(solution)/shard_map/ppermute | solution.py:208
  81.4 1.6 %collective-permute-start.27 = (bf16[2,2,160,256]{3,2,1,0:T(8,128)(2,1)S(1)}, bf16[2,2,160,256]{3,2,1,0:T(8,128)(2,1)S(1)}, u32[]{:S(2)}, u32[]{:S(2)}) collective-permute-start(bf16[2,2,160,256]{3,2,1,0:T(8,128)(2,1)S(1)} %pad_maximum_fusion.7), channel_id=1, source_target_pairs={{0,16},{4,20},{8,24},{12,28},{16,0},{20,4},{24,8},{28,12},{1,17},{... | collective-permute-start | bytes 983048 | tf_op jit(solution)/shard_map/ppermute | solution.py:208
  83.0 2.4 %collective-permute-start.34 = (bf16[160,256]{1,0:T(8,128)(2,1)S(1)}, bf16[160,256]{1,0:T(8,128)(2,1)S(1)}, u32[]{:S(2)}, u32[]{:S(2)}) collective-permute-start(bf16[160,256]{1,0:T(8,128)(2,1)S(1)} %get-tuple-element.139), channel_id=1, source_target_pairs={{0,2},{1,3},{2,0},{3,1},{4,6},{5,7},{6,4},{7,5},{8,10},{9,11},{10,... | collective-permute-start | bytes 245768 | tf_op jit(solution)/shard_map/ppermute | solution.py:208
  85.5 2.0 %collective-permute-start.35 = (bf16[160,256]{1,0:T(8,128)(2,1)S(1)}, bf16[160,256]{1,0:T(8,128)(2,1)S(1)}, u32[]{:S(2)}, u32[]{:S(2)}) collective-permute-start(bf16[160,256]{1,0:T(8,128)(2,1)S(1)} %get-tuple-element.138), channel_id=1, source_target_pairs={{0,3},{1,2},{2,1},{3,0},{4,7},{5,6},{6,5},{7,4},{8,11},{9,10},{10,... | collective-permute-start | bytes 245768 | tf_op jit(solution)/shard_map/ppermute | solution.py:208
  87.4 3.8 %query_grad.1 = bf16[640,1024]{1,0:T(8,128)(2,1)} custom-call(s32[40]{0:T(128)S(1)} %reshape.24.place_ref, bf16[5120,256]{1,0:T(8,128)(2,1)S(1)} %get-tuple-element.83.refs_0_.buffer_ref, bf16[5,1024,512]{2,1,0:T(8,128)(2,1)S(1)} %get-tuple-element.104.refs_0_, bf16[5,1024,512]{2,1,0:T(8,128)(2,1)S(1)} %get-tuple-element.119.refs_1_), custom_call_target="tpu_custom_call" | custom-call | flops 4294967296 | bytes 1048576 | tf_op jit(solution)/shard_map/query_grad/pallas_call | solution.py:514
  91.4 1.6 %collective-permute-start.29 = (bf16[2,160,256]{2,1,0:T(8,128)(2,1)S(1)}, bf16[2,160,256]{2,1,0:T(8,128)(2,1)S(1)}, u32[]{:S(2)}, u32[]{:S(2)}) collective-permute-start(bf16[2,160,256]{2,1,0:T(8,128)(2,1)S(1)} %get-tuple-element.127), channel_id=1, source_target_pairs={{0,8},{4,12},{8,0},{12,4},{16,24},{20,28},{24,16},{28,20},{1,9},{5... | collective-permute-start | bytes 491528 | tf_op jit(solution)/shard_map/ppermute | solution.py:208
  93.6 3.2 %collective-permute-done.29 = bf16[2,160,256]{2,1,0:T(8,128)(2,1)S(1)} collective-permute-done((bf16[2,160,256]{2,1,0:T(8,128)(2,1)S(1)}, bf16[2,160,256]{2,1,0:T(8,128)(2,1)S(1)}, u32[]{:S(2)}, u32[]{:S(2)}) %collective-permute-start.29) | collective-permute-done | bytes 163872 | tf_op jit(solution)/shard_map/ppermute | solution.py:208
  96.8 1.6 %collective-permute-done.28 = bf16[2,160,256]{2,1,0:T(8,128)(2,1)S(1)} collective-permute-done((bf16[2,160,256]{2,1,0:T(8,128)(2,1)S(1)}, bf16[2,160,256]{2,1,0:T(8,128)(2,1)S(1)}, u32[]{:S(2)}, u32[]{:S(2)}) %collective-permute-start.28) | collective-permute-done | bytes 163872 | tf_op jit(solution)/shard_map/ppermute | solution.py:208
  98.7 2.5 %collective-permute-start.31 = (bf16[160,256]{1,0:T(8,128)(2,1)S(1)}, bf16[160,256]{1,0:T(8,128)(2,1)S(1)}, u32[]{:S(2)}, u32[]{:S(2)}) collective-permute-start(bf16[160,256]{1,0:T(8,128)(2,1)S(1)} %get-tuple-element.142), channel_id=1, source_target_pairs={{0,2},{1,3},{2,0},{3,1},{4,6},{5,7},{6,4},{7,5},{8,10},{9,11},{10,... | collective-permute-start | bytes 245768 | tf_op jit(solution)/shard_map/ppermute | solution.py:208
  101.2 1.9 %collective-permute-start.32 = (bf16[160,256]{1,0:T(8,128)(2,1)S(1)}, bf16[160,256]{1,0:T(8,128)(2,1)S(1)}, u32[]{:S(2)}, u32[]{:S(2)}) collective-permute-start(bf16[160,256]{1,0:T(8,128)(2,1)S(1)} %get-tuple-element.141), channel_id=1, source_target_pairs={{0,3},{1,2},{2,1},{3,0},{4,7},{5,6},{6,5},{7,4},{8,11},{9,10},{10,... | collective-permute-start | bytes 245768 | tf_op jit(solution)/shard_map/ppermute | solution.py:208
  103.1 1.5 %collective-permute-done.30 = bf16[160,256]{1,0:T(8,128)(2,1)S(1)} collective-permute-done((bf16[160,256]{1,0:T(8,128)(2,1)S(1)}, bf16[160,256]{1,0:T(8,128)(2,1)S(1)}, u32[]{:S(2)}, u32[]{:S(2)}) %collective-permute-start.30) | collective-permute-done | bytes 81952 | tf_op jit(solution)/shard_map/ppermute | solution.py:208
  104.6 2.8 %collective-permute-done.32 = bf16[160,256]{1,0:T(8,128)(2,1)S(1)} collective-permute-done((bf16[160,256]{1,0:T(8,128)(2,1)S(1)}, bf16[160,256]{1,0:T(8,128)(2,1)S(1)}, u32[]{:S(2)}, u32[]{:S(2)}) %collective-permute-start.32) | collective-permute-done | bytes 81952 | tf_op jit(solution)/shard_map/ppermute | solution.py:208
  (98 shorter events, 16.3 us)
Async XLA Ops:
  1.8 8.1 %collective-permute-start.2 = (bf16[160,256]{1,0:T(8,128)(2,1)S(1)}, bf16[160,256]{1,0:T(8,128)(2,1)S(1)}, u32[]{:S(2)}, u32[]{:S(2)}) collective-permute-start(bf16[160,256]{1,0:T(8,128)(2,1)S(1)} %get-tuple-element.150), channel_id=1, source_target_pairs={{0,3},{1,2},{2,1},{3,0},{4,7},{5,6},{6,5},{7,4},{8,11},{9,10},{10,... | collective-permute-start | bytes 245768 | tf_op jit(solution)/shard_map/ppermute | solution.py:208
  6.9 6.9 %collective-permute-start.1 = (bf16[160,256]{1,0:T(8,128)(2,1)S(1)}, bf16[160,256]{1,0:T(8,128)(2,1)S(1)}, u32[]{:S(2)}, u32[]{:S(2)}) collective-permute-start(bf16[160,256]{1,0:T(8,128)(2,1)S(1)} %get-tuple-element.151), channel_id=1, source_target_pairs={{0,2},{1,3},{2,0},{3,1},{4,6},{5,7},{6,4},{7,5},{8,10},{9,11},{10,... | collective-permute-start | bytes 245768 | tf_op jit(solution)/shard_map/ppermute | solution.py:208
  6.9 6.9 %collective-permute-start = (bf16[160,256]{1,0:T(8,128)(2,1)S(1)}, bf16[160,256]{1,0:T(8,128)(2,1)S(1)}, u32[]{:S(2)}, u32[]{:S(2)}) collective-permute-start(bf16[160,256]{1,0:T(8,128)(2,1)S(1)} %get-tuple-element.149), channel_id=1, source_target_pairs={{0,1},{1,0},{2,3},{3,2},{4,5},{5,4},{6,7},{7,6},{8,9},{9,8},{10,11... | collective-permute-start | bytes 245768 | tf_op jit(solution)/shard_map/ppermute | solution.py:208
  13.8 12.7 %collective-permute-start.3 = (bf16[4,160,256]{2,1,0:T(8,128)(2,1)S(1)}, bf16[4,160,256]{2,1,0:T(8,128)(2,1)S(1)}, u32[]{:S(2)}, u32[]{:S(2)}) collective-permute-start(bf16[4,160,256]{2,1,0:T(8,128)(2,1)S(1)} %pad_maximum_fusion.2.refs_0_), channel_id=1, source_target_pairs={{0,8},{4,12},{8,0},{12,4},{16,24},{20,28},{24,16},{28,20},{1,9},{5... | collective-permute-start | bytes 983048 | tf_op jit(solution)/shard_map/ppermute | solution.py:208
  15.3 11.2 %collective-permute-start.4 = (bf16[4,160,256]{2,1,0:T(8,128)(2,1)S(1)}, bf16[4,160,256]{2,1,0:T(8,128)(2,1)S(1)}, u32[]{:S(2)}, u32[]{:S(2)}) collective-permute-start(bf16[4,160,256]{2,1,0:T(8,128)(2,1)S(1)} %pad_maximum_fusion.2.refs_0_), channel_id=1, source_target_pairs={{0,16},{4,20},{8,24},{12,28},{16,0},{20,4},{24,8},{28,12},{1,17},{... | collective-permute-start | bytes 983048 | tf_op jit(solution)/shard_map/ppermute | solution.py:208
  16.9 7.0 %collective-permute-start.7 = (bf16[160,256]{1,0:T(8,128)(2,1)S(1)}, bf16[160,256]{1,0:T(8,128)(2,1)S(1)}, u32[]{:S(2)}, u32[]{:S(2)}) collective-permute-start(bf16[160,256]{1,0:T(8,128)(2,1)S(1)} %get-tuple-element.146), channel_id=1, source_target_pairs={{0,3},{1,2},{2,1},{3,0},{4,7},{5,6},{6,5},{7,4},{8,11},{9,10},{10,... | collective-permute-start | bytes 245768 | tf_op jit(solution)/shard_map/ppermute | solution.py:208
  19.7 6.7 %collective-permute-start.6 = (bf16[160,256]{1,0:T(8,128)(2,1)S(1)}, bf16[160,256]{1,0:T(8,128)(2,1)S(1)}, u32[]{:S(2)}, u32[]{:S(2)}) collective-permute-start(bf16[160,256]{1,0:T(8,128)(2,1)S(1)} %get-tuple-element.147), channel_id=1, source_target_pairs={{0,2},{1,3},{2,0},{3,1},{4,6},{5,7},{6,4},{7,5},{8,10},{9,11},{10,... | collective-permute-start | bytes 245768 | tf_op jit(solution)/shard_map/ppermute | solution.py:208
  19.7 6.7 %collective-permute-start.5 = (bf16[160,256]{1,0:T(8,128)(2,1)S(1)}, bf16[160,256]{1,0:T(8,128)(2,1)S(1)}, u32[]{:S(2)}, u32[]{:S(2)}) collective-permute-start(bf16[160,256]{1,0:T(8,128)(2,1)S(1)} %get-tuple-element.145), channel_id=1, source_target_pairs={{0,1},{1,0},{2,3},{3,2},{4,5},{5,4},{6,7},{7,6},{8,9},{9,8},{10,11... | collective-permute-start | bytes 245768 | tf_op jit(solution)/shard_map/ppermute | solution.py:208
  27.6 5.3 %collective-permute-start.8 = (bf16[2,160,256]{2,1,0:T(8,128)(2,1)S(1)}, bf16[2,160,256]{2,1,0:T(8,128)(2,1)S(1)}, u32[]{:S(2)}, u32[]{:S(2)}) collective-permute-start(bf16[2,160,256]{2,1,0:T(8,128)(2,1)S(1)} %slice.144), channel_id=1, source_target_pairs={{0,8},{4,12},{8,0},{12,4},{16,24},{20,28},{24,16},{28,20},{1,9},{5... | collective-permute-start | bytes 491528 | tf_op jit(solution)/shard_map/ppermute | solution.py:208
  28.1 5.3 %collective-permute-start.9 = (bf16[2,160,256]{2,1,0:T(8,128)(2,1)S(1)}, bf16[2,160,256]{2,1,0:T(8,128)(2,1)S(1)}, u32[]{:S(2)}, u32[]{:S(2)}) collective-permute-start(bf16[2,160,256]{2,1,0:T(8,128)(2,1)S(1)} %slice.145), channel_id=1, source_target_pairs={{0,16},{4,20},{8,24},{12,28},{16,0},{20,4},{24,8},{28,12},{1,17},{... | collective-permute-start | bytes 491528 | tf_op jit(solution)/shard_map/ppermute | solution.py:208
  34.1 10.1 %collective-permute-start.10 = (bf16[4,160,256]{2,1,0:T(8,128)(2,1)S(1)}, bf16[4,160,256]{2,1,0:T(8,128)(2,1)S(1)}, u32[]{:S(2)}, u32[]{:S(2)}) collective-permute-start(bf16[4,160,256]{2,1,0:T(8,128)(2,1)S(1)} %pad_maximum_fusion.3.refs_0_), channel_id=1, source_target_pairs={{0,8},{4,12},{8,0},{12,4},{16,24},{20,28},{24,16},{28,20},{1,9},{5... | collective-permute-start | bytes 983048 | tf_op jit(solution)/shard_map/ppermute | solution.py:208
  35.6 9.8 %collective-permute-start.11 = (bf16[4,160,256]{2,1,0:T(8,128)(2,1)S(1)}, bf16[4,160,256]{2,1,0:T(8,128)(2,1)S(1)}, u32[]{:S(2)}, u32[]{:S(2)}) collective-permute-start(bf16[4,160,256]{2,1,0:T(8,128)(2,1)S(1)} %pad_maximum_fusion.3.refs_0_), channel_id=1, source_target_pairs={{0,16},{4,20},{8,24},{12,28},{16,0},{20,4},{24,8},{28,12},{1,17},{... | collective-permute-start | bytes 983048 | tf_op jit(solution)/shard_map/ppermute | solution.py:208
  45.5 7.0 %collective-permute-start.17 = (bf16[12,160,256]{2,1,0:T(8,128)(2,1)S(1)}, bf16[12,160,256]{2,1,0:T(8,128)(2,1)S(1)}, u32[]{:S(2)}, u32[]{:S(2)}) collective-permute-start(bf16[12,160,256]{2,1,0:T(8,128)(2,1)S(1)} %pad_maximum_fusion.1), channel_id=1, source_target_pairs={{0,4},{4,0},{8,12},{12,8},{16,20},{20,16},{24,28},{28,24},{1,5},{5... | collective-permute-start | bytes 2949128 | tf_op jit(solution)/shard_map/ppermute | solution.py:208
  45.6 6.6 %collective-permute-start.15 = (bf16[2,160,256]{2,1,0:T(8,128)(2,1)S(1)}, bf16[2,160,256]{2,1,0:T(8,128)(2,1)S(1)}, u32[]{:S(2)}, u32[]{:S(2)}) collective-permute-start(bf16[2,160,256]{2,1,0:T(8,128)(2,1)S(1)} %slice.146), channel_id=1, source_target_pairs={{0,8},{4,12},{8,0},{12,4},{16,24},{20,28},{24,16},{28,20},{1,9},{5... | collective-permute-start | bytes 491528 | tf_op jit(solution)/shard_map/ppermute | solution.py:208
  46.2 6.3 %collective-permute-start.16 = (bf16[2,160,256]{2,1,0:T(8,128)(2,1)S(1)}, bf16[2,160,256]{2,1,0:T(8,128)(2,1)S(1)}, u32[]{:S(2)}, u32[]{:S(2)}) collective-permute-start(bf16[2,160,256]{2,1,0:T(8,128)(2,1)S(1)} %slice.147), channel_id=1, source_target_pairs={{0,16},{4,20},{8,24},{12,28},{16,0},{20,4},{24,8},{28,12},{1,17},{... | collective-permute-start | bytes 491528 | tf_op jit(solution)/shard_map/ppermute | solution.py:208
  52.5 4.5 %collective-permute-start.19 = (bf16[2,160,256]{2,1,0:T(8,128)(2,1)S(1)}, bf16[2,160,256]{2,1,0:T(8,128)(2,1)S(1)}, u32[]{:S(2)}, u32[]{:S(2)}) collective-permute-start(bf16[2,160,256]{2,1,0:T(8,128)(2,1)S(1)} %collective-permute-done.16.refs_4_), channel_id=1, source_target_pairs={{0,4},{4,0},{8,12},{12,8},{16,20},{20,16},{24,28},{28,24},{1,5},{5... | collective-permute-start | bytes 491528 | tf_op jit(solution)/shard_map/ppermute | solution.py:208
  57.0 5.0 %collective-permute-start.20 = (bf16[4,4,160,256]{3,2,1,0:T(8,128)(2,1)S(1)}, bf16[4,4,160,256]{3,2,1,0:T(8,128)(2,1)S(1)}, u32[]{:S(2)}, u32[]{:S(2)}) collective-permute-start(bf16[4,4,160,256]{3,2,1,0:T(8,128)(2,1)S(1)} %get-tuple-element.96), channel_id=1, source_target_pairs={{0,4},{4,0},{8,12},{12,8},{16,20},{20,16},{24,28},{28,24},{1,5},{5... | collective-permute-start | bytes 3932168 | tf_op jit(solution)/shard_map/ppermute | solution.py:208
  62.2 10.2 %collective-permute-start.21 = (bf16[2,2,160,256]{3,2,1,0:T(8,128)(2,1)S(1)}, bf16[2,2,160,256]{3,2,1,0:T(8,128)(2,1)S(1)}, u32[]{:S(2)}, u32[]{:S(2)}) collective-permute-start(bf16[2,2,160,256]{3,2,1,0:T(8,128)(2,1)S(1)} %get-tuple-element.107), channel_id=1, source_target_pairs={{0,8},{4,12},{8,0},{12,4},{16,24},{20,28},{24,16},{28,20},{1,9},{5... | collective-permute-start | bytes 983048 | tf_op jit(solution)/shard_map/ppermute | solution.py:208
  63.7 9.8 %collective-permute-start.22 = (bf16[2,2,160,256]{3,2,1,0:T(8,128)(2,1)S(1)}, bf16[2,2,160,256]{3,2,1,0:T(8,128)(2,1)S(1)}, u32[]{:S(2)}, u32[]{:S(2)}) collective-permute-start(bf16[2,2,160,256]{3,2,1,0:T(8,128)(2,1)S(1)} %get-tuple-element.108), channel_id=1, source_target_pairs={{0,16},{4,20},{8,24},{12,28},{16,0},{20,4},{24,8},{28,12},{1,17},{... | collective-permute-start | bytes 983048 | tf_op jit(solution)/shard_map/ppermute | solution.py:208
  73.6 7.0 %collective-permute-start.23 = (bf16[4,4,160,256]{3,2,1,0:T(8,128)(2,1)S(1)}, bf16[4,4,160,256]{3,2,1,0:T(8,128)(2,1)S(1)}, u32[]{:S(2)}, u32[]{:S(2)}) collective-permute-start(bf16[4,4,160,256]{3,2,1,0:T(8,128)(2,1)S(1)} %get-tuple-element.109), channel_id=1, source_target_pairs={{0,4},{4,0},{8,12},{12,8},{16,20},{20,16},{24,28},{28,24},{1,5},{5... | collective-permute-start | bytes 3932168 | tf_op jit(solution)/shard_map/ppermute | solution.py:208
  73.6 6.7 %collective-permute-start.24 = (bf16[2,160,256]{2,1,0:T(8,128)(2,1)S(1)}, bf16[2,160,256]{2,1,0:T(8,128)(2,1)S(1)}, u32[]{:S(2)}, u32[]{:S(2)}) collective-permute-start(bf16[2,160,256]{2,1,0:T(8,128)(2,1)S(1)} %get-tuple-element.133), channel_id=1, source_target_pairs={{0,16},{4,20},{8,24},{12,28},{16,0},{20,4},{24,8},{28,12},{1,17},{... | collective-permute-start | bytes 491528 | tf_op jit(solution)/shard_map/ppermute | solution.py:208
  74.2 6.3 %collective-permute-start.25 = (bf16[2,160,256]{2,1,0:T(8,128)(2,1)S(1)}, bf16[2,160,256]{2,1,0:T(8,128)(2,1)S(1)}, u32[]{:S(2)}, u32[]{:S(2)}) collective-permute-start(bf16[2,160,256]{2,1,0:T(8,128)(2,1)S(1)} %get-tuple-element.132), channel_id=1, source_target_pairs={{0,8},{4,12},{8,0},{12,4},{16,24},{20,28},{24,16},{28,20},{1,9},{5... | collective-permute-start | bytes 491528 | tf_op jit(solution)/shard_map/ppermute | solution.py:208
  80.8 10.5 %collective-permute-start.26 = (bf16[2,2,160,256]{3,2,1,0:T(8,128)(2,1)S(1)}, bf16[2,2,160,256]{3,2,1,0:T(8,128)(2,1)S(1)}, u32[]{:S(2)}, u32[]{:S(2)}) collective-permute-start(bf16[2,2,160,256]{3,2,1,0:T(8,128)(2,1)S(1)} %pad_maximum_fusion.6), channel_id=1, source_target_pairs={{0,8},{4,12},{8,0},{12,4},{16,24},{20,28},{24,16},{28,20},{1,9},{5... | collective-permute-start | bytes 983048 | tf_op jit(solution)/shard_map/ppermute | solution.py:208
  81.4 10.0 %collective-permute-start.27 = (bf16[2,2,160,256]{3,2,1,0:T(8,128)(2,1)S(1)}, bf16[2,2,160,256]{3,2,1,0:T(8,128)(2,1)S(1)}, u32[]{:S(2)}, u32[]{:S(2)}) collective-permute-start(bf16[2,2,160,256]{3,2,1,0:T(8,128)(2,1)S(1)} %pad_maximum_fusion.7), channel_id=1, source_target_pairs={{0,16},{4,20},{8,24},{12,28},{16,0},{20,4},{24,8},{28,12},{1,17},{... | collective-permute-start | bytes 983048 | tf_op jit(solution)/shard_map/ppermute | solution.py:208
  83.0 8.3 %collective-permute-start.33 = (bf16[160,256]{1,0:T(8,128)(2,1)S(1)}, bf16[160,256]{1,0:T(8,128)(2,1)S(1)}, u32[]{:S(2)}, u32[]{:S(2)}) collective-permute-start(bf16[160,256]{1,0:T(8,128)(2,1)S(1)} %get-tuple-element.140), channel_id=1, source_target_pairs={{0,1},{1,0},{2,3},{3,2},{4,5},{5,4},{6,7},{7,6},{8,9},{9,8},{10,11... | collective-permute-start | bytes 245768 | tf_op jit(solution)/shard_map/ppermute | solution.py:208
  83.0 9.9 %collective-permute-start.34 = (bf16[160,256]{1,0:T(8,128)(2,1)S(1)}, bf16[160,256]{1,0:T(8,128)(2,1)S(1)}, u32[]{:S(2)}, u32[]{:S(2)}) collective-permute-start(bf16[160,256]{1,0:T(8,128)(2,1)S(1)} %get-tuple-element.139), channel_id=1, source_target_pairs={{0,2},{1,3},{2,0},{3,1},{4,6},{5,7},{6,4},{7,5},{8,10},{9,11},{10,... | collective-permute-start | bytes 245768 | tf_op jit(solution)/shard_map/ppermute | solution.py:208
  85.5 7.5 %collective-permute-start.35 = (bf16[160,256]{1,0:T(8,128)(2,1)S(1)}, bf16[160,256]{1,0:T(8,128)(2,1)S(1)}, u32[]{:S(2)}, u32[]{:S(2)}) collective-permute-start(bf16[160,256]{1,0:T(8,128)(2,1)S(1)} %get-tuple-element.138), channel_id=1, source_target_pairs={{0,3},{1,2},{2,1},{3,0},{4,7},{5,6},{6,5},{7,4},{8,11},{9,10},{10,... | collective-permute-start | bytes 245768 | tf_op jit(solution)/shard_map/ppermute | solution.py:208
  91.4 5.4 %collective-permute-start.29 = (bf16[2,160,256]{2,1,0:T(8,128)(2,1)S(1)}, bf16[2,160,256]{2,1,0:T(8,128)(2,1)S(1)}, u32[]{:S(2)}, u32[]{:S(2)}) collective-permute-start(bf16[2,160,256]{2,1,0:T(8,128)(2,1)S(1)} %get-tuple-element.127), channel_id=1, source_target_pairs={{0,8},{4,12},{8,0},{12,4},{16,24},{20,28},{24,16},{28,20},{1,9},{5... | collective-permute-start | bytes 491528 | tf_op jit(solution)/shard_map/ppermute | solution.py:208
  93.0 5.4 %collective-permute-start.28 = (bf16[2,160,256]{2,1,0:T(8,128)(2,1)S(1)}, bf16[2,160,256]{2,1,0:T(8,128)(2,1)S(1)}, u32[]{:S(2)}, u32[]{:S(2)}) collective-permute-start(bf16[2,160,256]{2,1,0:T(8,128)(2,1)S(1)} %get-tuple-element.126), channel_id=1, source_target_pairs={{0,16},{4,20},{8,24},{12,28},{16,0},{20,4},{24,8},{28,12},{1,17},{... | collective-permute-start | bytes 491528 | tf_op jit(solution)/shard_map/ppermute | solution.py:208
  98.5 6.0 %collective-permute-start.30 = (bf16[160,256]{1,0:T(8,128)(2,1)S(1)}, bf16[160,256]{1,0:T(8,128)(2,1)S(1)}, u32[]{:S(2)}, u32[]{:S(2)}) collective-permute-start(bf16[160,256]{1,0:T(8,128)(2,1)S(1)} %get-tuple-element.143), channel_id=1, source_target_pairs={{0,1},{1,0},{2,3},{3,2},{4,5},{5,4},{6,7},{7,6},{8,9},{9,8},{10,11... | collective-permute-start | bytes 245768 | tf_op jit(solution)/shard_map/ppermute | solution.py:208
  98.7 5.9 %collective-permute-start.31 = (bf16[160,256]{1,0:T(8,128)(2,1)S(1)}, bf16[160,256]{1,0:T(8,128)(2,1)S(1)}, u32[]{:S(2)}, u32[]{:S(2)}) collective-permute-start(bf16[160,256]{1,0:T(8,128)(2,1)S(1)} %get-tuple-element.142), channel_id=1, source_target_pairs={{0,2},{1,3},{2,0},{3,1},{4,6},{5,7},{6,4},{7,5},{8,10},{9,11},{10,... | collective-permute-start | bytes 245768 | tf_op jit(solution)/shard_map/ppermute | solution.py:208
  101.2 6.2 %collective-permute-start.32 = (bf16[160,256]{1,0:T(8,128)(2,1)S(1)}, bf16[160,256]{1,0:T(8,128)(2,1)S(1)}, u32[]{:S(2)}, u32[]{:S(2)}) collective-permute-start(bf16[160,256]{1,0:T(8,128)(2,1)S(1)} %get-tuple-element.141), channel_id=1, source_target_pairs={{0,3},{1,2},{2,1},{3,0},{4,7},{5,6},{6,5},{7,4},{8,11},{9,10},{10,... | collective-permute-start | bytes 245768 | tf_op jit(solution)/shard_map/ppermute | solution.py:208
  (11 other events, 56.5 us)

commit v4 on v3

--- a/solution.py
+++ b/solution.py
@@ -198,7 +198,7 @@
 
 LOG2E = 1.4426950408889634
 DENSE_SHARDS = 8
-VMEM_MIB = 12
+VMEM_MIB = 8
 NT = (((1,), (1,)), ((), ()))
 TN = (((0,), (0,)), ((), ()))
 
@@ -273,20 +273,26 @@
         return jnp.concatenate([ref[self.rows(row), part].T for part in self.parts(head)], axis=1)
 
 
-def exps_kernel(head, pieces, dims, tokens, place_ref, tp_ref, query_ref, grad_ref, *refs):
-    query, grad, score_ref, sems = refs[-4:]
-    query_copy = pltpu.make_async_copy(query_ref.at[:, dims.wide(head)], query, sems.at[0])
-    grad_copy = pltpu.make_async_copy(grad_ref.at[:, dims.wide(head)], grad, sems.at[1])
-    query_copy.start()
-    grad_copy.start()
-    if pieces:
-        count = len(pieces)
-        exp_ref, grad_t_ref, inv_ref, buffer = refs[count:-4]
-        place_pieces(refs[:count], pieces, tokens, tp_ref[0], buffer)
-    else:
-        buffer, exp_ref, grad_t_ref, inv_ref = refs[:-4]
-    query_copy.wait()
-    grad_copy.wait()
+def first_exps_kernel(pieces, dims, tokens, place_ref, tp_ref, query_hbm, grad_hbm, *refs):
+    count = len(pieces)
+    exp_ref, grad_t_ref, inv_ref, buffer, query, grad, score_ref, sems = refs[count:]
+    copies = []
+    for head in range(dims.heads):
+        for source, target in ((query_hbm, query), (grad_hbm, grad)):
+            lanes = dims.wide(head)
+            copies.append(
+                pltpu.make_async_copy(source.at[:, lanes], target.at[:, lanes], sems.at[len(copies)])
+            )
+            copies[-1].start()
+    place_pieces(refs[:count], pieces, tokens, tp_ref[0], buffer)
+    copies[0].wait()
+    copies[1].wait()
+    exps_kernel(0, dims, place_ref, query, grad, buffer, exp_ref, grad_t_ref, inv_ref, score_ref)
+    for copy in copies[2:]:
+        copy.wait()
+
+
+def exps_kernel(head, dims, place_ref, query, grad, buffer, exp_ref, grad_t_ref, inv_ref, score_ref):
     factor = LOG2E * float(HD) ** (-0.5)
     lanes = dims.lanes(head)
     tops = {}
@@ -294,7 +300,7 @@
         first, second = step, step - 1
         top_new = total = None
         if first < dims.blocks:
-            stacked = dims.stacked(query, first, 0)
+            stacked = dims.stacked(query, first, head)
         if 0 <= second:
             top = jnp.max(tops[second], axis=0, keepdims=True) * factor
         for column, chunk in dims.chunks():
@@ -311,7 +317,7 @@
         if 0 <= second:
             inverse = 1.0 / jnp.sum(total, axis=0, keepdims=True)
             inv_ref[second] = jnp.broadcast_to(inverse, inv_ref.shape[1:])
-            grad_t = dims.flipped(grad, second, 0).astype(jnp.float32)
+            grad_t = dims.flipped(grad, second, head).astype(jnp.float32)
             grad_t_ref[second] = (grad_t * inverse).astype(jnp.bfloat16)
 
 
@@ -341,73 +347,70 @@
         )
 
 
-def score_rows(head, dims, place_ref, exp_ref, grad_t_ref, inv_ref, buffer, ds_ref, dprob_ref, then):
+def score_rows(head, dims, place_ref, exp_ref, grad_t_ref, inv_ref, buffer, out_ref, ds_ref, listed, then):
     lanes = dims.lanes(head)
-    deltas = {}
-    for step in range(dims.blocks + 1):
-        first, second = step, step - 1
-        delta_new = None
-        if 0 <= second:
-            delta = jnp.sum(deltas[second], axis=0, keepdims=True) * inv_ref[second, 0:1]
+    for row in range(dims.blocks):
+        slot = row % 2
         for column, chunk in dims.chunks():
-            if first < dims.blocks:
-                values = buffer[block_of(place_ref, dims.entry(first, column)), lanes]
-                dprob = jnp.dot(values, grad_t_ref[first], preferred_element_type=jnp.float32)
-                dprob_ref[first % 2, chunk] = dprob
-                weight = exp_ref[first, chunk].astype(jnp.float32)
-                delta_new = joined(jnp.add, delta_new, fold(weight * dprob, jnp.sum))
-            if 0 <= second:
-                weight = exp_ref[second, chunk].astype(jnp.float32)
-                ds_ref[second, chunk] = (weight * (dprob_ref[second % 2, chunk] - delta)).astype(
-                    jnp.bfloat16
-                )
-        then(step - 1)
-        deltas[first] = delta_new
+            listed[slot, chunk] = buffer[block_of(place_ref, dims.entry(row, column)), lanes]
+        attended = lax.dot_general(
+            listed[slot], exp_ref[row], TN, preferred_element_type=jnp.float32
+        )
+        attended = (attended * inv_ref[row, 0:1]).astype(jnp.bfloat16)
+        grad_t = grad_t_ref[row]
+        delta = jnp.sum(
+            grad_t.astype(jnp.float32) * attended.astype(jnp.float32), axis=0, keepdims=True
+        )
+        for g, part in enumerate(dims.parts(0)):
+            out_ref[dims.rows(row), part] = attended[:, g * BLK : (g + 1) * BLK].T
+        for column, chunk in dims.chunks():
+            dprob = jnp.dot(listed[slot, chunk], grad_t, preferred_element_type=jnp.float32)
+            weight = exp_ref[row, chunk].astype(jnp.float32)
+            ds_ref[row, chunk] = (weight * (dprob - delta)).astype(jnp.bfloat16)
+        then(row)
 
 
 def scores_kernel(head, pieces, dims, tokens, place_ref, tp_ref, exp_ref, grad_t_ref, inv_ref, *refs):
     count = len(pieces)
-    ds_ref, buffer, flag_ref, dprob_ref = refs[count:]
+    out_ref, ds_ref, buffer, flag_ref, listed = refs[count:]
     flag_ref[...] = jnp.zeros_like(flag_ref)
     place_pieces(refs[:count], pieces, tokens, tp_ref[0], buffer)
-    score_rows(head, dims, place_ref, exp_ref, grad_t_ref, inv_ref, buffer, ds_ref, dprob_ref, lambda row: None)
+    score_rows(
+        head, dims, place_ref, exp_ref, grad_t_ref, inv_ref, buffer, out_ref, ds_ref, listed,
+        lambda row: None,
+    )
 
 
 def keys_kernel(dims, tokens, place_ref, tp_ref, exp_ref, grad_t_ref, inv_ref, buffer, *refs):
-    done_refs, query_ref = refs[: dims.heads - 1], refs[dims.heads - 1]
-    ds_ref, *out_refs, acc, dprob_ref, query, sem = refs[dims.heads :]
-    query_copy = pltpu.make_async_copy(query_ref, query, sem)
-    query_copy.start()
+    done_refs, query = refs[: dims.heads - 1], refs[dims.heads - 1]
+    out_ref, ds_ref, *sum_refs, acc, listed = refs[dims.heads :]
     acc[...] = jnp.zeros_like(acc)
-    query_copy.wait()
 
     def then(row):
-        if row < 0:
-            return
         for head, done_ref in enumerate(done_refs):
             add_keys(acc, dims, place_ref, row, head, done_ref, query)
         add_keys(acc, dims, place_ref, row, dims.heads - 1, ds_ref, query)
 
-    score_rows(dims.heads - 1, dims, place_ref, exp_ref, grad_t_ref, inv_ref, buffer, ds_ref, dprob_ref, then)
-    write_sums(acc, out_refs, tokens, tp_ref[0], float(HD) ** (-0.5))
-
-
-def rows_kernel(dims, scale, place_ref, buffer_ref, *refs):
-    weight_refs, inv_refs = refs[: dims.heads], refs[dims.heads : -2]
-    out_ref, listed = refs[-2:]
+    score_rows(
+        dims.heads - 1, dims, place_ref, exp_ref, grad_t_ref, inv_ref, buffer, out_ref, ds_ref,
+        listed, then,
+    )
+    write_sums(acc, sum_refs, tokens, tp_ref[0], float(HD) ** (-0.5))
+
+
+def rows_kernel(dims, place_ref, buffer_ref, *refs):
+    weight_refs = refs[: dims.heads]
+    out_ref, flag_ref, listed = refs[dims.heads :]
+    flag_ref[...] = jnp.zeros_like(flag_ref)
     for row in range(dims.blocks):
         for head in range(dims.heads):
             for column, chunk in dims.chunks():
                 block = block_of(place_ref, dims.entry(row, column))
-                listed[head, chunk] = buffer_ref[block, dims.lanes(head)]
+                listed[head % 2, chunk] = buffer_ref[block, dims.lanes(head)]
             result = lax.dot_general(
-                listed[head], weight_refs[head][row], TN, preferred_element_type=jnp.float32
+                listed[head % 2], weight_refs[head][row], TN, preferred_element_type=jnp.float32
             )
-            if scale is None:
-                result = result * inv_refs[head][row, 0:1]
-            else:
-                result = result * scale
-            result = result.astype(jnp.bfloat16)
+            result = (result * float(HD) ** (-0.5)).astype(jnp.bfloat16)
             for g, part in enumerate(dims.parts(head)):
                 out_ref[dims.rows(row), part] = result[:, g * BLK : (g + 1) * BLK].T
 
@@ -494,7 +497,9 @@
 
     in_vmem = pl.BlockSpec(memory_space=pltpu.VMEM)
     in_smem = pl.BlockSpec(memory_space=pltpu.SMEM)
-    in_any = pl.BlockSpec(memory_space=pl.ANY)
+    in_hbm = pl.BlockSpec(memory_space=pltpu.HBM)
+    queries = pltpu.with_memory_space_constraint(queries, pltpu.HBM)
+    out_grad = pltpu.with_memory_space_constraint(out_grad, pltpu.HBM)
     shape = jax.ShapeDtypeStruct
     sums = [shape((shard_total // 2, quarters, quarter, head_width), bf16)] * 2
     stash = shape((blocks, list_len, query_rows), bf16)
@@ -503,17 +508,16 @@
     ordered = shape((rows, head_width), bf16)
     flat = shape(queries.shape, bf16)
     flag = shape((8, HD), jnp.float32)
+    one_head = shape((tokens, group * HD), bf16)
     two_rows = pltpu.VMEM((2, list_len, query_rows), jnp.float32)
     total = pltpu.VMEM((rows, head_width), jnp.float32)
-    listed = pltpu.VMEM((heads, list_len, HD), bf16)
-    wide = pltpu.VMEM((tokens, group * HD), bf16)
-    whole = pltpu.VMEM(queries.shape, bf16)
+    listed = pltpu.VMEM((2, list_len, HD), bf16)
     sem = pltpu.SemaphoreType.DMA
 
     def call(name, kernel, outs, scratch, scalars, operands):
         return pl.pallas_call(
             kernel,
-            in_specs=[in_smem] * len(scalars) + [in_any if x is queries or x is out_grad else in_vmem for x in operands],
+            in_specs=[in_smem] * len(scalars) + [in_hbm if x is queries or x is out_grad else in_vmem for x in operands],
             out_specs=[in_vmem] * len(outs),
             out_shape=outs,
             scratch_shapes=scratch,
@@ -535,10 +539,10 @@
     keys += [swap(part, "ctx", 1) for part in (key_three, key_d1, key_d2)]
     value_x, value_y = with_near(held_until(value_own, key_d1))
 
-    rows_scratch = [wide, wide, two_rows, sem((2,))]
-    exp_0, grad_0, inverse_0, keys_in_order = call(
-        "exps_0", functools.partial(exps_kernel, 0, pieces, dims, tokens),
-        [stash, grads, inverses, ordered], rows_scratch, (places, me_tp), (queries, out_grad, *keys),
+    exp_0, grad_0, inverse_0, keys_in_order, query_here, grad_here = call(
+        "exps_0", functools.partial(first_exps_kernel, pieces, dims, tokens),
+        [stash, grads, inverses, ordered, flat, flat], [two_rows, sem((2 * heads,))],
+        (places, me_tp), (queries, out_grad, *keys),
     )
     value_x, value_y, inverse_0 = cut(value_x, value_y, inverse_0)
     value_y1, value_x2, value_three, places_1 = cut(
@@ -549,9 +553,9 @@
     exps, grad_ts, inverse = [exp_0], [grad_0], [inverse_0]
     for head in range(1, heads):
         made = call(
-            "exps", functools.partial(exps_kernel, head, [], dims, tokens),
-            [stash, grads, inverses], rows_scratch, (places_1, me_tp),
-            (queries, out_grad, keys_in_order),
+            "exps", functools.partial(exps_kernel, head, dims),
+            [stash, grads, inverses], [two_rows], (places_1,),
+            (query_here, grad_here, keys_in_order),
         )
         for kept, new in zip((exps, grad_ts, inverse), made):
             kept.append(new)
@@ -564,42 +568,40 @@
     )
     value_near, value_away, places_2, *values[-2:] = cut(value_near, value_away, places, *values[-2:])
     value_got = swap(value_away, "ctx", 1)
-    ds, token = [], None
+    ds, token, attended = [], None, []
     for head in range(heads - 1):
-        made, values_in_order, token = call(
+        out, made, values_in_order, token = call(
             "scores", functools.partial(scores_kernel, head, pieces, dims, tokens),
-            [stash, ordered, flag], [two_rows], (places_2, me_tp),
+            [one_head, stash, ordered, flag], [listed], (places_2, me_tp),
             (exps[head], grad_ts[head], inverse[head], *values),
         )
+        attended.append(out)
         ds.append(made)
     value_got, token = cut(value_got, token)
     to_x, to_y = to_diagonal(value_near, value_got)
     to_x, to_y, places_3 = cut(to_x, to_y, held_until(places, token))
     value_first = swap(to_x, "ctx", 2), swap(to_y, "ctx", 4)
-    made, key_near, key_away = call(
+    out, made, key_near, key_away = call(
         "key_sums", functools.partial(keys_kernel, dims, tokens),
-        [stash, *sums], [total, two_rows, whole, sem], (places_3, me_tp),
-        (exps[-1], grad_ts[-1], inverse[-1], values_in_order, *ds, queries),
-    )
+        [one_head, stash, *sums], [total, listed], (places_3, me_tp),
+        (exps[-1], grad_ts[-1], inverse[-1], values_in_order, *ds, query_here),
+    )
+    attended.append(out)
     ds.append(made)
     key_near, key_away, places_4, *value_first = cut(key_near, key_away, places, *value_first)
     key_got = swap(key_away, "ctx", 1)
     value_more = send_near(value_near, value_got, *value_first)
-    [attended] = call(
-        "attended", functools.partial(rows_kernel, dims, None),
-        [flat], [listed], (places_4,), (values_in_order, *exps, *inverse),
-    )
-    key_got, attended, *value_more = cut(key_got, attended, *value_more)
+    query_grad, token = call(
+        "query_grad", functools.partial(rows_kernel, dims),
+        [flat, flag], [listed], (places_4,), (keys_in_order, *ds),
+    )
+    key_got, token = cut(key_got, token)
+    to_x, to_y = cut(*to_diagonal(key_near, key_got))
+    key_first = swap(to_x, "ctx", 2), swap(to_y, "ctx", 4)
+    attended = jnp.concatenate(cut(*attended, to_x, to_y)[:heads], axis=1)
     value_sum = total_own(value_near, value_got, *value_first, *value_more)
-    to_x, to_y = to_diagonal(key_near, key_got)
-    to_x, to_y, places_5, value_sum = cut(to_x, to_y, places, value_sum)
-    key_first = swap(to_x, "ctx", 2), swap(to_y, "ctx", 4)
-    value_grad = to_quarters(value_sum)
-    [query_grad] = call(
-        "query_grad", functools.partial(rows_kernel, dims, float(HD) ** (-0.5)),
-        [flat], [listed], (places_5,), (keys_in_order, *ds),
-    )
-    query_grad, *key_first = cut(query_grad, *key_first)
+    value_grad = to_quarters(held_until(value_sum, attended))
+    key_first = cut(*key_first, attended)[:2]
     key_more = send_near(key_near, key_got, *key_first)
     key_sum = total_own(key_near, key_got, *key_first, *key_more)
     return attended, query_grad, to_quarters(key_sum), value_grad

time: 108 us -> 107 us (level)
  Pallas kernels: 34.2 us -> 28.8 us
  waiting for transfers between devices: 32.8 us -> 38 us
  local copies, waits for them, and re-layouts: 3.5 us -> 2.34 us
    pallas_call x7 -> x6, Pallas kernels: 34.2 us -> 28.8 us  [call(): pl.pallas_call(kernel, in_specs=[in_smem] * len(scalars) + [in_hbm if x i...]
    ppermute x36, waiting for transfers between devices: 32.8 us -> 38 us  [swap(): return lax.ppermute(value, axis, [(i, i ^ mask) for i in range(count)])]
    unnamed x14 -> x11, local copies, waits for them, and re-layouts: 2.06 us -> 0.82 us
  transfers between devices with their start and end apart: 36 -> 36, of which waited for: 20 -> 23; matrix products, arithmetic and copies ran while one was open for 0% -> 1% of each run, Pallas kernels for 32% -> 27%
where the time goes in v4:
time: 107 us
  waiting for transfers between devices  38 us (36%)
  starting transfers between devices  34.7 us (32%)
  Pallas kernels  28.8 us (27%)
  local copies, waits for them, and re-layouts  2.34 us (2%)
  other arithmetic  1.85 us (2%)
    ppermute x36, waiting for transfers between devices, swap(): return lax.ppermute(value, axis, [(i, i ^ mask) for i in range(count)])  38 us
    ppermute x36, starting transfers between devices, swap(): return lax.ppermute(value, axis, [(i, i ^ mask) for i in range(count)])  34.7 us
    pallas_call x6, Pallas kernels, call(): pl.pallas_call(kernel, in_specs=[in_smem] * len(scalars) + [in_hbm if x i...  28.8 us
  transfers between devices with their start and end apart: 36, of which 23 were waited for; matrix products, arithmetic and copies ran while one was open for 1% of the time, Pallas kernels for 27%

profile of v4, /device:TPU:0, one launch (start us, length us, event | category | flops | bytes accessed | tf_op | source)
XLA Modules:
  0.0 106.7 jit_solution(7433692150247456998)
XLA Ops:
  1.8 5.1 %collective-permute-start.2 = (bf16[160,256]{1,0:T(8,128)(2,1)S(1)}, bf16[160,256]{1,0:T(8,128)(2,1)S(1)}, u32[]{:S(2)}, u32[]{:S(2)}) collective-permute-start(bf16[160,256]{1,0:T(8,128)(2,1)S(1)} %get-tuple-element.152), channel_id=1, source_target_pairs={{0,3},{1,2},{2,1},{3,0},{4,7},{5,6},{6,5},{7,4},{8,11},{9,10},{10,... | collective-permute-start | bytes 245768 | tf_op jit(solution)/shard_map/ppermute | solution.py:208
  7.5 2.4 %collective-permute-done.2 = bf16[160,256]{1,0:T(8,128)(2,1)S(1)} collective-permute-done((bf16[160,256]{1,0:T(8,128)(2,1)S(1)}, bf16[160,256]{1,0:T(8,128)(2,1)S(1)}, u32[]{:S(2)}, u32[]{:S(2)}) %collective-permute-start.2) | collective-permute-done | bytes 81952 | tf_op jit(solution)/shard_map/ppermute | solution.py:208
  9.9 3.8 %collective-permute-done.1 = bf16[160,256]{1,0:T(8,128)(2,1)S(1)} collective-permute-done((bf16[160,256]{1,0:T(8,128)(2,1)S(1)}, bf16[160,256]{1,0:T(8,128)(2,1)S(1)}, u32[]{:S(2)}, u32[]{:S(2)}) %collective-permute-start.1) | collective-permute-done | bytes 81952 | tf_op jit(solution)/shard_map/ppermute | solution.py:208
  13.8 1.6 %collective-permute-start.3 = (bf16[4,160,256]{2,1,0:T(8,128)(2,1)S(1)}, bf16[4,160,256]{2,1,0:T(8,128)(2,1)S(1)}, u32[]{:S(2)}, u32[]{:S(2)}) collective-permute-start(bf16[4,160,256]{2,1,0:T(8,128)(2,1)S(1)} %pad_maximum_fusion.2.refs_0_), channel_id=1, source_target_pairs={{0,8},{4,12},{8,0},{12,4},{16,24},{20,28},{24,16},{28,20},{1,9},{5... | collective-permute-start | bytes 983048 | tf_op jit(solution)/shard_map/ppermute | solution.py:208
  15.3 1.5 %collective-permute-start.4 = (bf16[4,160,256]{2,1,0:T(8,128)(2,1)S(1)}, bf16[4,160,256]{2,1,0:T(8,128)(2,1)S(1)}, u32[]{:S(2)}, u32[]{:S(2)}) collective-permute-start(bf16[4,160,256]{2,1,0:T(8,128)(2,1)S(1)} %pad_maximum_fusion.2.refs_0_), channel_id=1, source_target_pairs={{0,16},{4,20},{8,24},{12,28},{16,0},{20,4},{24,8},{28,12},{1,17},{... | collective-permute-start | bytes 983048 | tf_op jit(solution)/shard_map/ppermute | solution.py:208
  16.9 2.8 %collective-permute-start.7 = (bf16[160,256]{1,0:T(8,128)(2,1)S(1)}, bf16[160,256]{1,0:T(8,128)(2,1)S(1)}, u32[]{:S(2)}, u32[]{:S(2)}) collective-permute-start(bf16[160,256]{1,0:T(8,128)(2,1)S(1)} %get-tuple-element.148), channel_id=1, source_target_pairs={{0,3},{1,2},{2,1},{3,0},{4,7},{5,6},{6,5},{7,4},{8,11},{9,10},{10,... | collective-permute-start | bytes 245768 | tf_op jit(solution)/shard_map/ppermute | solution.py:208
  19.7 1.7 %collective-permute-start.5 = (bf16[160,256]{1,0:T(8,128)(2,1)S(1)}, bf16[160,256]{1,0:T(8,128)(2,1)S(1)}, u32[]{:S(2)}, u32[]{:S(2)}) collective-permute-start(bf16[160,256]{1,0:T(8,128)(2,1)S(1)} %get-tuple-element.147), channel_id=1, source_target_pairs={{0,1},{1,0},{2,3},{3,2},{4,5},{5,4},{6,7},{7,6},{8,9},{9,8},{10,11... | collective-permute-start | bytes 245768 | tf_op jit(solution)/shard_map/ppermute | solution.py:208
  21.4 2.6 %collective-permute-done.7 = bf16[160,256]{1,0:T(8,128)(2,1)S(1)} collective-permute-done((bf16[160,256]{1,0:T(8,128)(2,1)S(1)}, bf16[160,256]{1,0:T(8,128)(2,1)S(1)}, u32[]{:S(2)}, u32[]{:S(2)}) %collective-permute-start.7) | collective-permute-done | bytes 81952 | tf_op jit(solution)/shard_map/ppermute | solution.py:208
  23.9 2.5 %collective-permute-done.6 = bf16[160,256]{1,0:T(8,128)(2,1)S(1)} collective-permute-done((bf16[160,256]{1,0:T(8,128)(2,1)S(1)}, bf16[160,256]{1,0:T(8,128)(2,1)S(1)}, u32[]{:S(2)}, u32[]{:S(2)}) %collective-permute-start.6) | collective-permute-done | bytes 81952 | tf_op jit(solution)/shard_map/ppermute | solution.py:208
  28.5 4.4 %collective-permute-done.8.refs_3_ = bf16[2,160,256]{2,1,0:T(8,128)(2,1)S(1)} collective-permute-done((bf16[2,160,256]{2,1,0:T(8,128)(2,1)S(1)}, bf16[2,160,256]{2,1,0:T(8,128)(2,1)S(1)}, u32[]{:S(2)}, u32[]{:S(2)}) %collective-permute-start.8) | collective-permute-done | bytes 163872 | tf_op jit(solution)/shard_map/ppermute | solution.py:208
  34.0 1.5 %collective-permute-start.10 = (bf16[4,160,256]{2,1,0:T(8,128)(2,1)S(1)}, bf16[4,160,256]{2,1,0:T(8,128)(2,1)S(1)}, u32[]{:S(2)}, u32[]{:S(2)}) collective-permute-start(bf16[4,160,256]{2,1,0:T(8,128)(2,1)S(1)} %pad_maximum_fusion.3.refs_0_), channel_id=1, source_target_pairs={{0,8},{4,12},{8,0},{12,4},{16,24},{20,28},{24,16},{28,20},{1,9},{5... | collective-permute-start | bytes 983048 | tf_op jit(solution)/shard_map/ppermute | solution.py:208
  36.5 5.8 %exps_0.1 = (bf16[5,1024,512]{2,1,0:T(8,128)(2,1)S(1)}, bf16[5,128,512]{2,1,0:T(8,128)(2,1)S(1)}, f32[5,8,512]{2,1,0:T(8,128)S(1)}, bf16[5120,256]{1,0:T(8,128)(...) custom-call(s32[40]{0:T(128)S(1)} %reshape.24.place_ref, s32[1]{0:T(128)} %bitcast.8.tp_ref, ...), custom_call_target="tpu_custom_call" | custom-call | flops 4294967296 | bytes 1048576 | tf_op jit(solution)/shard_map/exps_0/pallas_call | solution.py:518
  42.3 1.9 %collective-permute-done.10.refs_1_ = bf16[4,160,256]{2,1,0:T(8,128)(2,1)S(1)} collective-permute-done((bf16[4,160,256]{2,1,0:T(8,128)(2,1)S(1)}, bf16[4,160,256]{2,1,0:T(8,128)(2,1)S(1)}, u32[]{:S(2)}, u32[]{:S(2)}) %collective-permute-start.10) | collective-permute-done | bytes 327712 | tf_op jit(solution)/shard_map/ppermute | solution.py:208
  46.6 4.3 %exps.1 = (bf16[5,1024,512]{2,1,0:T(8,128)(2,1)S(1)}, bf16[5,128,512]{2,1,0:T(8,128)(2,1)S(1)}, f32[5,8,512]{2,1,0:T(8,128)S(1)}) custom-call(s32[40]{0:T(128)S(1)} %reshape.24.place_ref, bf16[640,1024]{1,0:T(8,128)(2,1)S(1)} %get-tuple-element.84.query.refs_1_, bf16[640,1024]{1,0:T(8,128)(2,1)S(1)} %get-tuple-element.85.grad, ...), custom_call_target="tpu_custom_call" | custom-call | flops 4294967296 | bytes 1048576 | tf_op jit(solution)/shard_map/exps/pallas_call | solution.py:518
  50.9 1.4 %collective-permute-done.15.refs_3_ = bf16[2,160,256]{2,1,0:T(8,128)(2,1)S(1)} collective-permute-done((bf16[2,160,256]{2,1,0:T(8,128)(2,1)S(1)}, bf16[2,160,256]{2,1,0:T(8,128)(2,1)S(1)}, u32[]{:S(2)}, u32[]{:S(2)}) %collective-permute-start.15) | collective-permute-done | bytes 163872 | tf_op jit(solution)/shard_map/ppermute | solution.py:208
  53.0 4.2 %value_sums.1 = (bf16[4,4,160,256]{3,2,1,0:T(8,128)(2,1)S(1)}, bf16[4,4,160,256]{3,2,1,0:T(8,128)(2,1)S(1)}) custom-call(s32[40]{0:T(128)S(1)} %reshape.24.place_ref, s32[1]{0:T(128)} %bitcast.8.tp_ref, bf16[5,1024,512]{2,1,0:T(8,128)(2,1)S(1)} %get-tuple-element.90.refs_0_.exp_ref, bf16[5,1024,512]{2,1,0:T(8,128)(2,1)S(1)} %get-tuple-element.91.refs_1_.exp_ref, ...), custom_call_target="tpu_custom_call" | custom-call | flops 4294967296 | bytes 1048576 | tf_op jit(solution)/shard_map/value_sums/pallas_call | solution.py:518
  57.3 4.0 %scores.1 = (bf16[640,512]{1,0:T(8,128)(2,1)S(1)}, bf16[5,1024,512]{2,1,0:T(8,128)(2,1)S(1)}, bf16[5120,256]{1,0:T(8,128)(2,1)S(1)}, f32[8,128]{1,0:T(8,128)}) custom-call(s32[40]{0:T(128)S(1)} %reshape.24.place_ref, s32[1]{0:T(128)} %bitcast.8.tp_ref, bf16[5,1024,512]{2,1,0:T(8,128)(2,1)S(1)} %get-tuple-element.90.refs_0_.exp_ref, ...), custom_call_target="tpu_custom_call" | custom-call | flops 4294967296 | bytes 1048576 | tf_op jit(solution)/shard_map/scores/pallas_call | solution.py:518
  61.5 1.6 %collective-permute-start.21 = (bf16[2,2,160,256]{3,2,1,0:T(8,128)(2,1)S(1)}, bf16[2,2,160,256]{3,2,1,0:T(8,128)(2,1)S(1)}, u32[]{:S(2)}, u32[]{:S(2)}) collective-permute-start(bf16[2,2,160,256]{3,2,1,0:T(8,128)(2,1)S(1)} %get-tuple-element.112), channel_id=1, source_target_pairs={{0,8},{4,12},{8,0},{12,4},{16,24},{20,28},{24,16},{28,20},{1,9},{5... | collective-permute-start | bytes 983048 | tf_op jit(solution)/shard_map/ppermute | solution.py:208
  63.5 6.7 %key_sums.1 = (bf16[640,512]{1,0:T(8,128)(2,1)S(1)}, bf16[5,1024,512]{2,1,0:T(8,128)(2,1)S(1)}, bf16[4,4,160,256]{3,2,1,0:T(8,128)(2,1)S(1)}, bf16[4,4,160,256]{3,2,1,0:T(8,128)(2,1)S(1)}) custom-call(s32[40]{0:T(128)S(1)} %reshape.24.place_ref, s32[1]{0:T(128)} %bitcast.8.tp_ref, bf16[5,1024,512]{2,1,0:T(8,128)(2,1)S(1)} %get-tuple-element.91.refs_1_.exp_ref, ...), custom_call_target="tpu_custom_call" | custom-call | flops 4294967296 | bytes 1048576 | tf_op jit(solution)/shard_map/key_sums/pallas_call | solution.py:518
  70.2 1.4 %collective-permute-done.21 = bf16[2,2,160,256]{3,2,1,0:T(8,128)(2,1)S(1)} collective-permute-done((bf16[2,2,160,256]{3,2,1,0:T(8,128)(2,1)S(1)}, bf16[2,2,160,256]{3,2,1,0:T(8,128)(2,1)S(1)}, u32[]{:S(2)}, u32[]{:S(2)}) %collective-permute-start.21) | collective-permute-done | bytes 327712 | tf_op jit(solution)/shard_map/ppermute | solution.py:208
  73.9 3.8 %query_grad.1 = (bf16[640,1024]{1,0:T(8,128)(2,1)}, f32[8,128]{1,0:T(8,128)}) custom-call(s32[40]{0:T(128)S(1)} %reshape.24.place_ref, bf16[5120,256]{1,0:T(8,128)(2,1)S(1)} %get-tuple-element.86.buffer.buffer_ref, bf16[5,1024,512]{2,1,0:T(8,128)(2,1)S(1)} %get-tuple-element.108.refs_0_, bf16[5,1024,512]{2,1,0:T(8,128)(2,1)S(1)} %get-tuple-element.121.refs_1_), custom_call_target="tpu_custom_call" | custom-call | flops 4294967296 | bytes 1048576 | tf_op jit(solution)/shard_map/query_grad/pallas_call | solution.py:518
  77.7 1.9 %collective-permute-done.32 = bf16[2,160,256]{2,1,0:T(8,128)(2,1)S(1)} collective-permute-done((bf16[2,160,256]{2,1,0:T(8,128)(2,1)S(1)}, bf16[2,160,256]{2,1,0:T(8,128)(2,1)S(1)}, u32[]{:S(2)}, u32[]{:S(2)}) %collective-permute-start.32) | collective-permute-done | bytes 163872 | tf_op jit(solution)/shard_map/ppermute | solution.py:208
  80.1 1.6 %collective-permute-start.24 = (bf16[2,2,160,256]{3,2,1,0:T(8,128)(2,1)S(1)}, bf16[2,2,160,256]{3,2,1,0:T(8,128)(2,1)S(1)}, u32[]{:S(2)}, u32[]{:S(2)}) collective-permute-start(bf16[2,2,160,256]{3,2,1,0:T(8,128)(2,1)S(1)} %pad_maximum_fusion.6), channel_id=1, source_target_pairs={{0,8},{4,12},{8,0},{12,4},{16,24},{20,28},{24,16},{28,20},{1,9},{5... | collective-permute-start | bytes 983048 | tf_op jit(solution)/shard_map/ppermute | solution.py:208
  82.5 2.5 %collective-permute-start.34 = (bf16[160,256]{1,0:T(8,128)(2,1)S(1)}, bf16[160,256]{1,0:T(8,128)(2,1)S(1)}, u32[]{:S(2)}, u32[]{:S(2)}) collective-permute-start(bf16[160,256]{1,0:T(8,128)(2,1)S(1)} %get-tuple-element.141), channel_id=1, source_target_pairs={{0,2},{1,3},{2,0},{3,1},{4,6},{5,7},{6,4},{7,5},{8,10},{9,11},{10,... | collective-permute-start | bytes 245768 | tf_op jit(solution)/shard_map/ppermute | solution.py:208
  85.0 2.0 %collective-permute-start.35 = (bf16[160,256]{1,0:T(8,128)(2,1)S(1)}, bf16[160,256]{1,0:T(8,128)(2,1)S(1)}, u32[]{:S(2)}, u32[]{:S(2)}) collective-permute-start(bf16[160,256]{1,0:T(8,128)(2,1)S(1)} %get-tuple-element.140), channel_id=1, source_target_pairs={{0,3},{1,2},{2,1},{3,0},{4,7},{5,6},{6,5},{7,4},{8,11},{9,10},{10,... | collective-permute-start | bytes 245768 | tf_op jit(solution)/shard_map/ppermute | solution.py:208
  87.0 2.3 %collective-permute-done.24 = bf16[2,2,160,256]{3,2,1,0:T(8,128)(2,1)S(1)} collective-permute-done((bf16[2,2,160,256]{3,2,1,0:T(8,128)(2,1)S(1)}, bf16[2,2,160,256]{3,2,1,0:T(8,128)(2,1)S(1)}, u32[]{:S(2)}, u32[]{:S(2)}) %collective-permute-start.24) | collective-permute-done | bytes 327712 | tf_op jit(solution)/shard_map/ppermute | solution.py:208
  91.4 1.6 %collective-permute-start.26 = (bf16[2,160,256]{2,1,0:T(8,128)(2,1)S(1)}, bf16[2,160,256]{2,1,0:T(8,128)(2,1)S(1)}, u32[]{:S(2)}, u32[]{:S(2)}) collective-permute-start(bf16[2,160,256]{2,1,0:T(8,128)(2,1)S(1)} %get-tuple-element.130), channel_id=1, source_target_pairs={{0,16},{4,20},{8,24},{12,28},{16,0},{20,4},{24,8},{28,12},{1,17},{... | collective-permute-start | bytes 491528 | tf_op jit(solution)/shard_map/ppermute | solution.py:208
  93.0 2.9 %collective-permute-done.27 = bf16[2,160,256]{2,1,0:T(8,128)(2,1)S(1)} collective-permute-done((bf16[2,160,256]{2,1,0:T(8,128)(2,1)S(1)}, bf16[2,160,256]{2,1,0:T(8,128)(2,1)S(1)}, u32[]{:S(2)}, u32[]{:S(2)}) %collective-permute-start.27) | collective-permute-done | bytes 163872 | tf_op jit(solution)/shard_map/ppermute | solution.py:208
  98.2 1.4 %collective-permute-start.29 = (bf16[160,256]{1,0:T(8,128)(2,1)S(1)}, bf16[160,256]{1,0:T(8,128)(2,1)S(1)}, u32[]{:S(2)}, u32[]{:S(2)}) collective-permute-start(bf16[160,256]{1,0:T(8,128)(2,1)S(1)} %get-tuple-element.144), channel_id=1, source_target_pairs={{0,2},{1,3},{2,0},{3,1},{4,6},{5,7},{6,4},{7,5},{8,10},{9,11},{10,... | collective-permute-start | bytes 245768 | tf_op jit(solution)/shard_map/ppermute | solution.py:208
  99.6 1.9 %collective-permute-start.30 = (bf16[160,256]{1,0:T(8,128)(2,1)S(1)}, bf16[160,256]{1,0:T(8,128)(2,1)S(1)}, u32[]{:S(2)}, u32[]{:S(2)}) collective-permute-start(bf16[160,256]{1,0:T(8,128)(2,1)S(1)} %get-tuple-element.143), channel_id=1, source_target_pairs={{0,3},{1,2},{2,1},{3,0},{4,7},{5,6},{6,5},{7,4},{8,11},{9,10},{10,... | collective-permute-start | bytes 245768 | tf_op jit(solution)/shard_map/ppermute | solution.py:208
  101.9 2.6 %collective-permute-done.29 = bf16[160,256]{1,0:T(8,128)(2,1)S(1)} collective-permute-done((bf16[160,256]{1,0:T(8,128)(2,1)S(1)}, bf16[160,256]{1,0:T(8,128)(2,1)S(1)}, u32[]{:S(2)}, u32[]{:S(2)}) %collective-permute-start.29) | collective-permute-done | bytes 81952 | tf_op jit(solution)/shard_map/ppermute | solution.py:208
  104.5 1.5 %collective-permute-done.30 = bf16[160,256]{1,0:T(8,128)(2,1)S(1)} collective-permute-done((bf16[160,256]{1,0:T(8,128)(2,1)S(1)}, bf16[160,256]{1,0:T(8,128)(2,1)S(1)}, u32[]{:S(2)}, u32[]{:S(2)}) %collective-permute-start.30) | collective-permute-done | bytes 81952 | tf_op jit(solution)/shard_map/ppermute | solution.py:208
  (95 shorter events, 18.8 us)
Async XLA Ops:
  1.8 8.1 %collective-permute-start.2 = (bf16[160,256]{1,0:T(8,128)(2,1)S(1)}, bf16[160,256]{1,0:T(8,128)(2,1)S(1)}, u32[]{:S(2)}, u32[]{:S(2)}) collective-permute-start(bf16[160,256]{1,0:T(8,128)(2,1)S(1)} %get-tuple-element.152), channel_id=1, source_target_pairs={{0,3},{1,2},{2,1},{3,0},{4,7},{5,6},{6,5},{7,4},{8,11},{9,10},{10,... | collective-permute-start | bytes 245768 | tf_op jit(solution)/shard_map/ppermute | solution.py:208
  6.9 6.9 %collective-permute-start.1 = (bf16[160,256]{1,0:T(8,128)(2,1)S(1)}, bf16[160,256]{1,0:T(8,128)(2,1)S(1)}, u32[]{:S(2)}, u32[]{:S(2)}) collective-permute-start(bf16[160,256]{1,0:T(8,128)(2,1)S(1)} %get-tuple-element.153), channel_id=1, source_target_pairs={{0,2},{1,3},{2,0},{3,1},{4,6},{5,7},{6,4},{7,5},{8,10},{9,11},{10,... | collective-permute-start | bytes 245768 | tf_op jit(solution)/shard_map/ppermute | solution.py:208
  6.9 6.9 %collective-permute-start = (bf16[160,256]{1,0:T(8,128)(2,1)S(1)}, bf16[160,256]{1,0:T(8,128)(2,1)S(1)}, u32[]{:S(2)}, u32[]{:S(2)}) collective-permute-start(bf16[160,256]{1,0:T(8,128)(2,1)S(1)} %get-tuple-element.151), channel_id=1, source_target_pairs={{0,1},{1,0},{2,3},{3,2},{4,5},{5,4},{6,7},{7,6},{8,9},{9,8},{10,11... | collective-permute-start | bytes 245768 | tf_op jit(solution)/shard_map/ppermute | solution.py:208
  13.8 12.7 %collective-permute-start.3 = (bf16[4,160,256]{2,1,0:T(8,128)(2,1)S(1)}, bf16[4,160,256]{2,1,0:T(8,128)(2,1)S(1)}, u32[]{:S(2)}, u32[]{:S(2)}) collective-permute-start(bf16[4,160,256]{2,1,0:T(8,128)(2,1)S(1)} %pad_maximum_fusion.2.refs_0_), channel_id=1, source_target_pairs={{0,8},{4,12},{8,0},{12,4},{16,24},{20,28},{24,16},{28,20},{1,9},{5... | collective-permute-start | bytes 983048 | tf_op jit(solution)/shard_map/ppermute | solution.py:208
  15.3 11.1 %collective-permute-start.4 = (bf16[4,160,256]{2,1,0:T(8,128)(2,1)S(1)}, bf16[4,160,256]{2,1,0:T(8,128)(2,1)S(1)}, u32[]{:S(2)}, u32[]{:S(2)}) collective-permute-start(bf16[4,160,256]{2,1,0:T(8,128)(2,1)S(1)} %pad_maximum_fusion.2.refs_0_), channel_id=1, source_target_pairs={{0,16},{4,20},{8,24},{12,28},{16,0},{20,4},{24,8},{28,12},{1,17},{... | collective-permute-start | bytes 983048 | tf_op jit(solution)/shard_map/ppermute | solution.py:208
  16.9 7.0 %collective-permute-start.7 = (bf16[160,256]{1,0:T(8,128)(2,1)S(1)}, bf16[160,256]{1,0:T(8,128)(2,1)S(1)}, u32[]{:S(2)}, u32[]{:S(2)}) collective-permute-start(bf16[160,256]{1,0:T(8,128)(2,1)S(1)} %get-tuple-element.148), channel_id=1, source_target_pairs={{0,3},{1,2},{2,1},{3,0},{4,7},{5,6},{6,5},{7,4},{8,11},{9,10},{10,... | collective-permute-start | bytes 245768 | tf_op jit(solution)/shard_map/ppermute | solution.py:208
  19.7 6.7 %collective-permute-start.6 = (bf16[160,256]{1,0:T(8,128)(2,1)S(1)}, bf16[160,256]{1,0:T(8,128)(2,1)S(1)}, u32[]{:S(2)}, u32[]{:S(2)}) collective-permute-start(bf16[160,256]{1,0:T(8,128)(2,1)S(1)} %get-tuple-element.149), channel_id=1, source_target_pairs={{0,2},{1,3},{2,0},{3,1},{4,6},{5,7},{6,4},{7,5},{8,10},{9,11},{10,... | collective-permute-start | bytes 245768 | tf_op jit(solution)/shard_map/ppermute | solution.py:208
  19.7 6.7 %collective-permute-start.5 = (bf16[160,256]{1,0:T(8,128)(2,1)S(1)}, bf16[160,256]{1,0:T(8,128)(2,1)S(1)}, u32[]{:S(2)}, u32[]{:S(2)}) collective-permute-start(bf16[160,256]{1,0:T(8,128)(2,1)S(1)} %get-tuple-element.147), channel_id=1, source_target_pairs={{0,1},{1,0},{2,3},{3,2},{4,5},{5,4},{6,7},{7,6},{8,9},{9,8},{10,11... | collective-permute-start | bytes 245768 | tf_op jit(solution)/shard_map/ppermute | solution.py:208
  27.6 5.3 %collective-permute-start.8 = (bf16[2,160,256]{2,1,0:T(8,128)(2,1)S(1)}, bf16[2,160,256]{2,1,0:T(8,128)(2,1)S(1)}, u32[]{:S(2)}, u32[]{:S(2)}) collective-permute-start(bf16[2,160,256]{2,1,0:T(8,128)(2,1)S(1)} %slice.144), channel_id=1, source_target_pairs={{0,8},{4,12},{8,0},{12,4},{16,24},{20,28},{24,16},{28,20},{1,9},{5... | collective-permute-start | bytes 491528 | tf_op jit(solution)/shard_map/ppermute | solution.py:208
  28.1 5.3 %collective-permute-start.9 = (bf16[2,160,256]{2,1,0:T(8,128)(2,1)S(1)}, bf16[2,160,256]{2,1,0:T(8,128)(2,1)S(1)}, u32[]{:S(2)}, u32[]{:S(2)}) collective-permute-start(bf16[2,160,256]{2,1,0:T(8,128)(2,1)S(1)} %slice.145), channel_id=1, source_target_pairs={{0,16},{4,20},{8,24},{12,28},{16,0},{20,4},{24,8},{28,12},{1,17},{... | collective-permute-start | bytes 491528 | tf_op jit(solution)/shard_map/ppermute | solution.py:208
  34.0 10.1 %collective-permute-start.10 = (bf16[4,160,256]{2,1,0:T(8,128)(2,1)S(1)}, bf16[4,160,256]{2,1,0:T(8,128)(2,1)S(1)}, u32[]{:S(2)}, u32[]{:S(2)}) collective-permute-start(bf16[4,160,256]{2,1,0:T(8,128)(2,1)S(1)} %pad_maximum_fusion.3.refs_0_), channel_id=1, source_target_pairs={{0,8},{4,12},{8,0},{12,4},{16,24},{20,28},{24,16},{28,20},{1,9},{5... | collective-permute-start | bytes 983048 | tf_op jit(solution)/shard_map/ppermute | solution.py:208
  35.5 9.8 %collective-permute-start.11 = (bf16[4,160,256]{2,1,0:T(8,128)(2,1)S(1)}, bf16[4,160,256]{2,1,0:T(8,128)(2,1)S(1)}, u32[]{:S(2)}, u32[]{:S(2)}) collective-permute-start(bf16[4,160,256]{2,1,0:T(8,128)(2,1)S(1)} %pad_maximum_fusion.3.refs_0_), channel_id=1, source_target_pairs={{0,16},{4,20},{8,24},{12,28},{16,0},{20,4},{24,8},{28,12},{1,17},{... | collective-permute-start | bytes 983048 | tf_op jit(solution)/shard_map/ppermute | solution.py:208
  45.5 7.0 %collective-permute-start.17 = (bf16[12,160,256]{2,1,0:T(8,128)(2,1)S(1)}, bf16[12,160,256]{2,1,0:T(8,128)(2,1)S(1)}, u32[]{:S(2)}, u32[]{:S(2)}) collective-permute-start(bf16[12,160,256]{2,1,0:T(8,128)(2,1)S(1)} %pad_maximum_fusion.1), channel_id=1, source_target_pairs={{0,4},{4,0},{8,12},{12,8},{16,20},{20,16},{24,28},{28,24},{1,5},{5... | collective-permute-start | bytes 2949128 | tf_op jit(solution)/shard_map/ppermute | solution.py:208
  45.6 6.6 %collective-permute-start.15 = (bf16[2,160,256]{2,1,0:T(8,128)(2,1)S(1)}, bf16[2,160,256]{2,1,0:T(8,128)(2,1)S(1)}, u32[]{:S(2)}, u32[]{:S(2)}) collective-permute-start(bf16[2,160,256]{2,1,0:T(8,128)(2,1)S(1)} %slice.146), channel_id=1, source_target_pairs={{0,8},{4,12},{8,0},{12,4},{16,24},{20,28},{24,16},{28,20},{1,9},{5... | collective-permute-start | bytes 491528 | tf_op jit(solution)/shard_map/ppermute | solution.py:208
  46.2 6.3 %collective-permute-start.16 = (bf16[2,160,256]{2,1,0:T(8,128)(2,1)S(1)}, bf16[2,160,256]{2,1,0:T(8,128)(2,1)S(1)}, u32[]{:S(2)}, u32[]{:S(2)}) collective-permute-start(bf16[2,160,256]{2,1,0:T(8,128)(2,1)S(1)} %slice.147), channel_id=1, source_target_pairs={{0,16},{4,20},{8,24},{12,28},{16,0},{20,4},{24,8},{28,12},{1,17},{... | collective-permute-start | bytes 491528 | tf_op jit(solution)/shard_map/ppermute | solution.py:208
  52.5 4.7 %collective-permute-start.18 = (bf16[2,160,256]{2,1,0:T(8,128)(2,1)S(1)}, bf16[2,160,256]{2,1,0:T(8,128)(2,1)S(1)}, u32[]{:S(2)}, u32[]{:S(2)}) collective-permute-start(bf16[2,160,256]{2,1,0:T(8,128)(2,1)S(1)} %collective-permute-done.15.refs_3_), channel_id=1, source_target_pairs={{0,4},{4,0},{8,12},{12,8},{16,20},{20,16},{24,28},{28,24},{1,5},{5... | collective-permute-start | bytes 491528 | tf_op jit(solution)/shard_map/ppermute | solution.py:208
  52.5 4.7 %collective-permute-start.19 = (bf16[2,160,256]{2,1,0:T(8,128)(2,1)S(1)}, bf16[2,160,256]{2,1,0:T(8,128)(2,1)S(1)}, u32[]{:S(2)}, u32[]{:S(2)}) collective-permute-start(bf16[2,160,256]{2,1,0:T(8,128)(2,1)S(1)} %collective-permute-done.16.refs_4_), channel_id=1, source_target_pairs={{0,4},{4,0},{8,12},{12,8},{16,20},{20,16},{24,28},{28,24},{1,5},{5... | collective-permute-start | bytes 491528 | tf_op jit(solution)/shard_map/ppermute | solution.py:208
  61.5 10.2 %collective-permute-start.21 = (bf16[2,2,160,256]{3,2,1,0:T(8,128)(2,1)S(1)}, bf16[2,2,160,256]{3,2,1,0:T(8,128)(2,1)S(1)}, u32[]{:S(2)}, u32[]{:S(2)}) collective-permute-start(bf16[2,2,160,256]{3,2,1,0:T(8,128)(2,1)S(1)} %get-tuple-element.112), channel_id=1, source_target_pairs={{0,8},{4,12},{8,0},{12,4},{16,24},{20,28},{24,16},{28,20},{1,9},{5... | collective-permute-start | bytes 983048 | tf_op jit(solution)/shard_map/ppermute | solution.py:208
  63.0 9.8 %collective-permute-start.22 = (bf16[2,2,160,256]{3,2,1,0:T(8,128)(2,1)S(1)}, bf16[2,2,160,256]{3,2,1,0:T(8,128)(2,1)S(1)}, u32[]{:S(2)}, u32[]{:S(2)}) collective-permute-start(bf16[2,2,160,256]{3,2,1,0:T(8,128)(2,1)S(1)} %get-tuple-element.113), channel_id=1, source_target_pairs={{0,16},{4,20},{8,24},{12,28},{16,0},{20,4},{24,8},{28,12},{1,17},{... | collective-permute-start | bytes 983048 | tf_op jit(solution)/shard_map/ppermute | solution.py:208
  72.8 7.1 %collective-permute-start.23 = (bf16[4,4,160,256]{3,2,1,0:T(8,128)(2,1)S(1)}, bf16[4,4,160,256]{3,2,1,0:T(8,128)(2,1)S(1)}, u32[]{:S(2)}, u32[]{:S(2)}) collective-permute-start(bf16[4,4,160,256]{3,2,1,0:T(8,128)(2,1)S(1)} %get-tuple-element.115), channel_id=1, source_target_pairs={{0,4},{4,0},{8,12},{12,8},{16,20},{20,16},{24,28},{28,24},{1,5},{5... | collective-permute-start | bytes 3932168 | tf_op jit(solution)/shard_map/ppermute | solution.py:208
  72.9 6.7 %collective-permute-start.32 = (bf16[2,160,256]{2,1,0:T(8,128)(2,1)S(1)}, bf16[2,160,256]{2,1,0:T(8,128)(2,1)S(1)}, u32[]{:S(2)}, u32[]{:S(2)}) collective-permute-start(bf16[2,160,256]{2,1,0:T(8,128)(2,1)S(1)} %get-tuple-element.129), channel_id=1, source_target_pairs={{0,8},{4,12},{8,0},{12,4},{16,24},{20,28},{24,16},{28,20},{1,9},{5... | collective-permute-start | bytes 491528 | tf_op jit(solution)/shard_map/ppermute | solution.py:208
  73.5 6.3 %collective-permute-start.31 = (bf16[2,160,256]{2,1,0:T(8,128)(2,1)S(1)}, bf16[2,160,256]{2,1,0:T(8,128)(2,1)S(1)}, u32[]{:S(2)}, u32[]{:S(2)}) collective-permute-start(bf16[2,160,256]{2,1,0:T(8,128)(2,1)S(1)} %get-tuple-element.128), channel_id=1, source_target_pairs={{0,16},{4,20},{8,24},{12,28},{16,0},{20,4},{24,8},{28,12},{1,17},{... | collective-permute-start | bytes 491528 | tf_op jit(solution)/shard_map/ppermute | solution.py:208
  80.1 9.2 %collective-permute-start.24 = (bf16[2,2,160,256]{3,2,1,0:T(8,128)(2,1)S(1)}, bf16[2,2,160,256]{3,2,1,0:T(8,128)(2,1)S(1)}, u32[]{:S(2)}, u32[]{:S(2)}) collective-permute-start(bf16[2,2,160,256]{3,2,1,0:T(8,128)(2,1)S(1)} %pad_maximum_fusion.6), channel_id=1, source_target_pairs={{0,8},{4,12},{8,0},{12,4},{16,24},{20,28},{24,16},{28,20},{1,9},{5... | collective-permute-start | bytes 983048 | tf_op jit(solution)/shard_map/ppermute | solution.py:208
  81.7 8.7 %collective-permute-start.25 = (bf16[2,2,160,256]{3,2,1,0:T(8,128)(2,1)S(1)}, bf16[2,2,160,256]{3,2,1,0:T(8,128)(2,1)S(1)}, u32[]{:S(2)}, u32[]{:S(2)}) collective-permute-start(bf16[2,2,160,256]{3,2,1,0:T(8,128)(2,1)S(1)} %pad_maximum_fusion.7), channel_id=1, source_target_pairs={{0,16},{4,20},{8,24},{12,28},{16,0},{20,4},{24,8},{28,12},{1,17},{... | collective-permute-start | bytes 983048 | tf_op jit(solution)/shard_map/ppermute | solution.py:208
  82.4 4.6 %collective-permute-start.33 = (bf16[160,256]{1,0:T(8,128)(2,1)S(1)}, bf16[160,256]{1,0:T(8,128)(2,1)S(1)}, u32[]{:S(2)}, u32[]{:S(2)}) collective-permute-start(bf16[160,256]{1,0:T(8,128)(2,1)S(1)} %get-tuple-element.142), channel_id=1, source_target_pairs={{0,1},{1,0},{2,3},{3,2},{4,5},{5,4},{6,7},{7,6},{8,9},{9,8},{10,11... | collective-permute-start | bytes 245768 | tf_op jit(solution)/shard_map/ppermute | solution.py:208
  82.5 8.6 %collective-permute-start.34 = (bf16[160,256]{1,0:T(8,128)(2,1)S(1)}, bf16[160,256]{1,0:T(8,128)(2,1)S(1)}, u32[]{:S(2)}, u32[]{:S(2)}) collective-permute-start(bf16[160,256]{1,0:T(8,128)(2,1)S(1)} %get-tuple-element.141), channel_id=1, source_target_pairs={{0,2},{1,3},{2,0},{3,1},{4,6},{5,7},{6,4},{7,5},{8,10},{9,11},{10,... | collective-permute-start | bytes 245768 | tf_op jit(solution)/shard_map/ppermute | solution.py:208
  85.0 6.3 %collective-permute-start.35 = (bf16[160,256]{1,0:T(8,128)(2,1)S(1)}, bf16[160,256]{1,0:T(8,128)(2,1)S(1)}, u32[]{:S(2)}, u32[]{:S(2)}) collective-permute-start(bf16[160,256]{1,0:T(8,128)(2,1)S(1)} %get-tuple-element.140), channel_id=1, source_target_pairs={{0,3},{1,2},{2,1},{3,0},{4,7},{5,6},{6,5},{7,4},{8,11},{9,10},{10,... | collective-permute-start | bytes 245768 | tf_op jit(solution)/shard_map/ppermute | solution.py:208
  90.5 5.4 %collective-permute-start.27 = (bf16[2,160,256]{2,1,0:T(8,128)(2,1)S(1)}, bf16[2,160,256]{2,1,0:T(8,128)(2,1)S(1)}, u32[]{:S(2)}, u32[]{:S(2)}) collective-permute-start(bf16[2,160,256]{2,1,0:T(8,128)(2,1)S(1)} %get-tuple-element.131), channel_id=1, source_target_pairs={{0,8},{4,12},{8,0},{12,4},{16,24},{20,28},{24,16},{28,20},{1,9},{5... | collective-permute-start | bytes 491528 | tf_op jit(solution)/shard_map/ppermute | solution.py:208
  91.4 5.4 %collective-permute-start.26 = (bf16[2,160,256]{2,1,0:T(8,128)(2,1)S(1)}, bf16[2,160,256]{2,1,0:T(8,128)(2,1)S(1)}, u32[]{:S(2)}, u32[]{:S(2)}) collective-permute-start(bf16[2,160,256]{2,1,0:T(8,128)(2,1)S(1)} %get-tuple-element.130), channel_id=1, source_target_pairs={{0,16},{4,20},{8,24},{12,28},{16,0},{20,4},{24,8},{28,12},{1,17},{... | collective-permute-start | bytes 491528 | tf_op jit(solution)/shard_map/ppermute | solution.py:208
  96.9 5.0 %collective-permute-start.28 = (bf16[160,256]{1,0:T(8,128)(2,1)S(1)}, bf16[160,256]{1,0:T(8,128)(2,1)S(1)}, u32[]{:S(2)}, u32[]{:S(2)}) collective-permute-start(bf16[160,256]{1,0:T(8,128)(2,1)S(1)} %get-tuple-element.145), channel_id=1, source_target_pairs={{0,1},{1,0},{2,3},{3,2},{4,5},{5,4},{6,7},{7,6},{8,9},{9,8},{10,11... | collective-permute-start | bytes 245768 | tf_op jit(solution)/shard_map/ppermute | solution.py:208
  98.2 6.3 %collective-permute-start.29 = (bf16[160,256]{1,0:T(8,128)(2,1)S(1)}, bf16[160,256]{1,0:T(8,128)(2,1)S(1)}, u32[]{:S(2)}, u32[]{:S(2)}) collective-permute-start(bf16[160,256]{1,0:T(8,128)(2,1)S(1)} %get-tuple-element.144), channel_id=1, source_target_pairs={{0,2},{1,3},{2,0},{3,1},{4,6},{5,7},{6,4},{7,5},{8,10},{9,11},{10,... | collective-permute-start | bytes 245768 | tf_op jit(solution)/shard_map/ppermute | solution.py:208
  99.6 6.3 %collective-permute-start.30 = (bf16[160,256]{1,0:T(8,128)(2,1)S(1)}, bf16[160,256]{1,0:T(8,128)(2,1)S(1)}, u32[]{:S(2)}, u32[]{:S(2)}) collective-permute-start(bf16[160,256]{1,0:T(8,128)(2,1)S(1)} %get-tuple-element.143), channel_id=1, source_target_pairs={{0,3},{1,2},{2,1},{3,0},{4,7},{5,6},{6,5},{7,4},{8,11},{9,10},{10,... | collective-permute-start | bytes 245768 | tf_op jit(solution)/shard_map/ppermute | solution.py:208
  (9 other events, 51.1 us)

commit v5 on v4

--- a/solution.py
+++ b/solution.py
@@ -219,15 +219,18 @@
             buffer[rows_of(ref.shape[1], shard, spot, tokens, me_tp)] = ref[at]
 
 
-def write_sums(acc, out_refs, tokens, me_tp, scale):
+def write_sums(accs, out_refs, tokens, me_tp, scale):
     near_ref, far_ref = out_refs
     for k in range(near_ref.shape[0]):
         for ref, shard in ((far_ref.at[k], 2 * k + 1), (near_ref.at[k], 2 * k)):
             for spot in range(ref.shape[0]):
-                part = acc[rows_of(ref.shape[1], shard, spot, tokens, me_tp)]
-                if scale is not None:
-                    part = part * scale
-                ref[spot] = part.astype(ref.dtype)
+                rows = rows_of(ref.shape[1], shard, spot, tokens, me_tp)
+                for at, acc in enumerate(accs):
+                    part = acc[rows]
+                    if scale is not None:
+                        part = part * scale
+                    lanes = slice(at * part.shape[1], (at + 1) * part.shape[1])
+                    ref[spot, :, lanes] = part.astype(ref.dtype)
 
 
 def block_of(place_ref, entry):
@@ -275,7 +278,7 @@
 
 def first_exps_kernel(pieces, dims, tokens, place_ref, tp_ref, query_hbm, grad_hbm, *refs):
     count = len(pieces)
-    exp_ref, grad_t_ref, inv_ref, buffer, query, grad, score_ref, sems = refs[count:]
+    exp_ref, grad_t_ref, inv_ref, acc, buffer, query, grad, score_ref, sems = refs[count:]
     copies = []
     for head in range(dims.heads):
         for source, target in ((query_hbm, query), (grad_hbm, grad)):
@@ -287,12 +290,21 @@
     place_pieces(refs[:count], pieces, tokens, tp_ref[0], buffer)
     copies[0].wait()
     copies[1].wait()
-    exps_kernel(0, dims, place_ref, query, grad, buffer, exp_ref, grad_t_ref, inv_ref, score_ref)
+    exp_rows(0, dims, place_ref, query, grad, buffer, exp_ref, grad_t_ref, inv_ref, score_ref)
+    add_values(acc, dims, place_ref, exp_ref, grad_t_ref)
     for copy in copies[2:]:
         copy.wait()
 
 
-def exps_kernel(head, dims, place_ref, query, grad, buffer, exp_ref, grad_t_ref, inv_ref, score_ref):
+def exps_kernel(head, dims, tokens, place_ref, tp_ref, query, grad, buffer, *refs):
+    accs, refs = refs[:head], refs[head:]
+    exp_ref, grad_t_ref, inv_ref, *sum_refs, acc, score_ref = refs
+    exp_rows(head, dims, place_ref, query, grad, buffer, exp_ref, grad_t_ref, inv_ref, score_ref)
+    add_values(acc, dims, place_ref, exp_ref, grad_t_ref)
+    write_sums([*accs, acc], sum_refs, tokens, tp_ref[0], None)
+
+
+def exp_rows(head, dims, place_ref, query, grad, buffer, exp_ref, grad_t_ref, inv_ref, score_ref):
     factor = LOG2E * float(HD) ** (-0.5)
     lanes = dims.lanes(head)
     tops = {}
@@ -321,22 +333,13 @@
             grad_t_ref[second] = (grad_t * inverse).astype(jnp.bfloat16)
 
 
-def values_kernel(dims, tokens, place_ref, tp_ref, *refs):
-    exp_refs, grad_t_refs = refs[: dims.heads], refs[dims.heads : 2 * dims.heads]
-    out_refs, acc = refs[2 * dims.heads : -1], refs[-1]
+def add_values(acc, dims, place_ref, exp_ref, grad_t_ref):
     acc[...] = jnp.zeros_like(acc)
     for row in range(dims.blocks):
-        for head in range(dims.heads):
-            for column, chunk in dims.chunks():
-                acc[block_of(place_ref, dims.entry(row, column)), dims.lanes(head)] += (
-                    lax.dot_general(
-                        exp_refs[head][row, chunk],
-                        grad_t_refs[head][row],
-                        NT,
-                        preferred_element_type=jnp.float32,
-                    )
-                )
-    write_sums(acc, out_refs, tokens, tp_ref[0], None)
+        for column, chunk in dims.chunks():
+            acc[block_of(place_ref, dims.entry(row, column))] += lax.dot_general(
+                exp_ref[row, chunk], grad_t_ref[row], NT, preferred_element_type=jnp.float32
+            )
 
 
 def add_keys(acc, dims, place_ref, row, head, ds_ref, query):
@@ -395,7 +398,7 @@
         dims.heads - 1, dims, place_ref, exp_ref, grad_t_ref, inv_ref, buffer, out_ref, ds_ref,
         listed, then,
     )
-    write_sums(acc, sum_refs, tokens, tp_ref[0], float(HD) ** (-0.5))
+    write_sums([acc], sum_refs, tokens, tp_ref[0], float(HD) ** (-0.5))
 
 
 def rows_kernel(dims, place_ref, buffer_ref, *refs):
@@ -419,11 +422,11 @@
     me = lax.axis_index("tp")
     count = lax.axis_size("tp")
     width = rows.shape[1] // count
-    parts = []
-    for mask in range(count):
+    parts = {}
+    for mask in reversed(range(count)):
         part = lax.dynamic_slice_in_dim(rows, (me ^ mask) * width, width, 1)
-        parts.append(part if mask == 0 else swap(part, "tp", mask))
-    return jnp.stack(parts)
+        parts[mask] = part if mask == 0 else swap(part, "tp", mask)
+    return jnp.stack([parts[mask] for mask in range(count)])
 
 
 def to_quarters(pieces):
@@ -448,27 +451,25 @@
     return swap(own, "ctx", 2), swap(own, "ctx", 4)
 
 
-def with_diagonal(along_half, across_half):
-    return swap(along_half, "ctx", 2), swap(across_half, "ctx", 4)
-
-
-def to_diagonal(near, got):
-    half = near.shape[1] // 2
-    to_x = jnp.stack([near[3, :half] + got[3, :half], near[1, :half] + got[1, :half]])
-    to_y = jnp.stack([near[3, half:] + got[3, half:], near[2, half:] + got[2, half:]])
+def swap_diagonal(value):
+    count = lax.axis_size("ctx")
+    return lax.ppermute(value, "ctx", [(i, i ^ (4 if i % 2 else 2)) for i in range(count)])
+
+
+def pick(first, second):
+    odd = lax.axis_index("ctx") % 2 == 1
+    return jnp.where(odd, second, first)
+
+
+def to_neighbours(near, got, diagonal):
+    nothing = jnp.zeros_like(diagonal)
+    to_x = near[1] + got[1] + pick(nothing, diagonal)
+    to_y = near[2] + got[2] + pick(diagonal, nothing)
     return to_x, to_y
 
 
-def send_near(near, got, from_x, from_y):
-    half = near.shape[1] // 2
-    more_b = swap(near[1, half:] + got[1, half:] + from_y[0], "ctx", 2)
-    more_a = swap(near[2, :half] + got[2, :half] + from_x[0], "ctx", 4)
-    return more_a, more_b
-
-
-def total_own(near, got, from_x, from_y, more_a, more_b):
-    own = near[0] + got[0]
-    return own + jnp.concatenate([from_x[1] + more_a, from_y[1] + more_b], axis=0)
+def total_own(near, got, from_x, from_y):
+    return near[0] + got[0] + from_x + from_y
 
 
 def dense_plan(queries, key_rows, value_rows, out_grad, block_list):
@@ -486,10 +487,8 @@
     places = ((block_list // blocks) ^ me_ctx) * blocks + block_list % blocks
     places = places.reshape(-1)
     quarter = tokens // quarters
-    half = quarters // 2
-    pieces = [((shard,), 0, quarters) for shard in (0, 2, 4)]
-    pieces += [((6,), 0, half), ((6,), half, half), ((1, 3, 5), 0, quarters)]
-    pieces += [((7,), 0, half), ((7,), half, half)]
+    pieces = [((shard,), 0, quarters) for shard in (0, 2, 4, 6)]
+    pieces += [((1, 3, 5), 0, quarters), ((7,), 0, quarters)]
     dims = Shape(blocks, width, heads, group)
     list_len = width * BLK
     query_rows = group * BLK
@@ -511,6 +510,8 @@
     one_head = shape((tokens, group * HD), bf16)
     two_rows = pltpu.VMEM((2, list_len, query_rows), jnp.float32)
     total = pltpu.VMEM((rows, head_width), jnp.float32)
+    head_sum = shape((rows, HD), jnp.float32)
+    head_total = pltpu.VMEM((rows, HD), jnp.float32)
     listed = pltpu.VMEM((2, list_len, HD), bf16)
     sem = pltpu.SemaphoreType.DMA
 
@@ -530,43 +531,35 @@
     key_x, key_y = with_near(key_own)
     value_own = to_head_groups(value_rows)
     key_x, key_y, key_own, value_own = cut(key_x, key_y, key_own, value_own)
-    key_y1, key_x2, key_three = cut(
-        key_y[:half], key_x[half:], jnp.concatenate([key_own, key_x, key_y])
-    )
-    key_d1, key_d2 = with_diagonal(key_y1, key_x2)
-    key_d1, key_d2, key_three = cut(key_d1, key_d2, key_three)
-    keys = [key_own, key_x, key_y, key_d1, key_d2]
-    keys += [swap(part, "ctx", 1) for part in (key_three, key_d1, key_d2)]
-    value_x, value_y = with_near(held_until(value_own, key_d1))
-
-    exp_0, grad_0, inverse_0, keys_in_order, query_here, grad_here = call(
+    key_next, key_three = cut(pick(key_y, key_x), jnp.concatenate([key_own, key_x, key_y]))
+    key_diag, key_three = cut(swap_diagonal(key_next), key_three)
+    keys = [key_own, key_x, key_y, key_diag]
+    keys += [swap(part, "ctx", 1) for part in (key_three, key_diag)]
+    value_x, value_y = with_near(held_until(value_own, key_diag))
+
+    exp_0, grad_0, inverse_0, sum_0, keys_in_order, query_here, grad_here = call(
         "exps_0", functools.partial(first_exps_kernel, pieces, dims, tokens),
-        [stash, grads, inverses, ordered, flat, flat], [two_rows, sem((2 * heads,))],
+        [stash, grads, inverses, head_sum, ordered, flat, flat], [two_rows, sem((2 * heads,))],
         (places, me_tp), (queries, out_grad, *keys),
     )
     value_x, value_y, inverse_0 = cut(value_x, value_y, inverse_0)
-    value_y1, value_x2, value_three, places_1 = cut(
-        value_y[:half], value_x[half:], jnp.concatenate([value_own, value_x, value_y]), places
-    )
-    value_d1, value_d2 = with_diagonal(value_y1, value_x2)
+    value_next, value_three, places_1 = cut(
+        pick(value_y, value_x), jnp.concatenate([value_own, value_x, value_y]), places
+    )
+    value_diag = swap_diagonal(value_next)
     value_far = swap(value_three, "ctx", 1)
-    exps, grad_ts, inverse = [exp_0], [grad_0], [inverse_0]
-    for head in range(1, heads):
-        made = call(
-            "exps", functools.partial(exps_kernel, head, dims),
-            [stash, grads, inverses], [two_rows], (places_1,),
-            (query_here, grad_here, keys_in_order),
-        )
-        for kept, new in zip((exps, grad_ts, inverse), made):
-            kept.append(new)
-    value_d1, value_d2, value_far, inverse[-1] = cut(value_d1, value_d2, value_far, inverse[-1])
-    values = [value_own, value_x, value_y, value_d1, value_d2, value_far]
-    values += [swap(part, "ctx", 1) for part in (value_d1, value_d2)]
-    value_near, value_away = call(
-        "value_sums", functools.partial(values_kernel, dims, tokens),
-        sums, [total], (held_until(places, inverse[-1]), me_tp), (*exps, *grad_ts),
-    )
-    value_near, value_away, places_2, *values[-2:] = cut(value_near, value_away, places, *values[-2:])
+    exp_1, grad_1, inverse_1, value_near, value_away = call(
+        "exps", functools.partial(exps_kernel, 1, dims, tokens),
+        [stash, grads, inverses, *sums], [head_total, two_rows], (places_1, me_tp),
+        (query_here, grad_here, keys_in_order, sum_0),
+    )
+    exps, grad_ts, inverse = (exp_0, exp_1), (grad_0, grad_1), (inverse_0, inverse_1)
+    value_diag, value_far, value_near, value_away = cut(
+        value_diag, value_far, value_near, value_away
+    )
+    value_last = swap(value_diag, "ctx", 1)
+    value_away, places_2, value_last = cut(value_away, places, value_last)
+    values = [value_own, value_x, value_y, value_diag, value_far, value_last]
     value_got = swap(value_away, "ctx", 1)
     ds, token, attended = [], None, []
     for head in range(heads - 1):
@@ -578,9 +571,8 @@
         attended.append(out)
         ds.append(made)
     value_got, token = cut(value_got, token)
-    to_x, to_y = to_diagonal(value_near, value_got)
-    to_x, to_y, places_3 = cut(to_x, to_y, held_until(places, token))
-    value_first = swap(to_x, "ctx", 2), swap(to_y, "ctx", 4)
+    diagonal, places_3 = cut(value_near[3] + value_got[3], held_until(places, token))
+    value_first = swap_diagonal(diagonal)
     out, made, key_near, key_away = call(
         "key_sums", functools.partial(keys_kernel, dims, tokens),
         [one_head, stash, *sums], [total, listed], (places_3, me_tp),
@@ -588,22 +580,25 @@
     )
     attended.append(out)
     ds.append(made)
-    key_near, key_away, places_4, *value_first = cut(key_near, key_away, places, *value_first)
+    key_near, key_away, places_4, value_first = cut(key_near, key_away, places, value_first)
     key_got = swap(key_away, "ctx", 1)
-    value_more = send_near(value_near, value_got, *value_first)
+    to_x, to_y = to_neighbours(value_near, value_got, value_first)
+    value_more = swap(to_x, "ctx", 2), swap(to_y, "ctx", 4)
     query_grad, token = call(
         "query_grad", functools.partial(rows_kernel, dims),
         [flat, flag], [listed], (places_4,), (keys_in_order, *ds),
     )
     key_got, token = cut(key_got, token)
-    to_x, to_y = cut(*to_diagonal(key_near, key_got))
-    key_first = swap(to_x, "ctx", 2), swap(to_y, "ctx", 4)
-    attended = jnp.concatenate(cut(*attended, to_x, to_y)[:heads], axis=1)
-    value_sum = total_own(value_near, value_got, *value_first, *value_more)
-    value_grad = to_quarters(held_until(value_sum, attended))
-    key_first = cut(*key_first, attended)[:2]
-    key_more = send_near(key_near, key_got, *key_first)
-    key_sum = total_own(key_near, key_got, *key_first, *key_more)
+    diagonal = held_until(key_near[3] + key_got[3], token)
+    key_first = swap_diagonal(diagonal)
+    attended = jnp.concatenate(cut(*attended, diagonal)[:heads], axis=1)
+    attended, *value_more = cut(attended, *value_more)
+    value_sum = total_own(value_near, value_got, *value_more)
+    key_first, attended = cut(key_first, attended)
+    to_x, to_y = to_neighbours(key_near, key_got, key_first)
+    value_grad = to_quarters(value_sum)
+    key_more = swap(to_x, "ctx", 2), swap(to_y, "ctx", 4)
+    key_sum = total_own(key_near, key_got, *key_more)
     return attended, query_grad, to_quarters(key_sum), value_grad
 
 

time: 107 us -> 102 us (0.953)
  waiting for transfers between devices: 38 us -> 34.9 us
  starting transfers between devices: 34.7 us -> 32.6 us
  other arithmetic: 1.85 us -> 2.97 us
    ppermute x36 -> x26, waiting for transfers between devices: 38 us -> 28 us  [swap(): return lax.ppermute(value, axis, [(i, i ^ mask) for i in range(count)])]
    ppermute x0 -> x4, waiting for transfers between devices: none -> 6.87 us  [swap_diagonal(): lax.ppermute(value, 'ctx', [(i, i ^ (4 if i % 2 else 2)) for i in range(c...]
    ppermute x36 -> x26, starting transfers between devices: 34.7 us -> 29.5 us  [swap(): return lax.ppermute(value, axis, [(i, i ^ mask) for i in range(count)])]
    ppermute x0 -> x4, starting transfers between devices: none -> 3.11 us  [swap_diagonal(): lax.ppermute(value, 'ctx', [(i, i ^ (4 if i % 2 else 2)) for i in range(c...]
    concatenate x0 -> x1, other arithmetic: none -> 1.25 us  [dense_plan(): attended = jnp.concatenate(cut(*attended, diagonal)[:heads], axis=1)]
    pallas_call x6 -> x5, Pallas kernels: 28.8 us -> 27.9 us  [call(): pl.pallas_call(kernel, in_specs=[in_smem] * len(scalars) + [in_hbm if x i...]
  transfers between devices with their start and end apart: 36 -> 30, of which waited for: 23 -> 17; matrix products, arithmetic and copies ran while one was open for 1% -> 2% of each run, Pallas kernels for 27% -> 28%
where the time goes in v5:
time: 102 us; the launch traced here: 101 us
  waiting for transfers between devices  34.9 us (34%)
  starting transfers between devices  32.6 us (32%)
  Pallas kernels  27.9 us (27%)
  other arithmetic  2.97 us (3%)
  local copies, waits for them, and re-layouts  2.12 us (2%)
    ppermute x26, starting transfers between devices, swap(): return lax.ppermute(value, axis, [(i, i ^ mask) for i in range(count)])  29.5 us
    ppermute x26, waiting for transfers between devices, swap(): return lax.ppermute(value, axis, [(i, i ^ mask) for i in range(count)])  28 us
    pallas_call x5, Pallas kernels, call(): pl.pallas_call(kernel, in_specs=[in_smem] * len(scalars) + [in_hbm if x i...  27.9 us
    ppermute x4, waiting for transfers between devices, swap_diagonal(): lax.ppermute(value, 'ctx', [(i, i ^ (4 if i % 2 else 2)) for i in range(c...  6.87 us
    ppermute x4, starting transfers between devices, swap_diagonal(): lax.ppermute(value, 'ctx', [(i, i ^ (4 if i % 2 else 2)) for i in range(c...  3.11 us
  transfers between devices with their start and end apart: 30, of which 17 were waited for; matrix products, arithmetic and copies ran while one was open for 2% of the time, Pallas kernels for 28%

profile of v5, /device:TPU:0, one launch (start us, length us, event | category | flops | bytes accessed | tf_op | source)
XLA Modules:
  0.0 101.4 jit_solution(8113079638869902266)
XLA Ops:
  1.7 3.1 %collective-permute-start = (bf16[160,256]{1,0:T(8,128)(2,1)S(1)}, bf16[160,256]{1,0:T(8,128)(2,1)S(1)}, u32[]{:S(2)}, u32[]{:S(2)}) collective-permute-start(bf16[160,256]{1,0:T(8,128)(2,1)S(1)} %get-tuple-element.129), channel_id=1, source_target_pairs={{0,1},{1,0},{2,3},{3,2},{4,5},{5,4},{6,7},{7,6},{8,9},{9,8},{10,11... | collective-permute-start | bytes 245768 | tf_op jit(solution)/shard_map/ppermute | solution.py:208
  4.8 2.6 %collective-permute-start.1 = (bf16[160,256]{1,0:T(8,128)(2,1)S(1)}, bf16[160,256]{1,0:T(8,128)(2,1)S(1)}, u32[]{:S(2)}, u32[]{:S(2)}) collective-permute-start(bf16[160,256]{1,0:T(8,128)(2,1)S(1)} %get-tuple-element.131), channel_id=1, source_target_pairs={{0,2},{1,3},{2,0},{3,1},{4,6},{5,7},{6,4},{7,5},{8,10},{9,11},{10,... | collective-permute-start | bytes 245768 | tf_op jit(solution)/shard_map/ppermute | solution.py:208
  7.4 6.6 %collective-permute-done.1 = bf16[160,256]{1,0:T(8,128)(2,1)S(1)} collective-permute-done((bf16[160,256]{1,0:T(8,128)(2,1)S(1)}, bf16[160,256]{1,0:T(8,128)(2,1)S(1)}, u32[]{:S(2)}, u32[]{:S(2)}) %collective-permute-start.1) | collective-permute-done | bytes 81952 | tf_op jit(solution)/shard_map/ppermute | solution.py:208
  14.1 1.6 %collective-permute-start.3 = (bf16[4,160,256]{2,1,0:T(8,128)(2,1)S(1)}, bf16[4,160,256]{2,1,0:T(8,128)(2,1)S(1)}, u32[]{:S(2)}, u32[]{:S(2)}) collective-permute-start(bf16[4,160,256]{2,1,0:T(8,128)(2,1)S(1)} %pad_maximum_fusion.3.refs_0_), channel_id=1, source_target_pairs={{0,8},{4,12},{8,0},{12,4},{16,24},{20,28},{24,16},{28,20},{1,9},{5... | collective-permute-start | bytes 983048 | tf_op jit(solution)/shard_map/ppermute | solution.py:208
  15.6 1.5 %collective-permute-start.4 = (bf16[4,160,256]{2,1,0:T(8,128)(2,1)S(1)}, bf16[4,160,256]{2,1,0:T(8,128)(2,1)S(1)}, u32[]{:S(2)}, u32[]{:S(2)}) collective-permute-start(bf16[4,160,256]{2,1,0:T(8,128)(2,1)S(1)} %pad_maximum_fusion.3.refs_0_), channel_id=1, source_target_pairs={{0,16},{4,20},{8,24},{12,28},{16,0},{20,4},{24,8},{28,12},{1,17},{... | collective-permute-start | bytes 983048 | tf_op jit(solution)/shard_map/ppermute | solution.py:208
  17.2 1.5 %collective-permute-start.5 = (bf16[160,256]{1,0:T(8,128)(2,1)S(1)}, bf16[160,256]{1,0:T(8,128)(2,1)S(1)}, u32[]{:S(2)}, u32[]{:S(2)}) collective-permute-start(bf16[160,256]{1,0:T(8,128)(2,1)S(1)} %get-tuple-element.125), channel_id=1, source_target_pairs={{0,1},{1,0},{2,3},{3,2},{4,5},{5,4},{6,7},{7,6},{8,9},{9,8},{10,11... | collective-permute-start | bytes 245768 | tf_op jit(solution)/shard_map/ppermute | solution.py:208
  18.7 1.6 %collective-permute-start.6 = (bf16[160,256]{1,0:T(8,128)(2,1)S(1)}, bf16[160,256]{1,0:T(8,128)(2,1)S(1)}, u32[]{:S(2)}, u32[]{:S(2)}) collective-permute-start(bf16[160,256]{1,0:T(8,128)(2,1)S(1)} %get-tuple-element.127), channel_id=1, source_target_pairs={{0,2},{1,3},{2,0},{3,1},{4,6},{5,7},{6,4},{7,5},{8,10},{9,11},{10,... | collective-permute-start | bytes 245768 | tf_op jit(solution)/shard_map/ppermute | solution.py:208
  20.3 1.3 %collective-permute-start.7 = (bf16[160,256]{1,0:T(8,128)(2,1)S(1)}, bf16[160,256]{1,0:T(8,128)(2,1)S(1)}, u32[]{:S(2)}, u32[]{:S(2)}) collective-permute-start(bf16[160,256]{1,0:T(8,128)(2,1)S(1)} %get-tuple-element.126), channel_id=1, source_target_pairs={{0,3},{1,2},{2,1},{3,0},{4,7},{5,6},{6,5},{7,4},{8,11},{9,10},{10,... | collective-permute-start | bytes 245768 | tf_op jit(solution)/shard_map/ppermute | solution.py:208
  21.7 3.7 %collective-permute-done.6 = bf16[160,256]{1,0:T(8,128)(2,1)S(1)} collective-permute-done((bf16[160,256]{1,0:T(8,128)(2,1)S(1)}, bf16[160,256]{1,0:T(8,128)(2,1)S(1)}, u32[]{:S(2)}, u32[]{:S(2)}) %collective-permute-start.6) | collective-permute-done | bytes 81952 | tf_op jit(solution)/shard_map/ppermute | solution.py:208
  25.5 1.2 %collective-permute-done.7 = bf16[160,256]{1,0:T(8,128)(2,1)S(1)} collective-permute-done((bf16[160,256]{1,0:T(8,128)(2,1)S(1)}, bf16[160,256]{1,0:T(8,128)(2,1)S(1)}, u32[]{:S(2)}, u32[]{:S(2)}) %collective-permute-start.7) | collective-permute-done | bytes 81952 | tf_op jit(solution)/shard_map/ppermute | solution.py:208
  28.4 6.5 %collective-permute-done.8.refs_3_ = bf16[4,160,256]{2,1,0:T(8,128)(2,1)S(1)} collective-permute-done((bf16[4,160,256]{2,1,0:T(8,128)(2,1)S(1)}, bf16[4,160,256]{2,1,0:T(8,128)(2,1)S(1)}, u32[]{:S(2)}, u32[]{:S(2)}) %collective-permute-start.8) | collective-permute-done | bytes 327712 | tf_op jit(solution)/shard_map/ppermute | solution.py:456
  38.2 7.2 %exps_0.1 = (bf16[5,1024,512]{2,1,0:T(8,128)(2,1)S(1)}, bf16[5,128,512]{2,1,0:T(8,128)(2,1)S(1)}, f32[5,8,512]{2,1,0:T(8,128)S(1)}, f32[5120,128]{1,0:T(8,128)S(...) custom-call(s32[40]{0:T(128)S(1)} %reshape.22.place_ref, ...), custom_call_target="tpu_custom_call" | custom-call | flops 4294967296 | bytes 1048576 | tf_op jit(solution)/shard_map/exps_0/pallas_call | solution.py:519
  46.4 6.2 %exps.1 = (bf16[5,1024,512]{2,1,0:T(8,128)(2,1)S(1)}, bf16[5,128,512]{2,1,0:T(8,128)(2,1)S(1)}, f32[5,8,512]{2,1,0:T(8,128)S(1)}, bf16[4,4,160,256]{3,2,1,0:T(8,128)(2,1)S(1)}, bf16[4,4,160,256]{3,2,1,0:T(8,128)(2,1)S(1)}) custom-call(s32[40]{0:T(128)S(1)} %reshape.22.place_ref, s32[1]{0:T(128)} %bitcast.8.tp_ref, ...), custom_call_target="tpu_custom_call" | custom-call | flops 4294967296 | bytes 1048576 | tf_op jit(solution)/shard_map/exps/pallas_call | solution.py:519
  53.7 1.3 %collective-permute-done.15.refs_5_ = bf16[4,160,256]{2,1,0:T(8,128)(2,1)S(1)} collective-permute-done((bf16[4,160,256]{2,1,0:T(8,128)(2,1)S(1)}, bf16[4,160,256]{2,1,0:T(8,128)(2,1)S(1)}, u32[]{:S(2)}, u32[]{:S(2)}) %collective-permute-start.15) | collective-permute-done | bytes 327712 | tf_op jit(solution)/shard_map/ppermute | solution.py:208
  55.3 4.0 %scores.1 = (bf16[640,512]{1,0:T(8,128)(2,1)S(1)}, bf16[5,1024,512]{2,1,0:T(8,128)(2,1)S(1)}, bf16[5120,256]{1,0:T(8,128)(2,1)S(1)}, f32[8,128]{1,0:T(8,128)}) custom-call(s32[40]{0:T(128)S(1)} %reshape.22.place_ref, s32[1]{0:T(128)} %bitcast.8.tp_ref, bf16[5,1024,512]{2,1,0:T(8,128)(2,1)S(1)} %get-tuple-element.89.exp_ref, ...), custom_call_target="tpu_custom_call" | custom-call | flops 4294967296 | bytes 1048576 | tf_op jit(solution)/shard_map/scores/pallas_call | solution.py:519
  60.0 6.7 %key_sums.1 = (bf16[640,512]{1,0:T(8,128)(2,1)S(1)}, bf16[5,1024,512]{2,1,0:T(8,128)(2,1)S(1)}, bf16[4,4,160,256]{3,2,1,0:T(8,128)(2,1)S(1)}, bf16[4,4,160,256]{3,2,1,0:T(8,128)(2,1)S(1)}) custom-call(s32[40]{0:T(128)S(1)} %reshape.22.place_ref, s32[1]{0:T(128)} %bitcast.8.tp_ref, bf16[5,1024,512]{2,1,0:T(8,128)(2,1)S(1)} %get-tuple-element.85.exp_ref, ...), custom_call_target="tpu_custom_call" | custom-call | flops 4294967296 | bytes 1048576 | tf_op jit(solution)/shard_map/key_sums/pallas_call | solution.py:519
  67.1 1.3 %collective-permute-start.20 = (bf16[4,160,256]{2,1,0:T(8,128)(2,1)S(1)}, bf16[4,160,256]{2,1,0:T(8,128)(2,1)S(1)}, u32[]{:S(2)}, u32[]{:S(2)}) collective-permute-start(bf16[4,160,256]{2,1,0:T(8,128)(2,1)S(1)} %get-tuple-element.117), channel_id=1, source_target_pairs={{0,8},{4,12},{8,0},{12,4},{16,24},{20,28},{24,16},{28,20},{1,9},{5... | collective-permute-start | bytes 983048 | tf_op jit(solution)/shard_map/ppermute | solution.py:208
  69.2 3.8 %query_grad.1 = (bf16[640,1024]{1,0:T(8,128)(2,1)}, f32[8,128]{1,0:T(8,128)}) custom-call(s32[40]{0:T(128)S(1)} %reshape.22.place_ref, bf16[5120,256]{1,0:T(8,128)(2,1)S(1)} %get-tuple-element.76.buffer.buffer_ref, bf16[5,1024,512]{2,1,0:T(8,128)(2,1)S(1)} %get-tuple-element.95.refs_0_, bf16[5,1024,512]{2,1,0:T(8,128)(2,1)S(1)} %get-tuple-element.109.refs_1_), custom_call_target="tpu_custom_call" | custom-call | flops 4294967296 | bytes 1048576 | tf_op jit(solution)/shard_map/query_grad/pallas_call | solution.py:519
  73.0 1.3 %collective-permute-start.19 = (bf16[4,160,256]{2,1,0:T(8,128)(2,1)S(1)}, bf16[4,160,256]{2,1,0:T(8,128)(2,1)S(1)}, u32[]{:S(2)}, u32[]{:S(2)}) collective-permute-start(bf16[4,160,256]{2,1,0:T(8,128)(2,1)S(1)} %fusion.14), channel_id=1, source_target_pairs={{0,8},{4,20},{8,0},{12,28},{16,24},{20,4},{24,16},{28,12},{1,9},{5... | collective-permute-start | bytes 983048 | tf_op jit(solution)/shard_map/ppermute | solution.py:456
  74.4 1.3 %pad_maximum_fusion = bf16[640,1024]{1,0:T(8,128)(2,1)} fusion(bf16[640,512]{1,0:T(8,128)(2,1)S(1)} %get-tuple-element.104, bf16[640,512]{1,0:T(8,128)(2,1)S(1)} %get-tuple-element.103), kind=kLoop, calls=%fused_computation | loop fusion | flops 2621440 | bytes 2621440 | tf_op jit(solution)/shard_map/concatenate | solution.py:594
  75.6 1.5 %collective-permute-done.20 = bf16[4,160,256]{2,1,0:T(8,128)(2,1)S(1)} collective-permute-done((bf16[4,160,256]{2,1,0:T(8,128)(2,1)S(1)}, bf16[4,160,256]{2,1,0:T(8,128)(2,1)S(1)}, u32[]{:S(2)}, u32[]{:S(2)}) %collective-permute-start.20) | collective-permute-done | bytes 327712 | tf_op jit(solution)/shard_map/ppermute | solution.py:208
  77.1 1.9 %collective-permute-done.21 = bf16[4,160,256]{2,1,0:T(8,128)(2,1)S(1)} collective-permute-done((bf16[4,160,256]{2,1,0:T(8,128)(2,1)S(1)}, bf16[4,160,256]{2,1,0:T(8,128)(2,1)S(1)}, u32[]{:S(2)}, u32[]{:S(2)}) %collective-permute-start.21) | collective-permute-done | bytes 327712 | tf_op jit(solution)/shard_map/ppermute | solution.py:208
  79.1 1.2 %collective-permute-start.27 = (bf16[160,256]{1,0:T(8,128)(2,1)S(1)}, bf16[160,256]{1,0:T(8,128)(2,1)S(1)}, u32[]{:S(2)}, u32[]{:S(2)}) collective-permute-start(bf16[160,256]{1,0:T(8,128)(2,1)S(1)} %get-tuple-element.120), channel_id=1, source_target_pairs={{0,1},{1,0},{2,3},{3,2},{4,5},{5,4},{6,7},{7,6},{8,9},{9,8},{10,11... | collective-permute-start | bytes 245768 | tf_op jit(solution)/shard_map/ppermute | solution.py:208
  80.3 1.2 %collective-permute-start.28 = (bf16[160,256]{1,0:T(8,128)(2,1)S(1)}, bf16[160,256]{1,0:T(8,128)(2,1)S(1)}, u32[]{:S(2)}, u32[]{:S(2)}) collective-permute-start(bf16[160,256]{1,0:T(8,128)(2,1)S(1)} %get-tuple-element.119), channel_id=1, source_target_pairs={{0,2},{1,3},{2,0},{3,1},{4,6},{5,7},{6,4},{7,5},{8,10},{9,11},{10,... | collective-permute-start | bytes 245768 | tf_op jit(solution)/shard_map/ppermute | solution.py:208
  81.5 2.0 %collective-permute-start.29 = (bf16[160,256]{1,0:T(8,128)(2,1)S(1)}, bf16[160,256]{1,0:T(8,128)(2,1)S(1)}, u32[]{:S(2)}, u32[]{:S(2)}) collective-permute-start(bf16[160,256]{1,0:T(8,128)(2,1)S(1)} %get-tuple-element.118), channel_id=1, source_target_pairs={{0,3},{1,2},{2,1},{3,0},{4,7},{5,6},{6,5},{7,4},{8,11},{9,10},{10,... | collective-permute-start | bytes 245768 | tf_op jit(solution)/shard_map/ppermute | solution.py:208
  85.8 2.5 %collective-permute-done.28 = bf16[160,256]{1,0:T(8,128)(2,1)S(1)} collective-permute-done((bf16[160,256]{1,0:T(8,128)(2,1)S(1)}, bf16[160,256]{1,0:T(8,128)(2,1)S(1)}, u32[]{:S(2)}, u32[]{:S(2)}) %collective-permute-start.28) | collective-permute-done | bytes 81952 | tf_op jit(solution)/shard_map/ppermute | solution.py:208
  88.3 3.1 %collective-permute-done.22 = bf16[4,160,256]{2,1,0:T(8,128)(2,1)S(1)} collective-permute-done((bf16[4,160,256]{2,1,0:T(8,128)(2,1)S(1)}, bf16[4,160,256]{2,1,0:T(8,128)(2,1)S(1)}, u32[]{:S(2)}, u32[]{:S(2)}) %collective-permute-start.22) | collective-permute-done | bytes 327712 | tf_op jit(solution)/shard_map/ppermute | solution.py:208
  91.8 1.2 %collective-permute-start.24 = (bf16[160,256]{1,0:T(8,128)(2,1)S(1)}, bf16[160,256]{1,0:T(8,128)(2,1)S(1)}, u32[]{:S(2)}, u32[]{:S(2)}) collective-permute-start(bf16[160,256]{1,0:T(8,128)(2,1)S(1)} %get-tuple-element.123), channel_id=1, source_target_pairs={{0,1},{1,0},{2,3},{3,2},{4,5},{5,4},{6,7},{7,6},{8,9},{9,8},{10,11... | collective-permute-start | bytes 245768 | tf_op jit(solution)/shard_map/ppermute | solution.py:208
  93.0 1.3 %collective-permute-start.25 = (bf16[160,256]{1,0:T(8,128)(2,1)S(1)}, bf16[160,256]{1,0:T(8,128)(2,1)S(1)}, u32[]{:S(2)}, u32[]{:S(2)}) collective-permute-start(bf16[160,256]{1,0:T(8,128)(2,1)S(1)} %get-tuple-element.122), channel_id=1, source_target_pairs={{0,2},{1,3},{2,0},{3,1},{4,6},{5,7},{6,4},{7,5},{8,10},{9,11},{10,... | collective-permute-start | bytes 245768 | tf_op jit(solution)/shard_map/ppermute | solution.py:208
  94.3 2.0 %collective-permute-start.26 = (bf16[160,256]{1,0:T(8,128)(2,1)S(1)}, bf16[160,256]{1,0:T(8,128)(2,1)S(1)}, u32[]{:S(2)}, u32[]{:S(2)}) collective-permute-start(bf16[160,256]{1,0:T(8,128)(2,1)S(1)} %get-tuple-element.121), channel_id=1, source_target_pairs={{0,3},{1,2},{2,1},{3,0},{4,7},{5,6},{6,5},{7,4},{8,11},{9,10},{10,... | collective-permute-start | bytes 245768 | tf_op jit(solution)/shard_map/ppermute | solution.py:208
  97.4 1.9 %collective-permute-done.25 = bf16[160,256]{1,0:T(8,128)(2,1)S(1)} collective-permute-done((bf16[160,256]{1,0:T(8,128)(2,1)S(1)}, bf16[160,256]{1,0:T(8,128)(2,1)S(1)}, u32[]{:S(2)}, u32[]{:S(2)}) %collective-permute-start.25) | collective-permute-done | bytes 81952 | tf_op jit(solution)/shard_map/ppermute | solution.py:208
  99.3 1.3 %collective-permute-done.26 = bf16[160,256]{1,0:T(8,128)(2,1)S(1)} collective-permute-done((bf16[160,256]{1,0:T(8,128)(2,1)S(1)}, bf16[160,256]{1,0:T(8,128)(2,1)S(1)}, u32[]{:S(2)}, u32[]{:S(2)}) %collective-permute-start.26) | collective-permute-done | bytes 81952 | tf_op jit(solution)/shard_map/ppermute | solution.py:208
  (70 shorter events, 15.0 us)
Async XLA Ops:
  0.6 16.5 %copy-start = (bf16[160,1024]{1,0:T(8,128)(2,1)S(1)}, bf16[160,1024]{1,0:T(8,128)(2,1)}, u32[]{:S(2)}) copy-start(bf16[160,1024]{1,0:T(8,128)(2,1)} %param.7) | copy-start | bytes 983044
  1.7 5.7 %collective-permute-start = (bf16[160,256]{1,0:T(8,128)(2,1)S(1)}, bf16[160,256]{1,0:T(8,128)(2,1)S(1)}, u32[]{:S(2)}, u32[]{:S(2)}) collective-permute-start(bf16[160,256]{1,0:T(8,128)(2,1)S(1)} %get-tuple-element.129), channel_id=1, source_target_pairs={{0,1},{1,0},{2,3},{3,2},{4,5},{5,4},{6,7},{7,6},{8,9},{9,8},{10,11... | collective-permute-start | bytes 245768 | tf_op jit(solution)/shard_map/ppermute | solution.py:208
  4.8 9.2 %collective-permute-start.1 = (bf16[160,256]{1,0:T(8,128)(2,1)S(1)}, bf16[160,256]{1,0:T(8,128)(2,1)S(1)}, u32[]{:S(2)}, u32[]{:S(2)}) collective-permute-start(bf16[160,256]{1,0:T(8,128)(2,1)S(1)} %get-tuple-element.131), channel_id=1, source_target_pairs={{0,2},{1,3},{2,0},{3,1},{4,6},{5,7},{6,4},{7,5},{8,10},{9,11},{10,... | collective-permute-start | bytes 245768 | tf_op jit(solution)/shard_map/ppermute | solution.py:208
  7.4 6.6 %collective-permute-start.2 = (bf16[160,256]{1,0:T(8,128)(2,1)S(1)}, bf16[160,256]{1,0:T(8,128)(2,1)S(1)}, u32[]{:S(2)}, u32[]{:S(2)}) collective-permute-start(bf16[160,256]{1,0:T(8,128)(2,1)S(1)} %get-tuple-element.130), channel_id=1, source_target_pairs={{0,3},{1,2},{2,1},{3,0},{4,7},{5,6},{6,5},{7,4},{8,11},{9,10},{10,... | collective-permute-start | bytes 245768 | tf_op jit(solution)/shard_map/ppermute | solution.py:208
  14.1 12.6 %collective-permute-start.3 = (bf16[4,160,256]{2,1,0:T(8,128)(2,1)S(1)}, bf16[4,160,256]{2,1,0:T(8,128)(2,1)S(1)}, u32[]{:S(2)}, u32[]{:S(2)}) collective-permute-start(bf16[4,160,256]{2,1,0:T(8,128)(2,1)S(1)} %pad_maximum_fusion.3.refs_0_), channel_id=1, source_target_pairs={{0,8},{4,12},{8,0},{12,4},{16,24},{20,28},{24,16},{28,20},{1,9},{5... | collective-permute-start | bytes 983048 | tf_op jit(solution)/shard_map/ppermute | solution.py:208
  15.6 11.1 %collective-permute-start.4 = (bf16[4,160,256]{2,1,0:T(8,128)(2,1)S(1)}, bf16[4,160,256]{2,1,0:T(8,128)(2,1)S(1)}, u32[]{:S(2)}, u32[]{:S(2)}) collective-permute-start(bf16[4,160,256]{2,1,0:T(8,128)(2,1)S(1)} %pad_maximum_fusion.3.refs_0_), channel_id=1, source_target_pairs={{0,16},{4,20},{8,24},{12,28},{16,0},{20,4},{24,8},{28,12},{1,17},{... | collective-permute-start | bytes 983048 | tf_op jit(solution)/shard_map/ppermute | solution.py:208
  17.2 4.5 %collective-permute-start.5 = (bf16[160,256]{1,0:T(8,128)(2,1)S(1)}, bf16[160,256]{1,0:T(8,128)(2,1)S(1)}, u32[]{:S(2)}, u32[]{:S(2)}) collective-permute-start(bf16[160,256]{1,0:T(8,128)(2,1)S(1)} %get-tuple-element.125), channel_id=1, source_target_pairs={{0,1},{1,0},{2,3},{3,2},{4,5},{5,4},{6,7},{7,6},{8,9},{9,8},{10,11... | collective-permute-start | bytes 245768 | tf_op jit(solution)/shard_map/ppermute | solution.py:208
  18.7 6.8 %collective-permute-start.6 = (bf16[160,256]{1,0:T(8,128)(2,1)S(1)}, bf16[160,256]{1,0:T(8,128)(2,1)S(1)}, u32[]{:S(2)}, u32[]{:S(2)}) collective-permute-start(bf16[160,256]{1,0:T(8,128)(2,1)S(1)} %get-tuple-element.127), channel_id=1, source_target_pairs={{0,2},{1,3},{2,0},{3,1},{4,6},{5,7},{6,4},{7,5},{8,10},{9,11},{10,... | collective-permute-start | bytes 245768 | tf_op jit(solution)/shard_map/ppermute | solution.py:208
  20.3 6.3 %collective-permute-start.7 = (bf16[160,256]{1,0:T(8,128)(2,1)S(1)}, bf16[160,256]{1,0:T(8,128)(2,1)S(1)}, u32[]{:S(2)}, u32[]{:S(2)}) collective-permute-start(bf16[160,256]{1,0:T(8,128)(2,1)S(1)} %get-tuple-element.126), channel_id=1, source_target_pairs={{0,3},{1,2},{2,1},{3,0},{4,7},{5,6},{6,5},{7,4},{8,11},{9,10},{10,... | collective-permute-start | bytes 245768 | tf_op jit(solution)/shard_map/ppermute | solution.py:208
  26.7 8.8 %copy-start.3 = (s32[5,8]{1,0:T(8,128)S(1)}, s32[5,8]{1,0:T(8,128)}, u32[]{:S(2)}) copy-start(s32[5,8]{1,0:T(8,128)} %param.9) | copy-start | bytes 484
  27.8 7.1 %collective-permute-start.8 = (bf16[4,160,256]{2,1,0:T(8,128)(2,1)S(1)}, bf16[4,160,256]{2,1,0:T(8,128)(2,1)S(1)}, u32[]{:S(2)}, u32[]{:S(2)}) collective-permute-start(bf16[4,160,256]{2,1,0:T(8,128)(2,1)S(1)} %broadcast_select_fusion.1), channel_id=1, source_target_pairs={{0,8},{4,20},{8,0},{12,28},{16,24},{20,4},{24,16},{28,12},{1,9},{5... | collective-permute-start | bytes 983048 | tf_op jit(solution)/shard_map/ppermute | solution.py:456
  35.0 3.2 %collective-permute-start.11 = (bf16[12,160,256]{2,1,0:T(8,128)(2,1)}, bf16[12,160,256]{2,1,0:T(8,128)(2,1)S(1)}, u32[]{:S(2)}, u32[]{:S(2)}) collective-permute-start(bf16[12,160,256]{2,1,0:T(8,128)(2,1)} %pad_maximum_fusion.1), channel_id=1, source_target_pairs={{0,4},{4,0},{8,12},{12,8},{16,20},{20,16},{24,28},{28,24},{1,5},{5... | collective-permute-start | bytes 2949128 | tf_op jit(solution)/shard_map/ppermute | solution.py:208
  35.0 2.7 %collective-permute-start.12 = (bf16[4,160,256]{2,1,0:T(8,128)(2,1)S(1)}, bf16[4,160,256]{2,1,0:T(8,128)(2,1)S(1)}, u32[]{:S(2)}, u32[]{:S(2)}) collective-permute-start(bf16[4,160,256]{2,1,0:T(8,128)(2,1)S(1)} %collective-permute-done.8.refs_3_), channel_id=1, source_target_pairs={{0,4},{4,0},{8,12},{12,8},{16,20},{20,16},{24,28},{28,24},{1,5},{5... | collective-permute-start | bytes 983048 | tf_op jit(solution)/shard_map/ppermute | solution.py:208
  35.6 9.9 %collective-permute-start.10 = (bf16[4,160,256]{2,1,0:T(8,128)(2,1)S(1)}, bf16[4,160,256]{2,1,0:T(8,128)(2,1)S(1)}, u32[]{:S(2)}, u32[]{:S(2)}) collective-permute-start(bf16[4,160,256]{2,1,0:T(8,128)(2,1)S(1)} %pad_maximum_fusion.4.refs_0_), channel_id=1, source_target_pairs={{0,16},{4,20},{8,24},{12,28},{16,0},{20,4},{24,8},{28,12},{1,17},{... | collective-permute-start | bytes 983048 | tf_op jit(solution)/shard_map/ppermute | solution.py:208
  36.1 9.4 %collective-permute-start.9 = (bf16[4,160,256]{2,1,0:T(8,128)(2,1)S(1)}, bf16[4,160,256]{2,1,0:T(8,128)(2,1)S(1)}, u32[]{:S(2)}, u32[]{:S(2)}) collective-permute-start(bf16[4,160,256]{2,1,0:T(8,128)(2,1)S(1)} %pad_maximum_fusion.4.refs_0_), channel_id=1, source_target_pairs={{0,8},{4,12},{8,0},{12,4},{16,24},{20,28},{24,16},{28,20},{1,9},{5... | collective-permute-start | bytes 983048 | tf_op jit(solution)/shard_map/ppermute | solution.py:208
  45.6 7.3 %collective-permute-start.14 = (bf16[12,160,256]{2,1,0:T(8,128)(2,1)S(1)}, bf16[12,160,256]{2,1,0:T(8,128)(2,1)S(1)}, u32[]{:S(2)}, u32[]{:S(2)}) collective-permute-start(bf16[12,160,256]{2,1,0:T(8,128)(2,1)S(1)} %pad_maximum_fusion.2), channel_id=1, source_target_pairs={{0,4},{4,0},{8,12},{12,8},{16,20},{20,16},{24,28},{28,24},{1,5},{5... | collective-permute-start | bytes 2949128 | tf_op jit(solution)/shard_map/ppermute | solution.py:208
  45.8 7.1 %collective-permute-start.13 = (bf16[4,160,256]{2,1,0:T(8,128)(2,1)S(1)}, bf16[4,160,256]{2,1,0:T(8,128)(2,1)S(1)}, u32[]{:S(2)}, u32[]{:S(2)}) collective-permute-start(bf16[4,160,256]{2,1,0:T(8,128)(2,1)S(1)} %broadcast_select_fusion), channel_id=1, source_target_pairs={{0,8},{4,20},{8,0},{12,28},{16,24},{20,4},{24,16},{28,12},{1,9},{5... | collective-permute-start | bytes 983048 | tf_op jit(solution)/shard_map/ppermute | solution.py:456
  52.9 2.1 %collective-permute-start.15 = (bf16[4,160,256]{2,1,0:T(8,128)(2,1)S(1)}, bf16[4,160,256]{2,1,0:T(8,128)(2,1)S(1)}, u32[]{:S(2)}, u32[]{:S(2)}) collective-permute-start(bf16[4,160,256]{2,1,0:T(8,128)(2,1)S(1)} %collective-permute-done.13.refs_3_), channel_id=1, source_target_pairs={{0,4},{4,0},{8,12},{12,8},{16,20},{20,16},{24,28},{28,24},{1,5},{5... | collective-permute-start | bytes 983048 | tf_op jit(solution)/shard_map/ppermute | solution.py:208
  55.0 4.4 %collective-permute-start.16 = (bf16[4,4,160,256]{3,2,1,0:T(8,128)(2,1)S(1)}, bf16[4,4,160,256]{3,2,1,0:T(8,128)(2,1)S(1)}, u32[]{:S(2)}, u32[]{:S(2)}) collective-permute-start(bf16[4,4,160,256]{3,2,1,0:T(8,128)(2,1)S(1)} %get-tuple-element.83), channel_id=1, source_target_pairs={{0,4},{4,0},{8,12},{12,8},{16,20},{20,16},{24,28},{28,24},{1,5},{5... | collective-permute-start | bytes 3932168 | tf_op jit(solution)/shard_map/ppermute | solution.py:208
  59.4 7.4 %collective-permute-start.17 = (bf16[4,160,256]{2,1,0:T(8,128)(2,1)S(1)}, bf16[4,160,256]{2,1,0:T(8,128)(2,1)S(1)}, u32[]{:S(2)}, u32[]{:S(2)}) collective-permute-start(bf16[4,160,256]{2,1,0:T(8,128)(2,1)S(1)} %fusion.15), channel_id=1, source_target_pairs={{0,8},{4,20},{8,0},{12,28},{16,24},{20,4},{24,16},{28,12},{1,9},{5... | collective-permute-start | bytes 983048 | tf_op jit(solution)/shard_map/ppermute | solution.py:456
  66.7 6.3 %collective-permute-start.18 = (bf16[4,4,160,256]{3,2,1,0:T(8,128)(2,1)S(1)}, bf16[4,4,160,256]{3,2,1,0:T(8,128)(2,1)S(1)}, u32[]{:S(2)}, u32[]{:S(2)}) collective-permute-start(bf16[4,4,160,256]{3,2,1,0:T(8,128)(2,1)S(1)} %get-tuple-element.100), channel_id=1, source_target_pairs={{0,4},{4,0},{8,12},{12,8},{16,20},{20,16},{24,28},{28,24},{1,5},{5... | collective-permute-start | bytes 3932168 | tf_op jit(solution)/shard_map/ppermute | solution.py:208
  67.1 9.9 %collective-permute-start.20 = (bf16[4,160,256]{2,1,0:T(8,128)(2,1)S(1)}, bf16[4,160,256]{2,1,0:T(8,128)(2,1)S(1)}, u32[]{:S(2)}, u32[]{:S(2)}) collective-permute-start(bf16[4,160,256]{2,1,0:T(8,128)(2,1)S(1)} %get-tuple-element.117), channel_id=1, source_target_pairs={{0,8},{4,12},{8,0},{12,4},{16,24},{20,28},{24,16},{28,20},{1,9},{5... | collective-permute-start | bytes 983048 | tf_op jit(solution)/shard_map/ppermute | solution.py:208
  68.5 10.6 %collective-permute-start.21 = (bf16[4,160,256]{2,1,0:T(8,128)(2,1)S(1)}, bf16[4,160,256]{2,1,0:T(8,128)(2,1)S(1)}, u32[]{:S(2)}, u32[]{:S(2)}) collective-permute-start(bf16[4,160,256]{2,1,0:T(8,128)(2,1)S(1)} %get-tuple-element.116), channel_id=1, source_target_pairs={{0,16},{4,20},{8,24},{12,28},{16,0},{20,4},{24,8},{28,12},{1,17},{... | collective-permute-start | bytes 983048 | tf_op jit(solution)/shard_map/ppermute | solution.py:208
  73.0 10.6 %collective-permute-start.19 = (bf16[4,160,256]{2,1,0:T(8,128)(2,1)S(1)}, bf16[4,160,256]{2,1,0:T(8,128)(2,1)S(1)}, u32[]{:S(2)}, u32[]{:S(2)}) collective-permute-start(bf16[4,160,256]{2,1,0:T(8,128)(2,1)S(1)} %fusion.14), channel_id=1, source_target_pairs={{0,8},{4,20},{8,0},{12,28},{16,24},{20,4},{24,16},{28,12},{1,9},{5... | collective-permute-start | bytes 983048 | tf_op jit(solution)/shard_map/ppermute | solution.py:456
  79.1 6.6 %collective-permute-start.27 = (bf16[160,256]{1,0:T(8,128)(2,1)S(1)}, bf16[160,256]{1,0:T(8,128)(2,1)S(1)}, u32[]{:S(2)}, u32[]{:S(2)}) collective-permute-start(bf16[160,256]{1,0:T(8,128)(2,1)S(1)} %get-tuple-element.120), channel_id=1, source_target_pairs={{0,1},{1,0},{2,3},{3,2},{4,5},{5,4},{6,7},{7,6},{8,9},{9,8},{10,11... | collective-permute-start | bytes 245768 | tf_op jit(solution)/shard_map/ppermute | solution.py:208
  80.3 7.9 %collective-permute-start.28 = (bf16[160,256]{1,0:T(8,128)(2,1)S(1)}, bf16[160,256]{1,0:T(8,128)(2,1)S(1)}, u32[]{:S(2)}, u32[]{:S(2)}) collective-permute-start(bf16[160,256]{1,0:T(8,128)(2,1)S(1)} %get-tuple-element.119), channel_id=1, source_target_pairs={{0,2},{1,3},{2,0},{3,1},{4,6},{5,7},{6,4},{7,5},{8,10},{9,11},{10,... | collective-permute-start | bytes 245768 | tf_op jit(solution)/shard_map/ppermute | solution.py:208
  81.5 6.7 %collective-permute-start.29 = (bf16[160,256]{1,0:T(8,128)(2,1)S(1)}, bf16[160,256]{1,0:T(8,128)(2,1)S(1)}, u32[]{:S(2)}, u32[]{:S(2)}) collective-permute-start(bf16[160,256]{1,0:T(8,128)(2,1)S(1)} %get-tuple-element.118), channel_id=1, source_target_pairs={{0,3},{1,2},{2,1},{3,0},{4,7},{5,6},{6,5},{7,4},{8,11},{9,10},{10,... | collective-permute-start | bytes 245768 | tf_op jit(solution)/shard_map/ppermute | solution.py:208
  83.7 7.6 %collective-permute-start.22 = (bf16[4,160,256]{2,1,0:T(8,128)(2,1)S(1)}, bf16[4,160,256]{2,1,0:T(8,128)(2,1)S(1)}, u32[]{:S(2)}, u32[]{:S(2)}) collective-permute-start(bf16[4,160,256]{2,1,0:T(8,128)(2,1)S(1)} %get-tuple-element.114), channel_id=1, source_target_pairs={{0,8},{4,12},{8,0},{12,4},{16,24},{20,28},{24,16},{28,20},{1,9},{5... | collective-permute-start | bytes 983048 | tf_op jit(solution)/shard_map/ppermute | solution.py:208
  84.6 7.1 %collective-permute-start.23 = (bf16[4,160,256]{2,1,0:T(8,128)(2,1)S(1)}, bf16[4,160,256]{2,1,0:T(8,128)(2,1)S(1)}, u32[]{:S(2)}, u32[]{:S(2)}) collective-permute-start(bf16[4,160,256]{2,1,0:T(8,128)(2,1)S(1)} %get-tuple-element.115), channel_id=1, source_target_pairs={{0,16},{4,20},{8,24},{12,28},{16,0},{20,4},{24,8},{28,12},{1,17},{... | collective-permute-start | bytes 983048 | tf_op jit(solution)/shard_map/ppermute | solution.py:208
  91.8 5.7 %collective-permute-start.24 = (bf16[160,256]{1,0:T(8,128)(2,1)S(1)}, bf16[160,256]{1,0:T(8,128)(2,1)S(1)}, u32[]{:S(2)}, u32[]{:S(2)}) collective-permute-start(bf16[160,256]{1,0:T(8,128)(2,1)S(1)} %get-tuple-element.123), channel_id=1, source_target_pairs={{0,1},{1,0},{2,3},{3,2},{4,5},{5,4},{6,7},{7,6},{8,9},{9,8},{10,11... | collective-permute-start | bytes 245768 | tf_op jit(solution)/shard_map/ppermute | solution.py:208
  93.0 6.3 %collective-permute-start.25 = (bf16[160,256]{1,0:T(8,128)(2,1)S(1)}, bf16[160,256]{1,0:T(8,128)(2,1)S(1)}, u32[]{:S(2)}, u32[]{:S(2)}) collective-permute-start(bf16[160,256]{1,0:T(8,128)(2,1)S(1)} %get-tuple-element.122), channel_id=1, source_target_pairs={{0,2},{1,3},{2,0},{3,1},{4,6},{5,7},{6,4},{7,5},{8,10},{9,11},{10,... | collective-permute-start | bytes 245768 | tf_op jit(solution)/shard_map/ppermute | solution.py:208
  94.3 6.3 %collective-permute-start.26 = (bf16[160,256]{1,0:T(8,128)(2,1)S(1)}, bf16[160,256]{1,0:T(8,128)(2,1)S(1)}, u32[]{:S(2)}, u32[]{:S(2)}) collective-permute-start(bf16[160,256]{1,0:T(8,128)(2,1)S(1)} %get-tuple-element.121), channel_id=1, source_target_pairs={{0,3},{1,2},{2,1},{3,0},{4,7},{5,6},{6,5},{7,4},{8,11},{9,10},{10,... | collective-permute-start | bytes 245768 | tf_op jit(solution)/shard_map/ppermute | solution.py:208
  (2 other events, 5.5 us)

commit v6 on v5

--- a/solution.py
+++ b/solution.py
@@ -531,7 +531,8 @@
     key_x, key_y = with_near(key_own)
     value_own = to_head_groups(value_rows)
     key_x, key_y, key_own, value_own = cut(key_x, key_y, key_own, value_own)
-    key_next, key_three = cut(pick(key_y, key_x), jnp.concatenate([key_own, key_x, key_y]))
+    key_next, key_x, key_y, key_own = cut(pick(key_y, key_x), key_x, key_y, key_own)
+    key_three = jnp.concatenate([key_own, key_x, key_y])
     key_diag, key_three = cut(swap_diagonal(key_next), key_three)
     keys = [key_own, key_x, key_y, key_diag]
     keys += [swap(part, "ctx", 1) for part in (key_three, key_diag)]

time: 102 us -> 101 us (level)
  waiting for transfers between devices: 34.9 us -> 33.8 us
    ppermute x4, waiting for transfers between devices: 6.87 us -> 5.8 us  [swap_diagonal(): lax.ppermute(value, 'ctx', [(i, i ^ (4 if i % 2 else 2)) for i in range(c...]
  transfers between devices with their start and end apart: 30 -> 30, of which waited for: 17 -> 17; matrix products, arithmetic and copies ran while one was open for 2% -> 3% of each run, Pallas kernels for 28% -> 28%
where the time goes in v6:
time: 101 us; the launch traced here: 100 us
  waiting for transfers between devices  33.8 us (33%)
  starting transfers between devices  32.6 us (32%)
  Pallas kernels  27.9 us (28%)
  other arithmetic  2.97 us (3%)
  local copies, waits for them, and re-layouts  2.12 us (2%)
    ppermute x26, starting transfers between devices, swap(): return lax.ppermute(value, axis, [(i, i ^ mask) for i in range(count)])  29.5 us
    ppermute x26, waiting for transfers between devices, swap(): return lax.ppermute(value, axis, [(i, i ^ mask) for i in range(count)])  28 us
    pallas_call x5, Pallas kernels, call(): pl.pallas_call(kernel, in_specs=[in_smem] * len(scalars) + [in_hbm if x i...  27.9 us
    ppermute x4, waiting for transfers between devices, swap_diagonal(): lax.ppermute(value, 'ctx', [(i, i ^ (4 if i % 2 else 2)) for i in range(c...  5.8 us
    ppermute x4, starting transfers between devices, swap_diagonal(): lax.ppermute(value, 'ctx', [(i, i ^ (4 if i % 2 else 2)) for i in range(c...  3.11 us
  transfers between devices with their start and end apart: 30, of which 17 were waited for; matrix products, arithmetic and copies ran while one was open for 3% of the time, Pallas kernels for 28%

profile of v6, /device:TPU:0, one launch (start us, length us, event | category | flops | bytes accessed | tf_op | source)
XLA Modules:
  0.0 100.4 jit_solution(3297077404193916556)
XLA Ops:
  1.7 3.1 %collective-permute-start = (bf16[160,256]{1,0:T(8,128)(2,1)S(1)}, bf16[160,256]{1,0:T(8,128)(2,1)S(1)}, u32[]{:S(2)}, u32[]{:S(2)}) collective-permute-start(bf16[160,256]{1,0:T(8,128)(2,1)S(1)} %get-tuple-element.133), channel_id=1, source_target_pairs={{0,1},{1,0},{2,3},{3,2},{4,5},{5,4},{6,7},{7,6},{8,9},{9,8},{10,11... | collective-permute-start | bytes 245768 | tf_op jit(solution)/shard_map/ppermute | solution.py:208
  4.8 2.6 %collective-permute-start.1 = (bf16[160,256]{1,0:T(8,128)(2,1)S(1)}, bf16[160,256]{1,0:T(8,128)(2,1)S(1)}, u32[]{:S(2)}, u32[]{:S(2)}) collective-permute-start(bf16[160,256]{1,0:T(8,128)(2,1)S(1)} %get-tuple-element.135), channel_id=1, source_target_pairs={{0,2},{1,3},{2,0},{3,1},{4,6},{5,7},{6,4},{7,5},{8,10},{9,11},{10,... | collective-permute-start | bytes 245768 | tf_op jit(solution)/shard_map/ppermute | solution.py:208
  7.4 6.6 %collective-permute-done.1 = bf16[160,256]{1,0:T(8,128)(2,1)S(1)} collective-permute-done((bf16[160,256]{1,0:T(8,128)(2,1)S(1)}, bf16[160,256]{1,0:T(8,128)(2,1)S(1)}, u32[]{:S(2)}, u32[]{:S(2)}) %collective-permute-start.1) | collective-permute-done | bytes 81952 | tf_op jit(solution)/shard_map/ppermute | solution.py:208
  14.1 1.6 %collective-permute-start.3 = (bf16[4,160,256]{2,1,0:T(8,128)(2,1)S(1)}, bf16[4,160,256]{2,1,0:T(8,128)(2,1)S(1)}, u32[]{:S(2)}, u32[]{:S(2)}) collective-permute-start(bf16[4,160,256]{2,1,0:T(8,128)(2,1)S(1)} %pad_maximum_fusion.3.refs_0_), channel_id=1, source_target_pairs={{0,8},{4,12},{8,0},{12,4},{16,24},{20,28},{24,16},{28,20},{1,9},{5... | collective-permute-start | bytes 983048 | tf_op jit(solution)/shard_map/ppermute | solution.py:208
  15.6 1.5 %collective-permute-start.4 = (bf16[4,160,256]{2,1,0:T(8,128)(2,1)S(1)}, bf16[4,160,256]{2,1,0:T(8,128)(2,1)S(1)}, u32[]{:S(2)}, u32[]{:S(2)}) collective-permute-start(bf16[4,160,256]{2,1,0:T(8,128)(2,1)S(1)} %pad_maximum_fusion.3.refs_0_), channel_id=1, source_target_pairs={{0,16},{4,20},{8,24},{12,28},{16,0},{20,4},{24,8},{28,12},{1,17},{... | collective-permute-start | bytes 983048 | tf_op jit(solution)/shard_map/ppermute | solution.py:208
  17.2 1.5 %collective-permute-start.5 = (bf16[160,256]{1,0:T(8,128)(2,1)S(1)}, bf16[160,256]{1,0:T(8,128)(2,1)S(1)}, u32[]{:S(2)}, u32[]{:S(2)}) collective-permute-start(bf16[160,256]{1,0:T(8,128)(2,1)S(1)} %get-tuple-element.129), channel_id=1, source_target_pairs={{0,1},{1,0},{2,3},{3,2},{4,5},{5,4},{6,7},{7,6},{8,9},{9,8},{10,11... | collective-permute-start | bytes 245768 | tf_op jit(solution)/shard_map/ppermute | solution.py:208
  18.7 1.6 %collective-permute-start.6 = (bf16[160,256]{1,0:T(8,128)(2,1)S(1)}, bf16[160,256]{1,0:T(8,128)(2,1)S(1)}, u32[]{:S(2)}, u32[]{:S(2)}) collective-permute-start(bf16[160,256]{1,0:T(8,128)(2,1)S(1)} %get-tuple-element.131), channel_id=1, source_target_pairs={{0,2},{1,3},{2,0},{3,1},{4,6},{5,7},{6,4},{7,5},{8,10},{9,11},{10,... | collective-permute-start | bytes 245768 | tf_op jit(solution)/shard_map/ppermute | solution.py:208
  20.3 1.3 %collective-permute-start.7 = (bf16[160,256]{1,0:T(8,128)(2,1)S(1)}, bf16[160,256]{1,0:T(8,128)(2,1)S(1)}, u32[]{:S(2)}, u32[]{:S(2)}) collective-permute-start(bf16[160,256]{1,0:T(8,128)(2,1)S(1)} %get-tuple-element.130), channel_id=1, source_target_pairs={{0,3},{1,2},{2,1},{3,0},{4,7},{5,6},{6,5},{7,4},{8,11},{9,10},{10,... | collective-permute-start | bytes 245768 | tf_op jit(solution)/shard_map/ppermute | solution.py:208
  21.7 3.7 %collective-permute-done.6 = bf16[160,256]{1,0:T(8,128)(2,1)S(1)} collective-permute-done((bf16[160,256]{1,0:T(8,128)(2,1)S(1)}, bf16[160,256]{1,0:T(8,128)(2,1)S(1)}, u32[]{:S(2)}, u32[]{:S(2)}) %collective-permute-start.6) | collective-permute-done | bytes 81952 | tf_op jit(solution)/shard_map/ppermute | solution.py:208
  25.5 1.2 %collective-permute-done.7 = bf16[160,256]{1,0:T(8,128)(2,1)S(1)} collective-permute-done((bf16[160,256]{1,0:T(8,128)(2,1)S(1)}, bf16[160,256]{1,0:T(8,128)(2,1)S(1)}, u32[]{:S(2)}, u32[]{:S(2)}) %collective-permute-start.7) | collective-permute-done | bytes 81952 | tf_op jit(solution)/shard_map/ppermute | solution.py:208
  28.4 5.5 %collective-permute-done.8.refs_3_ = bf16[4,160,256]{2,1,0:T(8,128)(2,1)S(1)} collective-permute-done((bf16[4,160,256]{2,1,0:T(8,128)(2,1)S(1)}, bf16[4,160,256]{2,1,0:T(8,128)(2,1)S(1)}, u32[]{:S(2)}, u32[]{:S(2)}) %collective-permute-start.8) | collective-permute-done | bytes 327712 | tf_op jit(solution)/shard_map/ppermute | solution.py:456
  37.2 7.2 %exps_0.1 = (bf16[5,1024,512]{2,1,0:T(8,128)(2,1)S(1)}, bf16[5,128,512]{2,1,0:T(8,128)(2,1)S(1)}, f32[5,8,512]{2,1,0:T(8,128)S(1)}, f32[5120,128]{1,0:T(8,128)S(...) custom-call(s32[40]{0:T(128)S(1)} %reshape.22.place_ref, ...), custom_call_target="tpu_custom_call" | custom-call | flops 4294967296 | bytes 1048576 | tf_op jit(solution)/shard_map/exps_0/pallas_call | solution.py:519
  45.3 6.2 %exps.1 = (bf16[5,1024,512]{2,1,0:T(8,128)(2,1)S(1)}, bf16[5,128,512]{2,1,0:T(8,128)(2,1)S(1)}, f32[5,8,512]{2,1,0:T(8,128)S(1)}, bf16[4,4,160,256]{3,2,1,0:T(8,128)(2,1)S(1)}, bf16[4,4,160,256]{3,2,1,0:T(8,128)(2,1)S(1)}) custom-call(s32[40]{0:T(128)S(1)} %reshape.22.place_ref, s32[1]{0:T(128)} %bitcast.8.tp_ref, ...), custom_call_target="tpu_custom_call" | custom-call | flops 4294967296 | bytes 1048576 | tf_op jit(solution)/shard_map/exps/pallas_call | solution.py:519
  52.7 1.3 %collective-permute-done.15.refs_5_ = bf16[4,160,256]{2,1,0:T(8,128)(2,1)S(1)} collective-permute-done((bf16[4,160,256]{2,1,0:T(8,128)(2,1)S(1)}, bf16[4,160,256]{2,1,0:T(8,128)(2,1)S(1)}, u32[]{:S(2)}, u32[]{:S(2)}) %collective-permute-start.15) | collective-permute-done | bytes 327712 | tf_op jit(solution)/shard_map/ppermute | solution.py:208
  54.3 4.0 %scores.1 = (bf16[640,512]{1,0:T(8,128)(2,1)S(1)}, bf16[5,1024,512]{2,1,0:T(8,128)(2,1)S(1)}, bf16[5120,256]{1,0:T(8,128)(2,1)S(1)}, f32[8,128]{1,0:T(8,128)}) custom-call(s32[40]{0:T(128)S(1)} %reshape.22.place_ref, s32[1]{0:T(128)} %bitcast.8.tp_ref, bf16[5,1024,512]{2,1,0:T(8,128)(2,1)S(1)} %get-tuple-element.93.exp_ref, ...), custom_call_target="tpu_custom_call" | custom-call | flops 4294967296 | bytes 1048576 | tf_op jit(solution)/shard_map/scores/pallas_call | solution.py:519
  59.0 6.7 %key_sums.1 = (bf16[640,512]{1,0:T(8,128)(2,1)S(1)}, bf16[5,1024,512]{2,1,0:T(8,128)(2,1)S(1)}, bf16[4,4,160,256]{3,2,1,0:T(8,128)(2,1)S(1)}, bf16[4,4,160,256]{3,2,1,0:T(8,128)(2,1)S(1)}) custom-call(s32[40]{0:T(128)S(1)} %reshape.22.place_ref, s32[1]{0:T(128)} %bitcast.8.tp_ref, bf16[5,1024,512]{2,1,0:T(8,128)(2,1)S(1)} %get-tuple-element.89.exp_ref, ...), custom_call_target="tpu_custom_call" | custom-call | flops 4294967296 | bytes 1048576 | tf_op jit(solution)/shard_map/key_sums/pallas_call | solution.py:519
  66.1 1.3 %collective-permute-start.20 = (bf16[4,160,256]{2,1,0:T(8,128)(2,1)S(1)}, bf16[4,160,256]{2,1,0:T(8,128)(2,1)S(1)}, u32[]{:S(2)}, u32[]{:S(2)}) collective-permute-start(bf16[4,160,256]{2,1,0:T(8,128)(2,1)S(1)} %get-tuple-element.121), channel_id=1, source_target_pairs={{0,8},{4,12},{8,0},{12,4},{16,24},{20,28},{24,16},{28,20},{1,9},{5... | collective-permute-start | bytes 983048 | tf_op jit(solution)/shard_map/ppermute | solution.py:208
  68.1 3.8 %query_grad.1 = (bf16[640,1024]{1,0:T(8,128)(2,1)}, f32[8,128]{1,0:T(8,128)}) custom-call(s32[40]{0:T(128)S(1)} %reshape.22.place_ref, bf16[5120,256]{1,0:T(8,128)(2,1)S(1)} %get-tuple-element.80.buffer.buffer_ref, bf16[5,1024,512]{2,1,0:T(8,128)(2,1)S(1)} %get-tuple-element.99.refs_0_, bf16[5,1024,512]{2,1,0:T(8,128)(2,1)S(1)} %get-tuple-element.113.refs_1_), custom_call_target="tpu_custom_call" | custom-call | flops 4294967296 | bytes 1048576 | tf_op jit(solution)/shard_map/query_grad/pallas_call | solution.py:519
  72.0 1.3 %collective-permute-start.19 = (bf16[4,160,256]{2,1,0:T(8,128)(2,1)S(1)}, bf16[4,160,256]{2,1,0:T(8,128)(2,1)S(1)}, u32[]{:S(2)}, u32[]{:S(2)}) collective-permute-start(bf16[4,160,256]{2,1,0:T(8,128)(2,1)S(1)} %fusion.14), channel_id=1, source_target_pairs={{0,8},{4,20},{8,0},{12,28},{16,24},{20,4},{24,16},{28,12},{1,9},{5... | collective-permute-start | bytes 983048 | tf_op jit(solution)/shard_map/ppermute | solution.py:456
  73.3 1.3 %pad_maximum_fusion = bf16[640,1024]{1,0:T(8,128)(2,1)} fusion(bf16[640,512]{1,0:T(8,128)(2,1)S(1)} %get-tuple-element.108, bf16[640,512]{1,0:T(8,128)(2,1)S(1)} %get-tuple-element.107), kind=kLoop, calls=%fused_computation | loop fusion | flops 2621440 | bytes 2621440 | tf_op jit(solution)/shard_map/concatenate | solution.py:595
  74.6 1.5 %collective-permute-done.20 = bf16[4,160,256]{2,1,0:T(8,128)(2,1)S(1)} collective-permute-done((bf16[4,160,256]{2,1,0:T(8,128)(2,1)S(1)}, bf16[4,160,256]{2,1,0:T(8,128)(2,1)S(1)}, u32[]{:S(2)}, u32[]{:S(2)}) %collective-permute-start.20) | collective-permute-done | bytes 327712 | tf_op jit(solution)/shard_map/ppermute | solution.py:208
  76.0 1.9 %collective-permute-done.21 = bf16[4,160,256]{2,1,0:T(8,128)(2,1)S(1)} collective-permute-done((bf16[4,160,256]{2,1,0:T(8,128)(2,1)S(1)}, bf16[4,160,256]{2,1,0:T(8,128)(2,1)S(1)}, u32[]{:S(2)}, u32[]{:S(2)}) %collective-permute-start.21) | collective-permute-done | bytes 327712 | tf_op jit(solution)/shard_map/ppermute | solution.py:208
  78.1 1.2 %collective-permute-start.27 = (bf16[160,256]{1,0:T(8,128)(2,1)S(1)}, bf16[160,256]{1,0:T(8,128)(2,1)S(1)}, u32[]{:S(2)}, u32[]{:S(2)}) collective-permute-start(bf16[160,256]{1,0:T(8,128)(2,1)S(1)} %get-tuple-element.124), channel_id=1, source_target_pairs={{0,1},{1,0},{2,3},{3,2},{4,5},{5,4},{6,7},{7,6},{8,9},{9,8},{10,11... | collective-permute-start | bytes 245768 | tf_op jit(solution)/shard_map/ppermute | solution.py:208
  79.3 1.2 %collective-permute-start.28 = (bf16[160,256]{1,0:T(8,128)(2,1)S(1)}, bf16[160,256]{1,0:T(8,128)(2,1)S(1)}, u32[]{:S(2)}, u32[]{:S(2)}) collective-permute-start(bf16[160,256]{1,0:T(8,128)(2,1)S(1)} %get-tuple-element.123), channel_id=1, source_target_pairs={{0,2},{1,3},{2,0},{3,1},{4,6},{5,7},{6,4},{7,5},{8,10},{9,11},{10,... | collective-permute-start | bytes 245768 | tf_op jit(solution)/shard_map/ppermute | solution.py:208
  80.5 2.0 %collective-permute-start.29 = (bf16[160,256]{1,0:T(8,128)(2,1)S(1)}, bf16[160,256]{1,0:T(8,128)(2,1)S(1)}, u32[]{:S(2)}, u32[]{:S(2)}) collective-permute-start(bf16[160,256]{1,0:T(8,128)(2,1)S(1)} %get-tuple-element.122), channel_id=1, source_target_pairs={{0,3},{1,2},{2,1},{3,0},{4,7},{5,6},{6,5},{7,4},{8,11},{9,10},{10,... | collective-permute-start | bytes 245768 | tf_op jit(solution)/shard_map/ppermute | solution.py:208
  84.7 2.5 %collective-permute-done.28 = bf16[160,256]{1,0:T(8,128)(2,1)S(1)} collective-permute-done((bf16[160,256]{1,0:T(8,128)(2,1)S(1)}, bf16[160,256]{1,0:T(8,128)(2,1)S(1)}, u32[]{:S(2)}, u32[]{:S(2)}) %collective-permute-start.28) | collective-permute-done | bytes 81952 | tf_op jit(solution)/shard_map/ppermute | solution.py:208
  87.2 3.1 %collective-permute-done.22 = bf16[4,160,256]{2,1,0:T(8,128)(2,1)S(1)} collective-permute-done((bf16[4,160,256]{2,1,0:T(8,128)(2,1)S(1)}, bf16[4,160,256]{2,1,0:T(8,128)(2,1)S(1)}, u32[]{:S(2)}, u32[]{:S(2)}) %collective-permute-start.22) | collective-permute-done | bytes 327712 | tf_op jit(solution)/shard_map/ppermute | solution.py:208
  90.7 1.2 %collective-permute-start.24 = (bf16[160,256]{1,0:T(8,128)(2,1)S(1)}, bf16[160,256]{1,0:T(8,128)(2,1)S(1)}, u32[]{:S(2)}, u32[]{:S(2)}) collective-permute-start(bf16[160,256]{1,0:T(8,128)(2,1)S(1)} %get-tuple-element.127), channel_id=1, source_target_pairs={{0,1},{1,0},{2,3},{3,2},{4,5},{5,4},{6,7},{7,6},{8,9},{9,8},{10,11... | collective-permute-start | bytes 245768 | tf_op jit(solution)/shard_map/ppermute | solution.py:208
  92.0 1.3 %collective-permute-start.25 = (bf16[160,256]{1,0:T(8,128)(2,1)S(1)}, bf16[160,256]{1,0:T(8,128)(2,1)S(1)}, u32[]{:S(2)}, u32[]{:S(2)}) collective-permute-start(bf16[160,256]{1,0:T(8,128)(2,1)S(1)} %get-tuple-element.126), channel_id=1, source_target_pairs={{0,2},{1,3},{2,0},{3,1},{4,6},{5,7},{6,4},{7,5},{8,10},{9,11},{10,... | collective-permute-start | bytes 245768 | tf_op jit(solution)/shard_map/ppermute | solution.py:208
  93.3 2.0 %collective-permute-start.26 = (bf16[160,256]{1,0:T(8,128)(2,1)S(1)}, bf16[160,256]{1,0:T(8,128)(2,1)S(1)}, u32[]{:S(2)}, u32[]{:S(2)}) collective-permute-start(bf16[160,256]{1,0:T(8,128)(2,1)S(1)} %get-tuple-element.125), channel_id=1, source_target_pairs={{0,3},{1,2},{2,1},{3,0},{4,7},{5,6},{6,5},{7,4},{8,11},{9,10},{10,... | collective-permute-start | bytes 245768 | tf_op jit(solution)/shard_map/ppermute | solution.py:208
  96.4 1.9 %collective-permute-done.25 = bf16[160,256]{1,0:T(8,128)(2,1)S(1)} collective-permute-done((bf16[160,256]{1,0:T(8,128)(2,1)S(1)}, bf16[160,256]{1,0:T(8,128)(2,1)S(1)}, u32[]{:S(2)}, u32[]{:S(2)}) %collective-permute-start.25) | collective-permute-done | bytes 81952 | tf_op jit(solution)/shard_map/ppermute | solution.py:208
  98.3 1.3 %collective-permute-done.26 = bf16[160,256]{1,0:T(8,128)(2,1)S(1)} collective-permute-done((bf16[160,256]{1,0:T(8,128)(2,1)S(1)}, bf16[160,256]{1,0:T(8,128)(2,1)S(1)}, u32[]{:S(2)}, u32[]{:S(2)}) %collective-permute-start.26) | collective-permute-done | bytes 81952 | tf_op jit(solution)/shard_map/ppermute | solution.py:208
  (70 shorter events, 15.0 us)
Async XLA Ops:
  0.6 16.5 %copy-start = (bf16[160,1024]{1,0:T(8,128)(2,1)S(1)}, bf16[160,1024]{1,0:T(8,128)(2,1)}, u32[]{:S(2)}) copy-start(bf16[160,1024]{1,0:T(8,128)(2,1)} %param.7) | copy-start | bytes 983044
  1.7 5.7 %collective-permute-start = (bf16[160,256]{1,0:T(8,128)(2,1)S(1)}, bf16[160,256]{1,0:T(8,128)(2,1)S(1)}, u32[]{:S(2)}, u32[]{:S(2)}) collective-permute-start(bf16[160,256]{1,0:T(8,128)(2,1)S(1)} %get-tuple-element.133), channel_id=1, source_target_pairs={{0,1},{1,0},{2,3},{3,2},{4,5},{5,4},{6,7},{7,6},{8,9},{9,8},{10,11... | collective-permute-start | bytes 245768 | tf_op jit(solution)/shard_map/ppermute | solution.py:208
  4.8 9.2 %collective-permute-start.1 = (bf16[160,256]{1,0:T(8,128)(2,1)S(1)}, bf16[160,256]{1,0:T(8,128)(2,1)S(1)}, u32[]{:S(2)}, u32[]{:S(2)}) collective-permute-start(bf16[160,256]{1,0:T(8,128)(2,1)S(1)} %get-tuple-element.135), channel_id=1, source_target_pairs={{0,2},{1,3},{2,0},{3,1},{4,6},{5,7},{6,4},{7,5},{8,10},{9,11},{10,... | collective-permute-start | bytes 245768 | tf_op jit(solution)/shard_map/ppermute | solution.py:208
  7.4 6.6 %collective-permute-start.2 = (bf16[160,256]{1,0:T(8,128)(2,1)S(1)}, bf16[160,256]{1,0:T(8,128)(2,1)S(1)}, u32[]{:S(2)}, u32[]{:S(2)}) collective-permute-start(bf16[160,256]{1,0:T(8,128)(2,1)S(1)} %get-tuple-element.134), channel_id=1, source_target_pairs={{0,3},{1,2},{2,1},{3,0},{4,7},{5,6},{6,5},{7,4},{8,11},{9,10},{10,... | collective-permute-start | bytes 245768 | tf_op jit(solution)/shard_map/ppermute | solution.py:208
  14.1 12.6 %collective-permute-start.3 = (bf16[4,160,256]{2,1,0:T(8,128)(2,1)S(1)}, bf16[4,160,256]{2,1,0:T(8,128)(2,1)S(1)}, u32[]{:S(2)}, u32[]{:S(2)}) collective-permute-start(bf16[4,160,256]{2,1,0:T(8,128)(2,1)S(1)} %pad_maximum_fusion.3.refs_0_), channel_id=1, source_target_pairs={{0,8},{4,12},{8,0},{12,4},{16,24},{20,28},{24,16},{28,20},{1,9},{5... | collective-permute-start | bytes 983048 | tf_op jit(solution)/shard_map/ppermute | solution.py:208
  15.6 11.1 %collective-permute-start.4 = (bf16[4,160,256]{2,1,0:T(8,128)(2,1)S(1)}, bf16[4,160,256]{2,1,0:T(8,128)(2,1)S(1)}, u32[]{:S(2)}, u32[]{:S(2)}) collective-permute-start(bf16[4,160,256]{2,1,0:T(8,128)(2,1)S(1)} %pad_maximum_fusion.3.refs_0_), channel_id=1, source_target_pairs={{0,16},{4,20},{8,24},{12,28},{16,0},{20,4},{24,8},{28,12},{1,17},{... | collective-permute-start | bytes 983048 | tf_op jit(solution)/shard_map/ppermute | solution.py:208
  17.2 4.5 %collective-permute-start.5 = (bf16[160,256]{1,0:T(8,128)(2,1)S(1)}, bf16[160,256]{1,0:T(8,128)(2,1)S(1)}, u32[]{:S(2)}, u32[]{:S(2)}) collective-permute-start(bf16[160,256]{1,0:T(8,128)(2,1)S(1)} %get-tuple-element.129), channel_id=1, source_target_pairs={{0,1},{1,0},{2,3},{3,2},{4,5},{5,4},{6,7},{7,6},{8,9},{9,8},{10,11... | collective-permute-start | bytes 245768 | tf_op jit(solution)/shard_map/ppermute | solution.py:208
  18.7 6.8 %collective-permute-start.6 = (bf16[160,256]{1,0:T(8,128)(2,1)S(1)}, bf16[160,256]{1,0:T(8,128)(2,1)S(1)}, u32[]{:S(2)}, u32[]{:S(2)}) collective-permute-start(bf16[160,256]{1,0:T(8,128)(2,1)S(1)} %get-tuple-element.131), channel_id=1, source_target_pairs={{0,2},{1,3},{2,0},{3,1},{4,6},{5,7},{6,4},{7,5},{8,10},{9,11},{10,... | collective-permute-start | bytes 245768 | tf_op jit(solution)/shard_map/ppermute | solution.py:208
  20.3 6.3 %collective-permute-start.7 = (bf16[160,256]{1,0:T(8,128)(2,1)S(1)}, bf16[160,256]{1,0:T(8,128)(2,1)S(1)}, u32[]{:S(2)}, u32[]{:S(2)}) collective-permute-start(bf16[160,256]{1,0:T(8,128)(2,1)S(1)} %get-tuple-element.130), channel_id=1, source_target_pairs={{0,3},{1,2},{2,1},{3,0},{4,7},{5,6},{6,5},{7,4},{8,11},{9,10},{10,... | collective-permute-start | bytes 245768 | tf_op jit(solution)/shard_map/ppermute | solution.py:208
  26.7 7.7 %copy-start.3 = (s32[5,8]{1,0:T(8,128)S(1)}, s32[5,8]{1,0:T(8,128)}, u32[]{:S(2)}) copy-start(s32[5,8]{1,0:T(8,128)} %param.9) | copy-start | bytes 484
  26.8 7.1 %collective-permute-start.8 = (bf16[4,160,256]{2,1,0:T(8,128)(2,1)S(1)}, bf16[4,160,256]{2,1,0:T(8,128)(2,1)S(1)}, u32[]{:S(2)}, u32[]{:S(2)}) collective-permute-start(bf16[4,160,256]{2,1,0:T(8,128)(2,1)S(1)} %broadcast_select_fusion.1), channel_id=1, source_target_pairs={{0,8},{4,20},{8,0},{12,28},{16,24},{20,4},{24,16},{28,12},{1,9},{5... | collective-permute-start | bytes 983048 | tf_op jit(solution)/shard_map/ppermute | solution.py:456
  33.9 3.2 %collective-permute-start.11 = (bf16[12,160,256]{2,1,0:T(8,128)(2,1)}, bf16[12,160,256]{2,1,0:T(8,128)(2,1)S(1)}, u32[]{:S(2)}, u32[]{:S(2)}) collective-permute-start(bf16[12,160,256]{2,1,0:T(8,128)(2,1)} %pad_maximum_fusion.1), channel_id=1, source_target_pairs={{0,4},{4,0},{8,12},{12,8},{16,20},{20,16},{24,28},{28,24},{1,5},{5... | collective-permute-start | bytes 2949128 | tf_op jit(solution)/shard_map/ppermute | solution.py:208
  33.9 2.7 %collective-permute-start.12 = (bf16[4,160,256]{2,1,0:T(8,128)(2,1)S(1)}, bf16[4,160,256]{2,1,0:T(8,128)(2,1)S(1)}, u32[]{:S(2)}, u32[]{:S(2)}) collective-permute-start(bf16[4,160,256]{2,1,0:T(8,128)(2,1)S(1)} %collective-permute-done.8.refs_3_), channel_id=1, source_target_pairs={{0,4},{4,0},{8,12},{12,8},{16,20},{20,16},{24,28},{28,24},{1,5},{5... | collective-permute-start | bytes 983048 | tf_op jit(solution)/shard_map/ppermute | solution.py:208
  34.5 9.9 %collective-permute-start.10 = (bf16[4,160,256]{2,1,0:T(8,128)(2,1)S(1)}, bf16[4,160,256]{2,1,0:T(8,128)(2,1)S(1)}, u32[]{:S(2)}, u32[]{:S(2)}) collective-permute-start(bf16[4,160,256]{2,1,0:T(8,128)(2,1)S(1)} %pad_maximum_fusion.4.refs_0_), channel_id=1, source_target_pairs={{0,16},{4,20},{8,24},{12,28},{16,0},{20,4},{24,8},{28,12},{1,17},{... | collective-permute-start | bytes 983048 | tf_op jit(solution)/shard_map/ppermute | solution.py:208
  35.0 9.4 %collective-permute-start.9 = (bf16[4,160,256]{2,1,0:T(8,128)(2,1)S(1)}, bf16[4,160,256]{2,1,0:T(8,128)(2,1)S(1)}, u32[]{:S(2)}, u32[]{:S(2)}) collective-permute-start(bf16[4,160,256]{2,1,0:T(8,128)(2,1)S(1)} %pad_maximum_fusion.4.refs_0_), channel_id=1, source_target_pairs={{0,8},{4,12},{8,0},{12,4},{16,24},{20,28},{24,16},{28,20},{1,9},{5... | collective-permute-start | bytes 983048 | tf_op jit(solution)/shard_map/ppermute | solution.py:208
  44.6 7.3 %collective-permute-start.14 = (bf16[12,160,256]{2,1,0:T(8,128)(2,1)S(1)}, bf16[12,160,256]{2,1,0:T(8,128)(2,1)S(1)}, u32[]{:S(2)}, u32[]{:S(2)}) collective-permute-start(bf16[12,160,256]{2,1,0:T(8,128)(2,1)S(1)} %pad_maximum_fusion.2), channel_id=1, source_target_pairs={{0,4},{4,0},{8,12},{12,8},{16,20},{20,16},{24,28},{28,24},{1,5},{5... | collective-permute-start | bytes 2949128 | tf_op jit(solution)/shard_map/ppermute | solution.py:208
  44.8 7.1 %collective-permute-start.13 = (bf16[4,160,256]{2,1,0:T(8,128)(2,1)S(1)}, bf16[4,160,256]{2,1,0:T(8,128)(2,1)S(1)}, u32[]{:S(2)}, u32[]{:S(2)}) collective-permute-start(bf16[4,160,256]{2,1,0:T(8,128)(2,1)S(1)} %broadcast_select_fusion), channel_id=1, source_target_pairs={{0,8},{4,20},{8,0},{12,28},{16,24},{20,4},{24,16},{28,12},{1,9},{5... | collective-permute-start | bytes 983048 | tf_op jit(solution)/shard_map/ppermute | solution.py:456
  51.9 2.1 %collective-permute-start.15 = (bf16[4,160,256]{2,1,0:T(8,128)(2,1)S(1)}, bf16[4,160,256]{2,1,0:T(8,128)(2,1)S(1)}, u32[]{:S(2)}, u32[]{:S(2)}) collective-permute-start(bf16[4,160,256]{2,1,0:T(8,128)(2,1)S(1)} %collective-permute-done.13.refs_3_), channel_id=1, source_target_pairs={{0,4},{4,0},{8,12},{12,8},{16,20},{20,16},{24,28},{28,24},{1,5},{5... | collective-permute-start | bytes 983048 | tf_op jit(solution)/shard_map/ppermute | solution.py:208
  53.9 4.4 %collective-permute-start.16 = (bf16[4,4,160,256]{3,2,1,0:T(8,128)(2,1)S(1)}, bf16[4,4,160,256]{3,2,1,0:T(8,128)(2,1)S(1)}, u32[]{:S(2)}, u32[]{:S(2)}) collective-permute-start(bf16[4,4,160,256]{3,2,1,0:T(8,128)(2,1)S(1)} %get-tuple-element.87), channel_id=1, source_target_pairs={{0,4},{4,0},{8,12},{12,8},{16,20},{20,16},{24,28},{28,24},{1,5},{5... | collective-permute-start | bytes 3932168 | tf_op jit(solution)/shard_map/ppermute | solution.py:208
  58.3 7.3 %collective-permute-start.17 = (bf16[4,160,256]{2,1,0:T(8,128)(2,1)S(1)}, bf16[4,160,256]{2,1,0:T(8,128)(2,1)S(1)}, u32[]{:S(2)}, u32[]{:S(2)}) collective-permute-start(bf16[4,160,256]{2,1,0:T(8,128)(2,1)S(1)} %fusion.15), channel_id=1, source_target_pairs={{0,8},{4,20},{8,0},{12,28},{16,24},{20,4},{24,16},{28,12},{1,9},{5... | collective-permute-start | bytes 983048 | tf_op jit(solution)/shard_map/ppermute | solution.py:456
  65.7 6.3 %collective-permute-start.18 = (bf16[4,4,160,256]{3,2,1,0:T(8,128)(2,1)S(1)}, bf16[4,4,160,256]{3,2,1,0:T(8,128)(2,1)S(1)}, u32[]{:S(2)}, u32[]{:S(2)}) collective-permute-start(bf16[4,4,160,256]{3,2,1,0:T(8,128)(2,1)S(1)} %get-tuple-element.104), channel_id=1, source_target_pairs={{0,4},{4,0},{8,12},{12,8},{16,20},{20,16},{24,28},{28,24},{1,5},{5... | collective-permute-start | bytes 3932168 | tf_op jit(solution)/shard_map/ppermute | solution.py:208
  66.1 9.9 %collective-permute-start.20 = (bf16[4,160,256]{2,1,0:T(8,128)(2,1)S(1)}, bf16[4,160,256]{2,1,0:T(8,128)(2,1)S(1)}, u32[]{:S(2)}, u32[]{:S(2)}) collective-permute-start(bf16[4,160,256]{2,1,0:T(8,128)(2,1)S(1)} %get-tuple-element.121), channel_id=1, source_target_pairs={{0,8},{4,12},{8,0},{12,4},{16,24},{20,28},{24,16},{28,20},{1,9},{5... | collective-permute-start | bytes 983048 | tf_op jit(solution)/shard_map/ppermute | solution.py:208
  67.4 10.6 %collective-permute-start.21 = (bf16[4,160,256]{2,1,0:T(8,128)(2,1)S(1)}, bf16[4,160,256]{2,1,0:T(8,128)(2,1)S(1)}, u32[]{:S(2)}, u32[]{:S(2)}) collective-permute-start(bf16[4,160,256]{2,1,0:T(8,128)(2,1)S(1)} %get-tuple-element.120), channel_id=1, source_target_pairs={{0,16},{4,20},{8,24},{12,28},{16,0},{20,4},{24,8},{28,12},{1,17},{... | collective-permute-start | bytes 983048 | tf_op jit(solution)/shard_map/ppermute | solution.py:208
  72.0 10.6 %collective-permute-start.19 = (bf16[4,160,256]{2,1,0:T(8,128)(2,1)S(1)}, bf16[4,160,256]{2,1,0:T(8,128)(2,1)S(1)}, u32[]{:S(2)}, u32[]{:S(2)}) collective-permute-start(bf16[4,160,256]{2,1,0:T(8,128)(2,1)S(1)} %fusion.14), channel_id=1, source_target_pairs={{0,8},{4,20},{8,0},{12,28},{16,24},{20,4},{24,16},{28,12},{1,9},{5... | collective-permute-start | bytes 983048 | tf_op jit(solution)/shard_map/ppermute | solution.py:456
  78.1 6.6 %collective-permute-start.27 = (bf16[160,256]{1,0:T(8,128)(2,1)S(1)}, bf16[160,256]{1,0:T(8,128)(2,1)S(1)}, u32[]{:S(2)}, u32[]{:S(2)}) collective-permute-start(bf16[160,256]{1,0:T(8,128)(2,1)S(1)} %get-tuple-element.124), channel_id=1, source_target_pairs={{0,1},{1,0},{2,3},{3,2},{4,5},{5,4},{6,7},{7,6},{8,9},{9,8},{10,11... | collective-permute-start | bytes 245768 | tf_op jit(solution)/shard_map/ppermute | solution.py:208
  79.3 7.9 %collective-permute-start.28 = (bf16[160,256]{1,0:T(8,128)(2,1)S(1)}, bf16[160,256]{1,0:T(8,128)(2,1)S(1)}, u32[]{:S(2)}, u32[]{:S(2)}) collective-permute-start(bf16[160,256]{1,0:T(8,128)(2,1)S(1)} %get-tuple-element.123), channel_id=1, source_target_pairs={{0,2},{1,3},{2,0},{3,1},{4,6},{5,7},{6,4},{7,5},{8,10},{9,11},{10,... | collective-permute-start | bytes 245768 | tf_op jit(solution)/shard_map/ppermute | solution.py:208
  80.5 6.7 %collective-permute-start.29 = (bf16[160,256]{1,0:T(8,128)(2,1)S(1)}, bf16[160,256]{1,0:T(8,128)(2,1)S(1)}, u32[]{:S(2)}, u32[]{:S(2)}) collective-permute-start(bf16[160,256]{1,0:T(8,128)(2,1)S(1)} %get-tuple-element.122), channel_id=1, source_target_pairs={{0,3},{1,2},{2,1},{3,0},{4,7},{5,6},{6,5},{7,4},{8,11},{9,10},{10,... | collective-permute-start | bytes 245768 | tf_op jit(solution)/shard_map/ppermute | solution.py:208
  82.7 7.6 %collective-permute-start.22 = (bf16[4,160,256]{2,1,0:T(8,128)(2,1)S(1)}, bf16[4,160,256]{2,1,0:T(8,128)(2,1)S(1)}, u32[]{:S(2)}, u32[]{:S(2)}) collective-permute-start(bf16[4,160,256]{2,1,0:T(8,128)(2,1)S(1)} %get-tuple-element.118), channel_id=1, source_target_pairs={{0,8},{4,12},{8,0},{12,4},{16,24},{20,28},{24,16},{28,20},{1,9},{5... | collective-permute-start | bytes 983048 | tf_op jit(solution)/shard_map/ppermute | solution.py:208
  83.5 7.1 %collective-permute-start.23 = (bf16[4,160,256]{2,1,0:T(8,128)(2,1)S(1)}, bf16[4,160,256]{2,1,0:T(8,128)(2,1)S(1)}, u32[]{:S(2)}, u32[]{:S(2)}) collective-permute-start(bf16[4,160,256]{2,1,0:T(8,128)(2,1)S(1)} %get-tuple-element.119), channel_id=1, source_target_pairs={{0,16},{4,20},{8,24},{12,28},{16,0},{20,4},{24,8},{28,12},{1,17},{... | collective-permute-start | bytes 983048 | tf_op jit(solution)/shard_map/ppermute | solution.py:208
  90.7 5.7 %collective-permute-start.24 = (bf16[160,256]{1,0:T(8,128)(2,1)S(1)}, bf16[160,256]{1,0:T(8,128)(2,1)S(1)}, u32[]{:S(2)}, u32[]{:S(2)}) collective-permute-start(bf16[160,256]{1,0:T(8,128)(2,1)S(1)} %get-tuple-element.127), channel_id=1, source_target_pairs={{0,1},{1,0},{2,3},{3,2},{4,5},{5,4},{6,7},{7,6},{8,9},{9,8},{10,11... | collective-permute-start | bytes 245768 | tf_op jit(solution)/shard_map/ppermute | solution.py:208
  92.0 6.3 %collective-permute-start.25 = (bf16[160,256]{1,0:T(8,128)(2,1)S(1)}, bf16[160,256]{1,0:T(8,128)(2,1)S(1)}, u32[]{:S(2)}, u32[]{:S(2)}) collective-permute-start(bf16[160,256]{1,0:T(8,128)(2,1)S(1)} %get-tuple-element.126), channel_id=1, source_target_pairs={{0,2},{1,3},{2,0},{3,1},{4,6},{5,7},{6,4},{7,5},{8,10},{9,11},{10,... | collective-permute-start | bytes 245768 | tf_op jit(solution)/shard_map/ppermute | solution.py:208
  93.3 6.3 %collective-permute-start.26 = (bf16[160,256]{1,0:T(8,128)(2,1)S(1)}, bf16[160,256]{1,0:T(8,128)(2,1)S(1)}, u32[]{:S(2)}, u32[]{:S(2)}) collective-permute-start(bf16[160,256]{1,0:T(8,128)(2,1)S(1)} %get-tuple-element.125), channel_id=1, source_target_pairs={{0,3},{1,2},{2,1},{3,0},{4,7},{5,6},{6,5},{7,4},{8,11},{9,10},{10,... | collective-permute-start | bytes 245768 | tf_op jit(solution)/shard_map/ppermute | solution.py:208
  (2 other events, 5.5 us)
